TPU v7x, 256 devices: a whole 4x4x8 slice. The times are simulated.
256 devices in a mesh: cache: 32 (over x, y, core), tp: 8 (over z).
Axes of the slice: x: 4, y: 4, z: 8, core: 2. Of those that a mesh axis runs over, the one named last changes fastest.
Arguments:
- x_in: bfloat16 [4096, 16384], P('cache', 'tp'), may hold values from -6 to 6
- conv_weight: float32 [4, 16384], P(None, 'tp'), may hold values from -3 to 3
- dt_in_weight: bfloat16 [16384, 512], P('tp'), may hold values from -0.046875 to 0.046875
- bc_weight: bfloat16 [32, 16384], P(None, 'tp'), may hold values from -0.046875 to 0.046875
- dt_weight: bfloat16 [512, 16384], P(None, 'tp'), may hold values from -0.25 to 0.25
- dt_bias: float32 [16384], P('tp'), may hold values from -6 to -2
- decay_rates: float32 [16, 16384], P(None, 'tp'), may hold values from 0.5 to 16
- skip_gain: float32 [16384], P('tp'), may hold values from 0.5 to 1.5
- queries: bfloat16 [4096, 4096], P('cache', 'tp'), may hold values from -40 to 40
- new_keys: bfloat16 [4096, 1024], P('cache', 'tp'), may hold values from -4.5 to 4.5
- new_values: bfloat16 [4096, 1024], P('cache', 'tp'), may hold values from -6 to 6
- store_state: float32 [640, 16, 16384], P('cache', None, 'tp'), may hold values from -6 to 6
- store_conv: bfloat16 [640, 3, 16384], P('cache', None, 'tp'), may hold values from -6 to 6
- store_keys: bfloat16 [640, 256, 1024], P('cache', None, 'tp'), may hold values from -4 to 4
- store_values: bfloat16 [640, 256, 1024], P('cache', None, 'tp'), may hold values from -6 to 6
- hit_entry: int32 [512], P('cache'), may hold values from 0 to 639, as said below
- hit_blocks: int32 [512], P('cache'), may hold values from 1 to 2
- seg_lengths: int32 [32, 16], P('cache'), may hold values from 1 to 64, 128 in all within a row
Outputs:
- mixer_out: bfloat16 [4096, 16384], P('cache', 'tp')
- attn_out: bfloat16 [4096, 4096], P('cache', 'tp')
- new_state: float32 [640, 16, 16384], P('cache', None, 'tp')
- new_conv: bfloat16 [640, 3, 16384], P('cache', None, 'tp')
Inputs may be any that keep to these rules, and one draw needn't show every extreme that they name: `hit_entry`: entry e lives on cache index e // 20. The 16 requests of one cache index come in consecutive groups of 1 that name entries of one owner, different groups different owners; every owner serves exactly 16 requests, and no entry is named twice.
All inputs are finite; a program needn't handle non-finite values.
Results may differ from a plain program's by a relative error of at most 0.012.
Values may be sent and summed in bfloat16 or wider, within the bound.
No kernel may reach another device: no remote copies, remote signals or barrier semaphores. Data moves between devices by JAX's collectives and lax.ppermute only.
A program may use at most 192 MiB of HBM per device.

v0:
```python
import functools
import math

import jax
import jax.numpy as jnp
from jax import lax
from jax.experimental import pallas as pl
from jax.experimental.pallas import tpu as pltpu
from jax.sharding import PartitionSpec as P

HEAD_DIM = 128
KVB = 128
LANES = 128
BF = jnp.bfloat16
F32 = jnp.float32
I32 = jnp.int32
VMEM = pltpu.VMEM
SMEM = pltpu.SMEM
MIB = 1 << 20


def params(mib):
    return pltpu.CompilerParams(vmem_limit_bytes=mib * MIB)


def in_vmem(count):
    return [pl.BlockSpec(memory_space=VMEM) for _ in range(count)]


def tiles_kernel(state_ref, out_ref, hold):
    entries, states, channels = state_ref.shape
    groups = channels // LANES
    for e in range(entries):
        for low in range(0, states, 8):
            for j in range(groups):
                hold[pl.ds(low * groups + j, 8, stride=groups), :] = state_ref[
                    e, low : low + 8, j * LANES : (j + 1) * LANES
                ]
        out_ref[e] = hold[...].astype(BF)


def state_tiles(store_state):
    slots, states, channels = store_state.shape
    rows = states * channels // LANES
    step = 4
    return pl.pallas_call(
        tiles_kernel,
        grid=(slots // step,),
        in_specs=[pl.BlockSpec((step, states, channels), lambda i: (i, 0, 0))],
        out_specs=pl.BlockSpec((step, rows, LANES), lambda i: (i, 0, 0)),
        out_shape=jax.ShapeDtypeStruct((slots, rows, LANES), BF),
        scratch_shapes=[VMEM((rows, LANES), F32)],
        compiler_params=params(16),
    )(store_state)


def pick_kernel(count, asked_ref, *refs):
    sources, out_ref, sem = refs[:count], refs[count], refs[count + 1]
    blocks = out_ref.shape[0]

    def copies(i):
        pick = jnp.maximum(asked_ref[i], 0)
        made, low = [], 0
        for n, source in enumerate(sources):
            rows = source.shape[1]
            made.append(
                pltpu.make_async_copy(
                    source.at[pick], out_ref.at[i, pl.ds(low, rows)], sem.at[i, n]
                )
            )
            low += rows
        return made

    for i in range(blocks):
        for copy in copies(i):
            copy.start()
    for i in range(blocks):
        for copy in copies(i):
            copy.wait()


def pick(asked, *sources):
    blocks = asked.shape[0]
    rows = sum(s.shape[1] for s in sources)
    return pl.pallas_call(
        functools.partial(pick_kernel, len(sources)),
        in_specs=[pl.BlockSpec(memory_space=SMEM)]
        + [pl.BlockSpec(memory_space=pl.ANY) for _ in sources],
        out_specs=pl.BlockSpec(memory_space=pl.ANY),
        out_shape=jax.ShapeDtypeStruct((blocks, rows, LANES), sources[0].dtype),
        scratch_shapes=[pltpu.SemaphoreType.DMA((blocks, len(sources)))],
        compiler_params=params(4),
    )(asked, *sources)


def conv_kernel(
    rank_ref, x_ref, got_ref, choose_ref, weight_ref, in_ref, bc_ref, *refs
):
    parts, (mixed_ref, tail_ref), (source, wide, total, tails) = refs[:8], refs[8:10], refs[10:]
    tokens, channels = x_ref.shape
    groups = channels // LANES
    olds = got_ref.shape[0] // groups
    wide[...] = got_ref[...].astype(F32)
    source[0:tokens, :] = x_ref[...]
    source[tokens + olds :, :] = jnp.zeros((source.shape[0] - tokens - olds, channels), BF)
    for j in range(groups):
        source[tokens : tokens + olds, j * LANES : (j + 1) * LANES] = wide[
            pl.ds(j, olds, stride=groups), :
        ].astype(BF)
    chunk = min(512, channels)
    rank_dim = in_ref.shape[1]
    for low in range(0, channels, chunk):
        cut = slice(low, low + chunk)
        taken = jnp.dot(choose_ref[...], source[:, cut], preferred_element_type=F32)
        running = weight_ref[3:4, cut] * x_ref[:, cut].astype(F32)
        for lag in range(1, 4):
            running = (
                running
                + weight_ref[3 - lag : 4 - lag, cut] * taken[(lag - 1) * tokens : lag * tokens]
            )
        mixed = (running / (1.0 + jnp.exp(-running))).astype(BF)
        mixed_ref[:, cut] = mixed
        for j in range(chunk // LANES):
            tails[pl.ds(low // LANES + j, olds, stride=groups), :] = taken[
                3 * tokens :, j * LANES : (j + 1) * LANES
            ]
        dt_part = jnp.dot(mixed, in_ref[cut, :], preferred_element_type=F32)
        bc_part = lax.dot_general(
            mixed, bc_ref[:, cut], (((1,), (1,)), ((), ())), preferred_element_type=F32
        )
        if low == 0:
            total[:, 0:rank_dim] = dt_part
            total[:, rank_dim:] = jnp.zeros((tokens, total.shape[1] - rank_dim), F32)
            total[:, rank_dim : rank_dim + bc_part.shape[1]] = bc_part
        else:
            total[:, 0:rank_dim] += dt_part
            total[:, rank_dim : rank_dim + bc_part.shape[1]] += bc_part
    tail_ref[...] = tails[...].astype(BF)
    share = tokens // 8
    for step, part in enumerate(parts):
        place = lax.rem(rank_ref[0] + step, 8) * share
        part[...] = total[pl.ds(pl.multiple_of(place, share), share), :]


def conv_project(rank, x_rows, got_conv, choose, conv_weight, dt_in_weight, bc_weight):
    tokens, channels = x_rows.shape
    width = dt_in_weight.shape[1] + LANES
    tail_rows = got_conv.shape[0]
    return pl.pallas_call(
        conv_kernel,
        in_specs=[pl.BlockSpec(memory_space=SMEM)] + in_vmem(6),
        out_specs=in_vmem(10),
        out_shape=[jax.ShapeDtypeStruct((tokens // 8, width), F32)] * 8
        + [
            jax.ShapeDtypeStruct((tokens, channels), BF),
            jax.ShapeDtypeStruct((tail_rows, LANES), BF),
        ],
        scratch_shapes=[
            VMEM((choose.shape[1], channels), BF),
            VMEM((tail_rows, LANES), F32),
            VMEM((tokens, width), F32),
            VMEM((tail_rows, LANES), F32),
        ],
        compiler_params=params(32),
    )(rank, x_rows, got_conv, choose, conv_weight, dt_in_weight, bc_weight)


def sum_kernel(*refs):
    out_ref = refs[-1]
    total = refs[0][...]
    for part in refs[1:-1]:
        total = total + part[...]
    width = total.shape[1]
    rank_dim = width - LANES
    out_ref[:, 0:rank_dim] = total[:, 0:rank_dim].astype(BF)
    maps = total[:, rank_dim:]
    high = maps.astype(BF)
    out_ref[:, rank_dim:width] = high
    out_ref[:, width:] = (maps - high.astype(F32)).astype(BF)


def sum_parts(parts):
    rows, width = parts[0].shape
    return pl.pallas_call(
        sum_kernel,
        in_specs=in_vmem(len(parts)),
        out_specs=pl.BlockSpec(memory_space=VMEM),
        out_shape=jax.ShapeDtypeStruct((rows, width + LANES), BF),
    )(*parts)


def scan_kernel(states, *refs):
    rank_ref, length_ref, owner_ref = refs[:3]
    pieces = refs[3:11]
    (mixed_ref, weight_ref, bias_ref, decay_ref, skip_ref, start_ref, tail_ref) = refs[11:18]
    out_ref, back_ref = refs[18:20]
    low_dt, maps, map_smem, rates, drives, sums, decays, hold, sem = refs[20:]
    tokens, channels = mixed_ref.shape
    groups = channels // LANES
    share = tokens // 8
    rank_dim = weight_ref.shape[0]
    for step, piece in enumerate(pieces):
        place = pl.multiple_of(lax.rem(rank_ref[0] + 8 - step, 8) * share, share)
        low_dt[pl.ds(place, share), :] = piece[:, 0:rank_dim]
        maps[pl.ds(place, share), :] = piece[:, rank_dim : rank_dim + LANES].astype(F32) + piece[
            :, rank_dim + LANES :
        ].astype(F32)
    copy = pltpu.make_async_copy(maps, map_smem, sem)
    copy.start()
    for low in range(0, states, 8):
        for j in range(groups):
            decays[pl.ds(low * groups + j, 8, stride=groups), :] = decay_ref[
                low : low + 8, j * LANES : (j + 1) * LANES
            ] * (-math.log2(math.e))
    chunk = min(512, channels)
    for low in range(0, channels, chunk):
        cut = slice(low, low + chunk)
        raw = (
            jnp.dot(low_dt[...], weight_ref[:, cut], preferred_element_type=F32) + bias_ref[:, cut]
        )
        rate = jnp.maximum(raw, 0.0) + jnp.log1p(jnp.exp(-jnp.abs(raw)))
        drive = rate * mixed_ref[:, cut].astype(F32)
        for j in range(chunk // LANES):
            rows = pl.ds(low // LANES + j, tokens, stride=groups)
            rates[rows, :] = rate[:, j * LANES : (j + 1) * LANES]
            drives[rows, :] = drive[:, j * LANES : (j + 1) * LANES]
    back_ref[:, states * groups :, :] = tail_ref[...]
    copy.wait()

    def segment(r, begin):
        finish = begin + length_ref[r]
        owner = owner_ref[r]
        held = tuple(
            start_ref[owner, n * groups : (n + 1) * groups, :].astype(F32) for n in range(states)
        )

        def token(t, held):
            place = pl.ds(pl.multiple_of(t * groups, groups), groups)
            rate, drive = rates[place, :], drives[place, :]
            total, later = None, []
            for n in range(states):
                decay = jnp.exp2(rate * decays[n * groups : (n + 1) * groups, :])
                value = decay * held[n] + drive * map_smem[t, n]
                term = value * map_smem[t, states + n]
                total = term if total is None else total + term
                later.append(value)
            sums[place, :] = total
            return tuple(later)

        held = lax.fori_loop(begin, finish, token, held)
        for n in range(states):
            back_ref[owner, n * groups : (n + 1) * groups, :] = held[n].astype(BF)
        return finish

    lax.fori_loop(0, length_ref.shape[0], segment, jnp.int32(0))
    for j in range(groups):
        cut = slice(j * LANES, (j + 1) * LANES)
        out_ref[:, cut] = (
            sums[pl.ds(j, tokens, stride=groups), :]
            + skip_ref[:, cut] * mixed_ref[:, cut].astype(F32)
        ).astype(BF)


def scan(
    rank, lengths, owners, pieces, mixed, dt_weight, dt_bias, decay_rates, skip_gain, start, tails
):
    tokens, channels = mixed.shape
    states = decay_rates.shape[0]
    groups = channels // LANES
    owners_count = start.shape[0]
    rank_dim = dt_weight.shape[0]
    tail_rows = tails.shape[1]
    return pl.pallas_call(
        functools.partial(scan_kernel, states),
        in_specs=[pl.BlockSpec(memory_space=SMEM)] * 3 + in_vmem(15),
        out_specs=in_vmem(2),
        out_shape=[
            jax.ShapeDtypeStruct((tokens, channels), BF),
            jax.ShapeDtypeStruct((owners_count, states * groups + tail_rows, LANES), BF),
        ],
        scratch_shapes=[
            VMEM((tokens, rank_dim), BF),
            VMEM((tokens, LANES), F32),
            SMEM((tokens, LANES), F32),
            VMEM((tokens * groups, LANES), F32),
            VMEM((tokens * groups, LANES), F32),
            VMEM((tokens * groups, LANES), F32),
            VMEM((states * groups, LANES), F32),
            VMEM((8, LANES), F32),
            pltpu.SemaphoreType.DMA,
        ],
        compiler_params=params(32),
    )(
        rank, lengths, owners, *pieces, mixed, dt_weight, dt_bias[None, :], decay_rates,
        skip_gain[None, :], start, tails,
    )


def attend_kernel(length_ref, owner_ref, live_ref, q_ref, k_ref, v_ref, prefix_ref, out_ref, rows_q, rows_o):
    tokens = q_ref.shape[0]
    heads = q_ref.shape[1] // HEAD_DIM
    prefix = prefix_ref.shape[1] // 2
    for h in range(heads):
        rows_q[h * tokens : (h + 1) * tokens, :] = q_ref[:, h * HEAD_DIM : (h + 1) * HEAD_DIM]
    contract = (((1,), (1,)), ((), ()))
    scale = HEAD_DIM**-0.5
    many = heads * tokens
    new_scores = lax.dot_general(
        rows_q[...], k_ref[...], contract, preferred_element_type=F32
    ) * scale
    query_of = lax.rem(lax.broadcasted_iota(I32, (many, tokens), 0), tokens)
    key_of = lax.broadcasted_iota(I32, (many, tokens), 1)
    new_scores = jnp.where(key_of <= query_of, new_scores, -1e30)
    token_of = lax.rem(lax.broadcasted_iota(I32, (many, HEAD_DIM), 0), tokens)
    place_of = lax.broadcasted_iota(I32, (many, prefix), 1)
    rows_o[...] = jnp.zeros((many, HEAD_DIM), F32)

    def request(r, begin):
        finish = begin + length_ref[r]
        owner = owner_ref[r]
        live = live_ref[r] * KVB
        old = lax.dot_general(
            rows_q[...], prefix_ref[owner, 0:prefix, :], contract, preferred_element_type=F32
        ) * scale
        old = jnp.where(place_of < live, old, -1e30)
        new = jnp.where(key_of >= begin, new_scores, -1e30)
        highest = jnp.maximum(
            jnp.max(old, axis=1, keepdims=True), jnp.max(new, axis=1, keepdims=True)
        )
        old, new = jnp.exp(old - highest), jnp.exp(new - highest)
        total = jnp.sum(old, axis=1, keepdims=True) + jnp.sum(new, axis=1, keepdims=True)
        inverse = 1.0 / total
        result = jnp.dot(
            (old * inverse).astype(BF), prefix_ref[owner, prefix:, :], preferred_element_type=F32
        ) + jnp.dot((new * inverse).astype(BF), v_ref[...], preferred_element_type=F32)
        mine = (token_of >= begin) & (token_of < finish)
        rows_o[...] = jnp.where(mine, result, rows_o[...])
        return finish

    lax.fori_loop(0, length_ref.shape[0], request, jnp.int32(0))
    for h in range(heads):
        out_ref[:, h * HEAD_DIM : (h + 1) * HEAD_DIM] = rows_o[
            h * tokens : (h + 1) * tokens, :
        ].astype(BF)


def attend(lengths, owners, live, queries, new_keys, new_values, prefix):
    tokens, width = queries.shape
    many = tokens * width // HEAD_DIM
    return pl.pallas_call(
        attend_kernel,
        in_specs=[pl.BlockSpec(memory_space=SMEM)] * 3 + in_vmem(4),
        out_specs=pl.BlockSpec(memory_space=VMEM),
        out_shape=jax.ShapeDtypeStruct((tokens, width), BF),
        scratch_shapes=[VMEM((many, HEAD_DIM), BF), VMEM((many, HEAD_DIM), F32)],
        compiler_params=params(32),
    )(lengths, owners, live, queries, new_keys, new_values, prefix)


def write_kernel(source_ref, store_ref, back_ref, out_ref, hold):
    step, states, channels = out_ref.shape
    groups = channels // LANES
    first = pl.program_id(0) * step
    for e in range(step):
        row = source_ref[first + e]

        @pl.when(row < 0)
        def _():
            out_ref[e] = store_ref[e]

        @pl.when(row >= 0)
        def _():
            hold[...] = back_ref[row, 0 : states * groups, :].astype(F32)
            for low in range(0, states, 8):
                for j in range(groups):
                    out_ref[e, low : low + 8, j * LANES : (j + 1) * LANES] = hold[
                        pl.ds(low * groups + j, 8, stride=groups), :
                    ]


def write_state(source, store_state, back):
    slots, states, channels = store_state.shape
    rows = states * channels // LANES
    step = 4
    return pl.pallas_call(
        write_kernel,
        grid_spec=pltpu.PrefetchScalarGridSpec(
            num_scalar_prefetch=1,
            grid=(slots // step,),
            in_specs=[
                pl.BlockSpec((step, states, channels), lambda i, s: (i, 0, 0)),
                pl.BlockSpec(memory_space=VMEM),
            ],
            out_specs=pl.BlockSpec((step, states, channels), lambda i, s: (i, 0, 0)),
            scratch_shapes=[VMEM((rows, LANES), F32)],
        ),
        out_shape=jax.ShapeDtypeStruct((slots, states, channels), F32),
        compiler_params=params(24),
    )(source, store_state, back)


def exchange(blocks, axis):
    return lax.all_to_all(blocks, axis, split_axis=0, concat_axis=0, tiled=True)


def choose_matrix(lengths, owners, tokens, owner_count, width):
    ends = jnp.cumsum(lengths, dtype=I32)
    starts = ends - lengths
    places = jnp.arange(tokens, dtype=I32)
    member = (places[:, None] >= starts[None, :]) & (places[:, None] < ends[None, :])
    offset = places - jnp.sum(jnp.where(member, starts[None, :], 0), axis=1, dtype=I32)
    owner = jnp.sum(jnp.where(member, owners[None, :], 0), axis=1, dtype=I32)
    lags = jnp.arange(1, 4, dtype=I32)[:, None]
    lagged = jnp.where(
        offset[None, :] >= lags,
        places[None, :] - lags,
        tokens + owner[None, :] * 3 + 3 + offset[None, :] - lags,
    )
    owner_ids = jnp.arange(owner_count, dtype=I32)
    served = owner_ids[:, None] == owners[None, :]
    ends_of = jnp.sum(jnp.where(served, ends[None, :], 0), axis=1, dtype=I32)[:, None]
    length_of = jnp.sum(jnp.where(served, lengths[None, :], 0), axis=1, dtype=I32)[:, None]
    rows = jnp.arange(3, dtype=I32)[None, :]
    tails = jnp.where(
        length_of + rows >= 3, ends_of - 3 + rows, tokens + owner_ids[:, None] * 3 + length_of + rows
    )
    tails = jnp.where(length_of > 0, tails, width)
    column = jnp.concatenate([lagged.reshape(-1), tails.reshape(-1)])
    return (column[:, None] == jnp.arange(width, dtype=I32)[None, :]).astype(BF)


def shards(
    x_in,
    conv_weight,
    dt_in_weight,
    bc_weight,
    dt_weight,
    dt_bias,
    decay_rates,
    skip_gain,
    queries,
    new_keys,
    new_values,
    store_state,
    store_conv,
    store_keys,
    store_values,
    hit_entry,
    hit_blocks,
    seg_lengths,
):
    owner_count = lax.axis_size("cache")
    tp_count = lax.axis_size("tp")
    rank = lax.axis_index("tp").astype(I32)[None]
    slot_count, states, channels = store_state.shape
    groups = channels // LANES
    tokens = x_in.shape[0]
    lengths = seg_lengths[0]
    owners = hit_entry // slot_count
    slots = hit_entry - owners * slot_count
    owner_ids = jnp.arange(owner_count, dtype=I32)
    served = owner_ids[:, None] == owners[None, :]
    table = jnp.sum(jnp.where(served, slots[None, :] + 1, 0), axis=1, dtype=I32) - 1
    asked = exchange(table[:, None], "cache")[:, 0]

    conv_tiles = store_conv.reshape(slot_count, 3 * groups, LANES)
    got_conv = exchange(pick(asked, conv_tiles), "cache")
    got_state = exchange(pick(asked, state_tiles(store_state)), "cache")
    got_prefix = exchange(pick(asked, store_keys, store_values), "cache")

    width = tokens + -(-3 * owner_count // LANES) * LANES
    choose = choose_matrix(lengths, owners, tokens, owner_count, width)
    *parts, mixed, tails = conv_project(
        rank, x_in, got_conv.reshape(-1, LANES), choose, conv_weight, dt_in_weight, bc_weight
    )

    def turned(step, value):
        return lax.ppermute(value, "tp", [(k, (k + step) % tp_count) for k in range(tp_count)])

    parts = [parts[0]] + [turned(step, parts[step]) for step in range(1, tp_count)]
    summed = sum_parts(parts)
    pieces = [summed] + [turned(step, summed) for step in range(1, tp_count)]

    mixer_out, back = scan(
        rank, lengths, owners, pieces, mixed, dt_weight, dt_bias, decay_rates, skip_gain,
        got_state, tails.reshape(owner_count, 3 * groups, LANES),
    )
    back = exchange(back, "cache")
    attn_out = attend(lengths, owners, hit_blocks, queries, new_keys, new_values, got_prefix)

    slot_ids = jnp.arange(slot_count, dtype=I32)
    landing = asked[None, :] == slot_ids[:, None]
    source = jnp.sum(jnp.where(landing, owner_ids[None, :] + 1, 0), axis=1, dtype=I32) - 1
    new_state = write_state(source, store_state, back)
    back_conv = back[:, states * groups :, :]
    placed_conv = jnp.take(back_conv, jnp.maximum(source, 0), axis=0, mode="clip")
    new_conv = jnp.where(
        (source >= 0)[:, None, None], placed_conv.reshape(store_conv.shape), store_conv
    )
    return (mixer_out, attn_out, new_state, new_conv)


def solution(mesh):
    placed = (
        P("cache", "tp"),
        P(None, "tp"),
        P("tp", None),
        P(None, "tp"),
        P(None, "tp"),
        P("tp"),
        P(None, "tp"),
        P("tp"),
        P("cache", "tp"),
        P("cache", "tp"),
        P("cache", "tp"),
        P("cache", None, "tp"),
        P("cache", None, "tp"),
        P("cache", None, "tp"),
        P("cache", None, "tp"),
        P("cache"),
        P("cache"),
        P("cache", None),
    )
    return jax.shard_map(
        shards,
        mesh=mesh,
        in_specs=placed,
        out_specs=(
            P("cache", "tp"),
            P("cache", "tp"),
            P("cache", None, "tp"),
            P("cache", None, "tp"),
        ),
        check_vma=False,
    )
```

profile of v0, /device:TPU:1, one launch (start us, length us, event | category | flops | bytes accessed | tf_op | source)
XLA Modules:
  0.0 191.3 jit_solution(16149989840687150830)
XLA Ops:
  4.3 8.6 %all-to-all-start = ((s32[32,1,1]{2,1,0:T(1,128)}), s32[32,1,1]{2,1,0:T(1,128)S(1)}, u32[]{:S(2)}, u32[]{:S(2)}) async-start(s32[32,1,1]{2,1,0:T(1,128)} %copy.39), calls=%async_computation | async-start | bytes 32768 | tf_op jit(solution)/shard_map/all_to_all | solution.py:403
  14.4 5.4 %all-to-all-done = s32[32,1,1]{2,1,0:T(1,128)S(1)} async-done(((s32[32,1,1]{2,1,0:T(1,128)}), s32[32,1,1]{2,1,0:T(1,128)S(1)}, u32[]{:S(2)}, u32[]{:S(2)}) %all-to-all-start) | async-done | bytes 160 | tf_op jit(solution)/shard_map/all_to_all | solution.py:403
  20.5 1.5 shard_map.201
  22.0 4.2 %all-to-all-start.1 = ((bf16[32,48,128]{2,1,0:T(8,128)(2,1)}), bf16[32,48,128]{2,1,0:T(8,128)(2,1)S(1)}, u32[]{:S(2)}, u32[]{:S(2)}) async-start(bf16[32,48,128]{2,1,0:T(8,128)(2,1)} %shard_map.201), calls=%async_computation.1 | async-start | bytes 786432 | tf_op jit(solution)/shard_map/all_to_all | solution.py:403
  27.2 3.7 %shard_map.205 = bf16[32,256,128]{2,1,0:T(8,128)(2,1)S(1)} custom-call(s32[32]{0:T(128)S(1)} %reduce.asked_ref, bf16[20,256,128]{2,1,0:T(8,128)(2,1)S(1)} %shard_map.204.refs_0_), custom_call_target="tpu_custom_call" | custom-call | tf_op jit(solution)/shard_map/pallas_call | solution.py:85
  32.3 4.4 %all-to-all-done.1 = bf16[32,48,128]{2,1,0:T(8,128)(2,1)S(1)} async-done(((bf16[32,48,128]{2,1,0:T(8,128)(2,1)}), bf16[32,48,128]{2,1,0:T(8,128)(2,1)S(1)}, u32[]{:S(2)}, u32[]{:S(2)}) %all-to-all-start.1) | async-done | bytes 393248 | tf_op jit(solution)/shard_map/all_to_all | solution.py:403
  36.6 3.8 %all-to-all-start.2 = ((bf16[32,256,128]{2,1,0:T(8,128)(2,1)}), bf16[32,256,128]{2,1,0:T(8,128)(2,1)S(1)}, u32[]{:S(2)}, u32[]{:S(2)}) async-start(bf16[32,256,128]{2,1,0:T(8,128)(2,1)} %copy-done.3), calls=%async_computation.2 | async-start | bytes 4194304 | tf_op jit(solution)/shard_map/all_to_all | solution.py:403
  43.1 6.8 %shard_map.207 = bf16[32,512,128]{2,1,0:T(8,128)(2,1)S(1)} custom-call(s32[32]{0:T(128)S(1)} %reduce.asked_ref, bf16[20,256,128]{2,1,0:T(8,128)(2,1)S(1)} %copy-done.7, bf16[20,256,128]{2,1,0:T(8,128)(2,1)S(1)} %copy-done.8), custom_call_target="tpu_custom_call" | custom-call | tf_op jit(solution)/shard_map/pallas_call | solution.py:85
  49.9 2.0 %copy-done = bf16[32,512,128]{2,1,0:T(8,128)(2,1)} copy-done((bf16[32,512,128]{2,1,0:T(8,128)(2,1)}, bf16[32,512,128]{2,1,0:T(8,128)(2,1)S(1)}, u32[]{:S(2)}) %copy-start) | copy-done | bytes 4194328
  51.9 16.6 %all-to-all-done.2.refs_16_ = bf16[32,256,128]{2,1,0:T(8,128)(2,1)S(1)} async-done(((bf16[32,256,128]{2,1,0:T(8,128)(2,1)}), bf16[32,256,128]{2,1,0:T(8,128)(2,1)S(1)}, u32[]{:S(2)}, u32[]{:S(2)}) %all-to-all-start.2) | async-done | bytes 2097184 | tf_op jit(solution)/shard_map/all_to_all | solution.py:403
  68.6 5.3 %all-to-all-start.3 = ((bf16[32,512,128]{2,1,0:T(8,128)(2,1)}), bf16[32,512,128]{2,1,0:T(8,128)(2,1)}, u32[]{:S(2)}, u32[]{:S(2)}) async-start(bf16[32,512,128]{2,1,0:T(8,128)(2,1)} %copy-done), calls=%async_computation.3 | async-start | bytes 8388608 | tf_op jit(solution)/shard_map/all_to_all | solution.py:403
  74.6 1.6 copy-done.6
  77.8 1.9 %shard_map.202 = (f32[16,640]{1,0:T(8,128)S(1)}, f32[16,640]{1,0:T(8,128)S(1)}, f32[16,640]{1,0:T(8,128)S(1)}, f32[16,640]{1,0:T(8,128)S(1)}, f32[16,640]{1,0:T(...) custom-call(s32[1]{0:T(128)} %bitcast.rank_ref.refs_0_, ...), custom_call_target="tpu_custom_call" | custom-call | tf_op jit(solution)/shard_map/pallas_call | solution.py:149
  81.1 1.6 collective-permute-start
  82.8 3.0 %collective-permute-start.1 = (f32[16,640]{1,0:T(8,128)S(1)}, f32[16,640]{1,0:T(8,128)S(1)}, u32[]{:S(2)}, u32[]{:S(2)}) collective-permute-start(f32[16,640]{1,0:T(8,128)S(1)} %get-tuple-element.18), channel_id=1, source_target_pairs={{0,2},{1,3},{2,4},{3,5},{4,6},{5,7},{6,0},{7,1},{8,10},{9,11},{10,... | collective-permute-start | bytes 122888 | tf_op jit(solution)/shard_map/ppermute | solution.py:478
  85.7 3.8 %collective-permute-start.2 = (f32[16,640]{1,0:T(8,128)S(1)}, f32[16,640]{1,0:T(8,128)S(1)}, u32[]{:S(2)}, u32[]{:S(2)}) collective-permute-start(f32[16,640]{1,0:T(8,128)S(1)} %get-tuple-element.19), channel_id=1, source_target_pairs={{0,3},{1,4},{2,5},{3,6},{4,7},{5,0},{6,1},{7,2},{8,11},{9,12},{10,... | collective-permute-start | bytes 122888 | tf_op jit(solution)/shard_map/ppermute | solution.py:478
  90.0 4.5 %collective-permute-start.4 = (f32[16,640]{1,0:T(8,128)S(1)}, f32[16,640]{1,0:T(8,128)S(1)}, u32[]{:S(2)}, u32[]{:S(2)}) collective-permute-start(f32[16,640]{1,0:T(8,128)S(1)} %get-tuple-element.21), channel_id=1, source_target_pairs={{0,5},{1,6},{2,7},{3,0},{4,1},{5,2},{6,3},{7,4},{8,13},{9,14},{10,... | collective-permute-start | bytes 122888 | tf_op jit(solution)/shard_map/ppermute | solution.py:478
  94.4 2.4 %collective-permute-start.5 = (f32[16,640]{1,0:T(8,128)S(1)}, f32[16,640]{1,0:T(8,128)S(1)}, u32[]{:S(2)}, u32[]{:S(2)}) collective-permute-start(f32[16,640]{1,0:T(8,128)S(1)} %get-tuple-element.22), channel_id=1, source_target_pairs={{0,6},{1,7},{2,0},{3,1},{4,2},{5,3},{6,4},{7,5},{8,14},{9,15},{10,... | collective-permute-start | bytes 122888 | tf_op jit(solution)/shard_map/ppermute | solution.py:478
  97.6 4.1 %collective-permute-done.5.refs_6_ = f32[16,640]{1,0:T(8,128)S(1)} collective-permute-done((f32[16,640]{1,0:T(8,128)S(1)}, f32[16,640]{1,0:T(8,128)S(1)}, u32[]{:S(2)}, u32[]{:S(2)}) %collective-permute-start.5) | collective-permute-done | bytes 40992 | tf_op jit(solution)/shard_map/ppermute | solution.py:478
  102.7 1.6 shard_map.203.refs_3_
  105.1 3.2 %collective-permute-start.9 = (bf16[16,768]{1,0:T(8,128)(2,1)}, bf16[16,768]{1,0:T(8,128)(2,1)S(1)}, u32[]{:S(2)}, u32[]{:S(2)}) collective-permute-start(bf16[16,768]{1,0:T(8,128)(2,1)} %shard_map.203.refs_3_), channel_id=1, source_target_pairs={{0,3},{1,4},{2,5},{3,6},{4,7},{5,0},{6,1},{7,2},{8,11},{9,12},{10,... | collective-permute-start | bytes 73736 | tf_op jit(solution)/shard_map/ppermute | solution.py:478
  108.3 2.2 %collective-permute-start.10 = (bf16[16,768]{1,0:T(8,128)(2,1)}, bf16[16,768]{1,0:T(8,128)(2,1)S(1)}, u32[]{:S(2)}, u32[]{:S(2)}) collective-permute-start(bf16[16,768]{1,0:T(8,128)(2,1)} %shard_map.203.refs_3_), channel_id=1, source_target_pairs={{0,4},{1,5},{2,6},{3,7},{4,0},{5,1},{6,2},{7,3},{8,12},{9,13},{10,... | collective-permute-start | bytes 73736 | tf_op jit(solution)/shard_map/ppermute | solution.py:478
  110.4 2.9 %collective-permute-start.11 = (bf16[16,768]{1,0:T(8,128)(2,1)}, bf16[16,768]{1,0:T(8,128)(2,1)S(1)}, u32[]{:S(2)}, u32[]{:S(2)}) collective-permute-start(bf16[16,768]{1,0:T(8,128)(2,1)} %shard_map.203.refs_3_), channel_id=1, source_target_pairs={{0,5},{1,6},{2,7},{3,0},{4,1},{5,2},{6,3},{7,4},{8,13},{9,14},{10,... | collective-permute-start | bytes 73736 | tf_op jit(solution)/shard_map/ppermute | solution.py:478
  115.7 1.7 collective-permute-done.12.refs_9_
  118.0 1.6 copy-done.5
  123.6 11.9 %shard_map.206 = (bf16[128,2048]{1,0:T(8,128)(2,1)}, bf16[32,304,128]{2,1,0:T(8,128)(2,1)S(1)}) custom-call(s32[1]{0:T(128)} %bitcast.rank_ref.refs_0_, s32[16]{0:T(128)S(1)} %bitcast.23, s32[16]{0:T(128)S(1)} %copy-done.29, bf16[16,768]{1,0:T(8,128)(2,1)S(1)} %copy-done.15, bf16[16,768]{1,0:T(8,128)(2,1)S(1)} %collective-permute-done.7.refs_4_, ...), custom_call_target="tpu_custom_call" | custom-call | tf_op jit(solution)/shard_map/pallas_call | solution.py:273
  136.9 11.3 %all-to-all-start.4 = ((bf16[32,304,128]{2,1,0:T(8,128)(2,1)}), bf16[32,304,128]{2,1,0:T(8,128)(2,1)S(1)}, u32[]{:S(2)}, u32[]{:S(2)}) async-start(bf16[32,304,128]{2,1,0:T(8,128)(2,1)} %copy-done.4), calls=%async_computation.4 | async-start | bytes 4980736 | tf_op jit(solution)/shard_map/all_to_all | solution.py:403
  148.5 14.6 %shard_map.208 = bf16[128,512]{1,0:T(8,128)(2,1)} custom-call(s32[16]{0:T(128)S(1)} %bitcast.24, s32[16]{0:T(128)S(1)} %copy-done.30, s32[16]{0:T(128)S(1)} %copy-done.31, bf16[128,512]{1,0:T(8,128)(2,1)S(1)} %copy-done.14, bf16[128,128]{1,0:T(8,128)(2,1)S(1)} %copy-done.18, bf16[128,128]{1,0:T(8,128)(2,1)S(1)} %copy-done.19, ...), custom_call_target="tpu_custom_call" | custom-call | tf_op jit(solution)/shard_map/pallas_call | solution.py:350
  163.1 17.7 %all-to-all-done.4.back_ref = bf16[32,304,128]{2,1,0:T(8,128)(2,1)S(1)} async-done(((bf16[32,304,128]{2,1,0:T(8,128)(2,1)}), bf16[32,304,128]{2,1,0:T(8,128)(2,1)S(1)}, u32[]{:S(2)}, u32[]{:S(2)}) %all-to-all-start.4) | async-done | bytes 2490400 | tf_op jit(solution)/shard_map/all_to_all | solution.py:403
  181.5 2.3 %gather_fusion = bf16[20,48,128]{2,1,0:T(8,128)(2,1)} fusion(bf16[32,48,128]{2,1,0:T(8,128)(2,1)} %slice.6, s32[1024]{0:T(1024)S(1)} %pad_clamp_fusion), kind=kCustom, calls=%fused_computation | custom fusion | bytes 491600 | tf_op jit(solution)/shard_map/jit(_take)/gather | solution.py:496
  186.0 1.7 copy-done.2
  187.8 3.5 %shard_map.209 = f32[20,16,2048]{2,1,0:T(8,128)} custom-call(s32[20]{0:T(128)S(1)} %get-tuple-element.52.source_ref, f32[20,16,2048]{2,1,0:T(8,128)S(1)} %copy-done.2, bf16[32,304,128]{2,1,0:T(8,128)(2,1)S(1)} %all-to-all-done.4.back_ref), custom_call_target="tpu_custom_call" | custom-call | tf_op jit(solution)/shard_map/pallas_call | solution.py:385
  (134 shorter events, 28.7 us)
Async XLA Ops:
  0.6 25.6 %copy-start.1 = (f32[20,16,2048]{2,1,0:T(8,128)S(1)}, f32[20,16,2048]{2,1,0:T(8,128)}, u32[]{:S(2)}) copy-start(f32[20,16,2048]{2,1,0:T(8,128)} %store_ref.1) | copy-start | bytes 7864324
  4.3 15.5 %all-to-all-start = ((s32[32,1,1]{2,1,0:T(1,128)}), s32[32,1,1]{2,1,0:T(1,128)S(1)}, u32[]{:S(2)}, u32[]{:S(2)}) async-start(s32[32,1,1]{2,1,0:T(1,128)} %copy.39), calls=%async_computation | async-start | bytes 32768 | tf_op jit(solution)/shard_map/all_to_all | solution.py:403
  20.4 20.0 %copy-start.22 = (s32[32]{0:T(128)}, s32[32]{0:T(128)S(1)}, u32[]{:S(2)}) copy-start(s32[32]{0:T(128)S(1)} %reduce.asked_ref) | copy-start | bytes 388
  22.0 14.6 %all-to-all-start.1 = ((bf16[32,48,128]{2,1,0:T(8,128)(2,1)}), bf16[32,48,128]{2,1,0:T(8,128)(2,1)S(1)}, u32[]{:S(2)}, u32[]{:S(2)}) async-start(bf16[32,48,128]{2,1,0:T(8,128)(2,1)} %shard_map.201), calls=%async_computation.1 | async-start | bytes 786432 | tf_op jit(solution)/shard_map/all_to_all | solution.py:403
  36.6 31.9 %all-to-all-start.2 = ((bf16[32,256,128]{2,1,0:T(8,128)(2,1)}), bf16[32,256,128]{2,1,0:T(8,128)(2,1)S(1)}, u32[]{:S(2)}, u32[]{:S(2)}) async-start(bf16[32,256,128]{2,1,0:T(8,128)(2,1)} %copy-done.3), calls=%async_computation.2 | async-start | bytes 4194304 | tf_op jit(solution)/shard_map/all_to_all | solution.py:403
  51.9 22.0 %copy-start.42 = (s32[32]{0:T(128)S(1)}, s32[32]{0:T(128)}, u32[]{:S(2)}) copy-start(s32[32]{0:T(128)} %get-tuple-element.47) | copy-start | bytes 388
  51.9 22.0 %copy-start.43 = (s32[32]{0:T(128)S(1)}, s32[32]{0:T(128)}, u32[]{:S(2)}) copy-start(s32[32]{0:T(128)} %get-tuple-element.46) | copy-start | bytes 388
  51.9 22.3 %copy-start.24 = (s32[1,16]{1,0:T(1,128)S(1)}, s32[1,16]{1,0:T(1,128)}, u32[]{:S(2)}) copy-start(s32[1,16]{1,0:T(1,128)} %param.35) | copy-start | bytes 196
  51.9 22.3 %copy-start.41 = (s32[16]{0:T(128)S(1)}, s32[16]{0:T(128)}, u32[]{:S(2)}) copy-start(s32[16]{0:T(128)} %copy-done.40) | copy-start | bytes 196
  51.9 22.3 %copy-start.28 = (s32[16]{0:T(128)S(1)}, s32[16]{0:T(128)}, u32[]{:S(2)}) copy-start(s32[16]{0:T(128)} %copy-done.27) | copy-start | bytes 196
  51.9 22.6 %copy-start.9 = (bf16[128,2048]{1,0:T(8,128)(2,1)S(1)}, bf16[128,2048]{1,0:T(8,128)(2,1)}, u32[]{:S(2)}) copy-start(bf16[128,2048]{1,0:T(8,128)(2,1)} %x_ref.1) | copy-start | bytes 1572868
  68.6 68.3 %all-to-all-start.3 = ((bf16[32,512,128]{2,1,0:T(8,128)(2,1)}), bf16[32,512,128]{2,1,0:T(8,128)(2,1)}, u32[]{:S(2)}, u32[]{:S(2)}) async-start(bf16[32,512,128]{2,1,0:T(8,128)(2,1)} %copy-done), calls=%async_computation.3 | async-start | bytes 8388608 | tf_op jit(solution)/shard_map/all_to_all | solution.py:403
  73.9 44.1 %copy-start.20 = (f32[2048]{0:T(1024)S(1)}, f32[2048]{0:T(1024)}, u32[]{:S(2)}) copy-start(f32[2048]{0:T(1024)} %param.23) | copy-start | bytes 24580
  73.9 44.1 %copy-start.21 = (f32[2048]{0:T(1024)S(1)}, f32[2048]{0:T(1024)}, u32[]{:S(2)}) copy-start(f32[2048]{0:T(1024)} %param.25) | copy-start | bytes 24580
  81.1 13.3 %collective-permute-start = (f32[16,640]{1,0:T(8,128)S(1)}, f32[16,640]{1,0:T(8,128)S(1)}, u32[]{:S(2)}, u32[]{:S(2)}) collective-permute-start(f32[16,640]{1,0:T(8,128)S(1)} %get-tuple-element.17), channel_id=1, source_target_pairs={{0,1},{1,2},{2,3},{3,4},{4,5},{5,6},{6,7},{7,0},{8,9},{9,10},{10,1... | collective-permute-start | bytes 122888 | tf_op jit(solution)/shard_map/ppermute | solution.py:478
  82.8 14.1 %collective-permute-start.1 = (f32[16,640]{1,0:T(8,128)S(1)}, f32[16,640]{1,0:T(8,128)S(1)}, u32[]{:S(2)}, u32[]{:S(2)}) collective-permute-start(f32[16,640]{1,0:T(8,128)S(1)} %get-tuple-element.18), channel_id=1, source_target_pairs={{0,2},{1,3},{2,4},{3,5},{4,6},{5,7},{6,0},{7,1},{8,10},{9,11},{10,... | collective-permute-start | bytes 122888 | tf_op jit(solution)/shard_map/ppermute | solution.py:478
  85.7 11.8 %collective-permute-start.2 = (f32[16,640]{1,0:T(8,128)S(1)}, f32[16,640]{1,0:T(8,128)S(1)}, u32[]{:S(2)}, u32[]{:S(2)}) collective-permute-start(f32[16,640]{1,0:T(8,128)S(1)} %get-tuple-element.19), channel_id=1, source_target_pairs={{0,3},{1,4},{2,5},{3,6},{4,7},{5,0},{6,1},{7,2},{8,11},{9,12},{10,... | collective-permute-start | bytes 122888 | tf_op jit(solution)/shard_map/ppermute | solution.py:478
  89.5 8.1 %collective-permute-start.3 = (f32[16,640]{1,0:T(8,128)S(1)}, f32[16,640]{1,0:T(8,128)S(1)}, u32[]{:S(2)}, u32[]{:S(2)}) collective-permute-start(f32[16,640]{1,0:T(8,128)S(1)} %get-tuple-element.20), channel_id=1, source_target_pairs={{0,4},{1,5},{2,6},{3,7},{4,0},{5,1},{6,2},{7,3},{8,12},{9,13},{10,... | collective-permute-start | bytes 122888 | tf_op jit(solution)/shard_map/ppermute | solution.py:478
  90.0 7.6 %collective-permute-start.4 = (f32[16,640]{1,0:T(8,128)S(1)}, f32[16,640]{1,0:T(8,128)S(1)}, u32[]{:S(2)}, u32[]{:S(2)}) collective-permute-start(f32[16,640]{1,0:T(8,128)S(1)} %get-tuple-element.21), channel_id=1, source_target_pairs={{0,5},{1,6},{2,7},{3,0},{4,1},{5,2},{6,3},{7,4},{8,13},{9,14},{10,... | collective-permute-start | bytes 122888 | tf_op jit(solution)/shard_map/ppermute | solution.py:478
  94.4 7.3 %collective-permute-start.5 = (f32[16,640]{1,0:T(8,128)S(1)}, f32[16,640]{1,0:T(8,128)S(1)}, u32[]{:S(2)}, u32[]{:S(2)}) collective-permute-start(f32[16,640]{1,0:T(8,128)S(1)} %get-tuple-element.22), channel_id=1, source_target_pairs={{0,6},{1,7},{2,0},{3,1},{4,2},{5,3},{6,4},{7,5},{8,14},{9,15},{10,... | collective-permute-start | bytes 122888 | tf_op jit(solution)/shard_map/ppermute | solution.py:478
  96.8 5.3 %collective-permute-start.6 = (f32[16,640]{1,0:T(8,128)S(1)}, f32[16,640]{1,0:T(8,128)S(1)}, u32[]{:S(2)}, u32[]{:S(2)}) collective-permute-start(f32[16,640]{1,0:T(8,128)S(1)} %get-tuple-element.23), channel_id=1, source_target_pairs={{0,7},{1,0},{2,1},{3,2},{4,3},{5,4},{6,5},{7,6},{8,15},{9,8},{10,9... | collective-permute-start | bytes 122888 | tf_op jit(solution)/shard_map/ppermute | solution.py:478
  104.3 9.0 %collective-permute-start.7 = (bf16[16,768]{1,0:T(8,128)(2,1)}, bf16[16,768]{1,0:T(8,128)(2,1)S(1)}, u32[]{:S(2)}, u32[]{:S(2)}) collective-permute-start(bf16[16,768]{1,0:T(8,128)(2,1)} %shard_map.203.refs_3_), channel_id=1, source_target_pairs={{0,1},{1,2},{2,3},{3,4},{4,5},{5,6},{6,7},{7,0},{8,9},{9,10},{10,1... | collective-permute-start | bytes 73736 | tf_op jit(solution)/shard_map/ppermute | solution.py:478
  105.0 9.2 %collective-permute-start.8 = (bf16[16,768]{1,0:T(8,128)(2,1)}, bf16[16,768]{1,0:T(8,128)(2,1)S(1)}, u32[]{:S(2)}, u32[]{:S(2)}) collective-permute-start(bf16[16,768]{1,0:T(8,128)(2,1)} %shard_map.203.refs_3_), channel_id=1, source_target_pairs={{0,2},{1,3},{2,4},{3,5},{4,6},{5,7},{6,0},{7,1},{8,10},{9,11},{10,... | collective-permute-start | bytes 73736 | tf_op jit(solution)/shard_map/ppermute | solution.py:478
  105.1 10.6 %collective-permute-start.9 = (bf16[16,768]{1,0:T(8,128)(2,1)}, bf16[16,768]{1,0:T(8,128)(2,1)S(1)}, u32[]{:S(2)}, u32[]{:S(2)}) collective-permute-start(bf16[16,768]{1,0:T(8,128)(2,1)} %shard_map.203.refs_3_), channel_id=1, source_target_pairs={{0,3},{1,4},{2,5},{3,6},{4,7},{5,0},{6,1},{7,2},{8,11},{9,12},{10,... | collective-permute-start | bytes 73736 | tf_op jit(solution)/shard_map/ppermute | solution.py:478
  108.3 7.4 %collective-permute-start.10 = (bf16[16,768]{1,0:T(8,128)(2,1)}, bf16[16,768]{1,0:T(8,128)(2,1)S(1)}, u32[]{:S(2)}, u32[]{:S(2)}) collective-permute-start(bf16[16,768]{1,0:T(8,128)(2,1)} %shard_map.203.refs_3_), channel_id=1, source_target_pairs={{0,4},{1,5},{2,6},{3,7},{4,0},{5,1},{6,2},{7,3},{8,12},{9,13},{10,... | collective-permute-start | bytes 73736 | tf_op jit(solution)/shard_map/ppermute | solution.py:478
  110.4 5.2 %collective-permute-start.11 = (bf16[16,768]{1,0:T(8,128)(2,1)}, bf16[16,768]{1,0:T(8,128)(2,1)S(1)}, u32[]{:S(2)}, u32[]{:S(2)}) collective-permute-start(bf16[16,768]{1,0:T(8,128)(2,1)} %shard_map.203.refs_3_), channel_id=1, source_target_pairs={{0,5},{1,6},{2,7},{3,0},{4,1},{5,2},{6,3},{7,4},{8,13},{9,14},{10,... | collective-permute-start | bytes 73736 | tf_op jit(solution)/shard_map/ppermute | solution.py:478
  113.3 4.1 %collective-permute-start.12 = (bf16[16,768]{1,0:T(8,128)(2,1)}, bf16[16,768]{1,0:T(8,128)(2,1)S(1)}, u32[]{:S(2)}, u32[]{:S(2)}) collective-permute-start(bf16[16,768]{1,0:T(8,128)(2,1)} %shard_map.203.refs_3_), channel_id=1, source_target_pairs={{0,6},{1,7},{2,0},{3,1},{4,2},{5,3},{6,4},{7,5},{8,14},{9,15},{10,... | collective-permute-start | bytes 73736 | tf_op jit(solution)/shard_map/ppermute | solution.py:478
  114.2 3.8 %collective-permute-start.13 = (bf16[16,768]{1,0:T(8,128)(2,1)}, bf16[16,768]{1,0:T(8,128)(2,1)S(1)}, u32[]{:S(2)}, u32[]{:S(2)}) collective-permute-start(bf16[16,768]{1,0:T(8,128)(2,1)} %shard_map.203.refs_3_), channel_id=1, source_target_pairs={{0,7},{1,0},{2,1},{3,2},{4,3},{5,4},{6,5},{7,6},{8,15},{9,8},{10,9... | collective-permute-start | bytes 73736 | tf_op jit(solution)/shard_map/ppermute | solution.py:478
  136.9 11.5 %copy-start.19 = (bf16[128,128]{1,0:T(8,128)(2,1)S(1)}, bf16[128,128]{1,0:T(8,128)(2,1)}, u32[]{:S(2)}) copy-start(bf16[128,128]{1,0:T(8,128)(2,1)} %v_ref.1) | copy-start | bytes 98308
  136.9 11.5 %copy-start.26 = (s32[1,16]{1,0:T(1,128)S(1)}, s32[1,16]{1,0:T(1,128)}, u32[]{:S(2)}) copy-start(s32[1,16]{1,0:T(1,128)} %param.35) | copy-start | bytes 196
  136.9 43.8 %all-to-all-start.4 = ((bf16[32,304,128]{2,1,0:T(8,128)(2,1)}), bf16[32,304,128]{2,1,0:T(8,128)(2,1)S(1)}, u32[]{:S(2)}, u32[]{:S(2)}) async-start(bf16[32,304,128]{2,1,0:T(8,128)(2,1)} %copy-done.4), calls=%async_computation.4 | async-start | bytes 4980736 | tf_op jit(solution)/shard_map/all_to_all | solution.py:403
  148.5 36.4 %copy-start.32 = (bf16[20,3,2048]{2,0,1:T(8,128)(2,1)S(1)}, bf16[20,3,2048]{2,0,1:T(8,128)(2,1)}, u32[]{:S(2)}) copy-start(bf16[20,3,2048]{2,0,1:T(8,128)(2,1)} %param.30) | copy-start | bytes 737284
  (31 other events, 126.7 us)
where the time goes:
time: 192 us; the launch traced here: 191 us
  starting transfers between devices  61 us (32%)
  waiting for transfers between devices  50.9 us (27%)
  Pallas kernels  46.5 us (24%)
  local copies, waits for them, and re-layouts  27.9 us (15%)
  other arithmetic  3.75 us (2%)
    all_to_all x5, waiting for transfers between devices, exchange(): return lax.all_to_all(blocks, axis, split_axis=0, concat_axis=0, tiled=True)  44 us
    all_to_all x5, starting transfers between devices, exchange(): return lax.all_to_all(blocks, axis, split_axis=0, concat_axis=0, tiled=True)  33.2 us
    ppermute x14, starting transfers between devices, turned(): lax.ppermute(value, 'tp', [(k, (k + step) % tp_count) for k in range(tp_c...  27.8 us
    unnamed x90, local copies, waits for them, and re-layouts  22.1 us
    pallas_call x1, Pallas kernels, attend(): pl.pallas_call(attend_kernel, in_specs=[pl.BlockSpec(memory_space=SMEM)]...  14.6 us
    pallas_call x3, Pallas kernels, pick(): pl.pallas_call(functools.partial(pick_kernel, len(sources)), in_specs=[pl...  12.1 us
    pallas_call x1, Pallas kernels, scan(): pl.pallas_call(functools.partial(scan_kernel, states), in_specs=[pl.Block...  11.9 us
    ppermute x14, waiting for transfers between devices, turned(): lax.ppermute(value, 'tp', [(k, (k + step) % tp_count) for k in range(tp_c...  6.87 us
  transfers between devices with their start and end apart: 19, of which 8 were waited for; matrix products, arithmetic and copies ran while one was open for 1% of the time, Pallas kernels for 22%

commit v1 on v0

--- a/solution.py
+++ b/solution.py
@@ -10,6 +10,7 @@
 
 HEAD_DIM = 128
 KVB = 128
+SMALL = 32
 LANES = 128
 BF = jnp.bfloat16
 F32 = jnp.float32
@@ -25,6 +26,52 @@
 
 def in_vmem(count):
     return [pl.BlockSpec(memory_space=VMEM) for _ in range(count)]
+
+
+def in_smem(count):
+    return [pl.BlockSpec(memory_space=SMEM) for _ in range(count)]
+
+
+def in_hbm(count):
+    return [pl.BlockSpec(memory_space=pltpu.HBM) for _ in range(count)]
+
+
+def whole(*arrays):
+    return [
+        pl.BlockSpec(a.shape, lambda i, n=len(a.shape): (0,) * n, pipeline_mode=pl.Buffered(1))
+        for a in arrays
+    ]
+
+
+def ask_kernel(entry_ref, block_ref, length_ref, out_ref, owner_ref, *, slots):
+    shape = out_ref.shape
+    owner_of = lax.broadcasted_iota(I32, shape, 0)
+    field_of = lax.broadcasted_iota(I32, shape, 2)
+    table = jnp.full(shape, -1, I32)
+    begin = jnp.int32(0)
+    for r in range(entry_ref.shape[0]):
+        owner = lax.div(entry_ref[r], slots)
+        slot = entry_ref[r] - owner * slots
+        owner_ref[r] = owner
+        fields = jnp.where(field_of == 0, slot, jnp.where(field_of == 1, begin, 0))
+        fields = jnp.where(field_of == 2, begin + length_ref[r], fields)
+        fields = jnp.where(field_of == 3, block_ref[r], fields)
+        table = jnp.where(owner_of == owner, fields, table)
+        begin = begin + length_ref[r]
+    out_ref[...] = table
+
+
+def ask(hit_entry, hit_blocks, lengths, slots, owner_count):
+    return pl.pallas_call(
+        functools.partial(ask_kernel, slots=slots),
+        in_specs=in_smem(3),
+        out_specs=in_vmem(1) + in_smem(1),
+        out_shape=[
+            jax.ShapeDtypeStruct((owner_count, 1, LANES), I32),
+            jax.ShapeDtypeStruct(hit_entry.shape, I32),
+        ],
+        compiler_params=params(4),
+    )(hit_entry, hit_blocks, lengths)
 
 
 def tiles_kernel(state_ref, out_ref, hold):
@@ -59,7 +106,7 @@
     blocks = out_ref.shape[0]
 
     def copies(i):
-        pick = jnp.maximum(asked_ref[i], 0)
+        pick = jnp.maximum(asked_ref[i, 0], 0)
         made, low = [], 0
         for n, source in enumerate(sources):
             rows = source.shape[1]
@@ -86,7 +133,7 @@
         functools.partial(pick_kernel, len(sources)),
         in_specs=[pl.BlockSpec(memory_space=SMEM)]
         + [pl.BlockSpec(memory_space=pl.ANY) for _ in sources],
-        out_specs=pl.BlockSpec(memory_space=pl.ANY),
+        out_specs=in_hbm(1)[0],
         out_shape=jax.ShapeDtypeStruct((blocks, rows, LANES), sources[0].dtype),
         scratch_shapes=[pltpu.SemaphoreType.DMA((blocks, len(sources)))],
         compiler_params=params(4),
@@ -148,7 +195,9 @@
     tail_rows = got_conv.shape[0]
     return pl.pallas_call(
         conv_kernel,
-        in_specs=[pl.BlockSpec(memory_space=SMEM)] + in_vmem(6),
+        grid=(1,),
+        in_specs=in_smem(1)
+        + whole(x_rows, got_conv, choose, conv_weight, dt_in_weight, bc_weight),
         out_specs=in_vmem(10),
         out_shape=[jax.ShapeDtypeStruct((tokens // 8, width), F32)] * 8
         + [
@@ -194,7 +243,7 @@
     pieces = refs[3:11]
     (mixed_ref, weight_ref, bias_ref, decay_ref, skip_ref, start_ref, tail_ref) = refs[11:18]
     out_ref, back_ref = refs[18:20]
-    low_dt, maps, map_smem, rates, drives, sums, decays, hold, sem = refs[20:]
+    low_dt, maps, map_smem, rates, drives, sums, decays, ready, sem, sems = refs[20:]
     tokens, channels = mixed_ref.shape
     groups = channels // LANES
     share = tokens // 8
@@ -224,8 +273,19 @@
             rows = pl.ds(low // LANES + j, tokens, stride=groups)
             rates[rows, :] = rate[:, j * LANES : (j + 1) * LANES]
             drives[rows, :] = drive[:, j * LANES : (j + 1) * LANES]
-    back_ref[:, states * groups :, :] = tail_ref[...]
     copy.wait()
+    state_rows = states * groups
+
+    def send(r):
+        owner = owner_ref[r]
+        return (
+            pltpu.make_async_copy(
+                ready.at[r], back_ref.at[owner, pl.ds(0, state_rows)], sems.at[r, 0]
+            ),
+            pltpu.make_async_copy(
+                tail_ref.at[owner], back_ref.at[owner, pl.ds(state_rows, 3 * groups)], sems.at[r, 1]
+            ),
+        )
 
     def segment(r, begin):
         finish = begin + length_ref[r]
@@ -249,7 +309,9 @@
 
         held = lax.fori_loop(begin, finish, token, held)
         for n in range(states):
-            back_ref[owner, n * groups : (n + 1) * groups, :] = held[n].astype(BF)
+            ready[r, n * groups : (n + 1) * groups, :] = held[n].astype(BF)
+        for copy in send(r):
+            copy.start()
         return finish
 
     lax.fori_loop(0, length_ref.shape[0], segment, jnp.int32(0))
@@ -259,6 +321,9 @@
             sums[pl.ds(j, tokens, stride=groups), :]
             + skip_ref[:, cut] * mixed_ref[:, cut].astype(F32)
         ).astype(BF)
+    for r in range(length_ref.shape[0]):
+        for copy in send(r):
+            copy.wait()
 
 
 def scan(
@@ -272,8 +337,11 @@
     tail_rows = tails.shape[1]
     return pl.pallas_call(
         functools.partial(scan_kernel, states),
-        in_specs=[pl.BlockSpec(memory_space=SMEM)] * 3 + in_vmem(15),
-        out_specs=in_vmem(2),
+        grid=(1,),
+        in_specs=in_smem(3)
+        + whole(*pieces, mixed, dt_weight, dt_bias[None, :], decay_rates, skip_gain[None, :])
+        + whole(start, tails),
+        out_specs=in_vmem(1) + in_hbm(1),
         out_shape=[
             jax.ShapeDtypeStruct((tokens, channels), BF),
             jax.ShapeDtypeStruct((owners_count, states * groups + tail_rows, LANES), BF),
@@ -286,8 +354,9 @@
             VMEM((tokens * groups, LANES), F32),
             VMEM((tokens * groups, LANES), F32),
             VMEM((states * groups, LANES), F32),
-            VMEM((8, LANES), F32),
+            VMEM((lengths.shape[0], states * groups, LANES), BF),
             pltpu.SemaphoreType.DMA,
+            pltpu.SemaphoreType.DMA((lengths.shape[0], 2)),
         ],
         compiler_params=params(32),
     )(
@@ -296,107 +365,253 @@
     )
 
 
-def attend_kernel(length_ref, owner_ref, live_ref, q_ref, k_ref, v_ref, prefix_ref, out_ref, rows_q, rows_o):
-    tokens = q_ref.shape[0]
-    heads = q_ref.shape[1] // HEAD_DIM
-    prefix = prefix_ref.shape[1] // 2
-    for h in range(heads):
-        rows_q[h * tokens : (h + 1) * tokens, :] = q_ref[:, h * HEAD_DIM : (h + 1) * HEAD_DIM]
+def attend_kernel(
+    asked_ref, rows_ref, key_ref, value_ref, pass_ref, out_ref, pass_out, who, rows, prefix, done, sems
+):
+    count, tokens, _ = rows.shape
+    heads = done.shape[2] // HEAD_DIM
+    held = prefix.shape[1] // 2
+    half = done.shape[1]
+    pass_out[...] = pass_ref[...]
+
+    def arrivals(i):
+        row = who[i]
+        slot = jnp.maximum(asked_ref[row, 0], 0)
+        return (
+            pltpu.make_async_copy(
+                rows_ref.at[pl.ds(pl.multiple_of(row * tokens, tokens), tokens)],
+                rows.at[i],
+                sems.at[i, 0],
+            ),
+            pltpu.make_async_copy(key_ref.at[slot], prefix.at[i, pl.ds(0, held)], sems.at[i, 1]),
+            pltpu.make_async_copy(
+                value_ref.at[slot], prefix.at[i, pl.ds(held, held)], sems.at[i, 2]
+            ),
+        )
+
+    def departure(i):
+        return pltpu.make_async_copy(done.at[i], out_ref.at[who[i]], sems.at[i, 3])
+
+    found = jnp.int32(0)
+    for row in range(asked_ref.shape[0]):
+        who[found] = row
+        found = found + jnp.where(asked_ref[row, 0] >= 0, 1, 0)
+    for i in range(count):
+        for copy in arrivals(i):
+            copy.start()
+    factor = HEAD_DIM**-0.5 * math.log2(math.e)
     contract = (((1,), (1,)), ((), ()))
-    scale = HEAD_DIM**-0.5
-    many = heads * tokens
-    new_scores = lax.dot_general(
-        rows_q[...], k_ref[...], contract, preferred_element_type=F32
-    ) * scale
-    query_of = lax.rem(lax.broadcasted_iota(I32, (many, tokens), 0), tokens)
-    key_of = lax.broadcasted_iota(I32, (many, tokens), 1)
-    new_scores = jnp.where(key_of <= query_of, new_scores, -1e30)
-    token_of = lax.rem(lax.broadcasted_iota(I32, (many, HEAD_DIM), 0), tokens)
-    place_of = lax.broadcasted_iota(I32, (many, prefix), 1)
-    rows_o[...] = jnp.zeros((many, HEAD_DIM), F32)
-
-    def request(r, begin):
+    wide = heads * HEAD_DIM
+
+    def part(i, window):
+        row = who[i]
+        begin, finish, live = asked_ref[row, 1], asked_ref[row, 2], asked_ref[row, 3] * KVB
+        first = jnp.minimum(lax.div(begin, 16), (tokens - window) // 16)
+        low = pl.multiple_of(first * 16, 16)
+        many = heads * window
+        q = jnp.concatenate(
+            [
+                rows[i, pl.ds(low, window), h * HEAD_DIM : (h + 1) * HEAD_DIM]
+                for h in range(heads)
+            ],
+            axis=0,
+        )
+        token_of = lax.broadcasted_iota(I32, (window, tokens), 0) + low
+        key_of = lax.broadcasted_iota(I32, (window, tokens), 1)
+        hidden = jnp.where((key_of >= begin) & (key_of <= token_of), 0.0, -1e30)
+        hidden = jnp.concatenate([hidden] * heads, axis=0)
+        old = lax.dot_general(q, prefix[i, 0:held, :], contract, preferred_element_type=F32)
+        new = lax.dot_general(
+            q, rows[i, :, wide : wide + HEAD_DIM], contract, preferred_element_type=F32
+        )
+        new = jnp.where(hidden < 0.0, -1e30, new)
+        tiles = [
+            old[:, b * KVB : (b + 1) * KVB] if b == 0
+            else jnp.where(live > b * KVB, old[:, b * KVB : (b + 1) * KVB], -1e30)
+            for b in range(held // KVB)
+        ] + [new]
+        highest = functools.reduce(jnp.maximum, tiles)
+        highest = jnp.max(highest, axis=1, keepdims=True)
+        tiles = [jnp.exp2((tile - highest) * factor) for tile in tiles]
+        inverse = 1.0 / jnp.sum(functools.reduce(jnp.add, tiles), axis=1, keepdims=True)
+        result = jnp.dot(
+            jnp.concatenate([tile.astype(BF) for tile in tiles[:-1]], axis=1),
+            prefix[i, held:, :],
+            preferred_element_type=F32,
+        ) + jnp.dot(
+            tiles[-1].astype(BF),
+            rows[i, :, wide + HEAD_DIM : wide + 2 * HEAD_DIM],
+            preferred_element_type=F32,
+        )
+        result = result * inverse
+        result = jnp.concatenate(
+            [result[h * window : (h + 1) * window] for h in range(heads)], axis=1
+        )
+        for k in range(min(window, half) // 16):
+            block = result[k * 16 : (k + 1) * 16]
+            if k == 0 and window > half:
+                near = lax.broadcasted_iota(I32, (16, wide), 0) + low
+                block = jnp.where((near >= begin) & (near < finish), block, result[half:])
+            place = pl.multiple_of(lax.rem(first + k, half // 16) * 16, 16)
+            done[i, pl.ds(place, 16), :] = block.astype(BF)
+
+    def request(i, carry):
+        row = who[i]
+        for copy in arrivals(i):
+            copy.wait()
+        low = jnp.minimum(lax.div(asked_ref[row, 1], 16), (tokens - SMALL) // 16) * 16
+        fits = asked_ref[row, 2] <= low + SMALL
+
+        @pl.when(fits)
+        def _():
+            part(i, SMALL)
+
+        @pl.when(jnp.logical_not(fits))
+        def _():
+            part(i, half + 16)
+
+        departure(i).start()
+        return carry
+
+    lax.fori_loop(0, count, request, 0)
+    for i in range(count):
+        departure(i).wait()
+
+
+def attend(asked, all_rows, store_keys, store_values, passed, count, tokens):
+    owner_count = asked.shape[0]
+    wide = all_rows.shape[1] - 2 * HEAD_DIM
+    half = tokens // 2
+    return pl.pallas_call(
+        attend_kernel,
+        in_specs=in_smem(1) + in_hbm(3) + in_vmem(1),
+        out_specs=in_hbm(1) + in_vmem(1),
+        out_shape=[
+            jax.ShapeDtypeStruct((owner_count, half, wide), BF),
+            jax.ShapeDtypeStruct(passed.shape, passed.dtype),
+        ],
+        scratch_shapes=[
+            SMEM((count + 1,), I32),
+            VMEM((count, tokens, all_rows.shape[1]), BF),
+            VMEM((count, 2 * store_keys.shape[1], HEAD_DIM), BF),
+            VMEM((count, half, wide), BF),
+            pltpu.SemaphoreType.DMA((count, 4)),
+        ],
+        compiler_params=params(32),
+    )(asked, all_rows, store_keys, store_values, passed)
+
+
+def settle_kernel(length_ref, owner_ref, got_ref, out_ref, held, sems):
+    half = got_ref.shape[1]
+    count = length_ref.shape[0]
+    copies = [
+        pltpu.make_async_copy(got_ref.at[owner_ref[r]], held.at[r], sems.at[r])
+        for r in range(count)
+    ]
+    for copy in copies:
+        copy.start()
+    place = lax.broadcasted_iota(I32, (half, got_ref.shape[2]), 0)
+    lower = jnp.zeros((half, got_ref.shape[2]), F32)
+    upper = lower
+    begin = jnp.int32(0)
+    for r, copy in enumerate(copies):
+        copy.wait()
         finish = begin + length_ref[r]
-        owner = owner_ref[r]
-        live = live_ref[r] * KVB
-        old = lax.dot_general(
-            rows_q[...], prefix_ref[owner, 0:prefix, :], contract, preferred_element_type=F32
-        ) * scale
-        old = jnp.where(place_of < live, old, -1e30)
-        new = jnp.where(key_of >= begin, new_scores, -1e30)
-        highest = jnp.maximum(
-            jnp.max(old, axis=1, keepdims=True), jnp.max(new, axis=1, keepdims=True)
-        )
-        old, new = jnp.exp(old - highest), jnp.exp(new - highest)
-        total = jnp.sum(old, axis=1, keepdims=True) + jnp.sum(new, axis=1, keepdims=True)
-        inverse = 1.0 / total
-        result = jnp.dot(
-            (old * inverse).astype(BF), prefix_ref[owner, prefix:, :], preferred_element_type=F32
-        ) + jnp.dot((new * inverse).astype(BF), v_ref[...], preferred_element_type=F32)
-        mine = (token_of >= begin) & (token_of < finish)
-        rows_o[...] = jnp.where(mine, result, rows_o[...])
-        return finish
-
-    lax.fori_loop(0, length_ref.shape[0], request, jnp.int32(0))
-    for h in range(heads):
-        out_ref[:, h * HEAD_DIM : (h + 1) * HEAD_DIM] = rows_o[
-            h * tokens : (h + 1) * tokens, :
-        ].astype(BF)
-
-
-def attend(lengths, owners, live, queries, new_keys, new_values, prefix):
-    tokens, width = queries.shape
-    many = tokens * width // HEAD_DIM
-    return pl.pallas_call(
-        attend_kernel,
-        in_specs=[pl.BlockSpec(memory_space=SMEM)] * 3 + in_vmem(4),
-        out_specs=pl.BlockSpec(memory_space=VMEM),
-        out_shape=jax.ShapeDtypeStruct((tokens, width), BF),
-        scratch_shapes=[VMEM((many, HEAD_DIM), BF), VMEM((many, HEAD_DIM), F32)],
-        compiler_params=params(32),
-    )(lengths, owners, live, queries, new_keys, new_values, prefix)
-
-
-def write_kernel(source_ref, store_ref, back_ref, out_ref, hold):
-    step, states, channels = out_ref.shape
+        block = held[r].astype(F32)
+        lower = jnp.where((place >= begin) & (place < finish), block, lower)
+        upper = jnp.where((place >= begin - half) & (place < finish - half), block, upper)
+        begin = finish
+    out_ref[0:half, :] = lower.astype(BF)
+    out_ref[half:, :] = upper.astype(BF)
+
+
+def settle(lengths, owners, got):
+    count = lengths.shape[0]
+    _, half, width = got.shape
+    return pl.pallas_call(
+        settle_kernel,
+        in_specs=in_smem(2) + in_hbm(1),
+        out_specs=in_vmem(1)[0],
+        out_shape=jax.ShapeDtypeStruct((2 * half, width), BF),
+        scratch_shapes=[VMEM((count, half, width), BF), pltpu.SemaphoreType.DMA((count,))],
+        compiler_params=params(8),
+    )(lengths, owners, got)
+
+
+def write_kernel(asked_ref, store_ref, conv_ref, back_ref, out_ref, conv_out, source, hold, stage, tails, sems):
+    slots, states, channels = out_ref.shape
     groups = channels // LANES
-    first = pl.program_id(0) * step
-    for e in range(step):
-        row = source_ref[first + e]
-
-        @pl.when(row < 0)
+    rows = states * groups
+    for s in range(slots):
+        source[s] = -1
+    for row in range(asked_ref.shape[0]):
+        slot = asked_ref[row, 0]
+
+        @pl.when(slot >= 0)
         def _():
-            out_ref[e] = store_ref[e]
+            source[slot] = row
+
+    def kept(s):
+        return pltpu.make_async_copy(store_ref.at[s], out_ref.at[s], sems.at[s])
+
+    def changed(s):
+        return pltpu.make_async_copy(stage.at[s], out_ref.at[s], sems.at[s])
+
+    for s in range(slots):
+
+        @pl.when(source[s] < 0)
+        def _():
+            kept(s).start()
+            tails[s * 3 * groups : (s + 1) * 3 * groups, :] = jnp.zeros((3 * groups, LANES), F32)
+
+    landed = jnp.zeros((slots, LANES), I32)
+    slot_of = lax.broadcasted_iota(I32, (slots, LANES), 0)
+    for s in range(slots):
+        row = source[s]
+        landed = jnp.where(slot_of == s, row + 1, landed)
 
         @pl.when(row >= 0)
         def _():
-            hold[...] = back_ref[row, 0 : states * groups, :].astype(F32)
+            hold[s % 2] = back_ref[row, 0:rows, :].astype(F32)
             for low in range(0, states, 8):
                 for j in range(groups):
-                    out_ref[e, low : low + 8, j * LANES : (j + 1) * LANES] = hold[
-                        pl.ds(low * groups + j, 8, stride=groups), :
+                    stage[s, low : low + 8, j * LANES : (j + 1) * LANES] = hold[
+                        s % 2, pl.ds(low * groups + j, 8, stride=groups), :
                     ]
-
-
-def write_state(source, store_state, back):
+            changed(s).start()
+            tails[s * 3 * groups : (s + 1) * 3 * groups, :] = back_ref[row, rows:, :].astype(F32)
+
+    for i in range(3):
+        for j in range(groups):
+            cut = slice(j * LANES, (j + 1) * LANES)
+            fresh = tails[pl.ds(i * groups + j, slots, stride=3 * groups), :]
+            conv_out[i, :, cut] = jnp.where(
+                landed > 0, fresh, conv_ref[i, :, cut].astype(F32)
+            ).astype(BF)
+    for s in range(slots):
+        changed(s).wait()
+
+
+def write_store(asked, store_state, conv_rows, back):
     slots, states, channels = store_state.shape
-    rows = states * channels // LANES
-    step = 4
+    groups = channels // LANES
     return pl.pallas_call(
         write_kernel,
-        grid_spec=pltpu.PrefetchScalarGridSpec(
-            num_scalar_prefetch=1,
-            grid=(slots // step,),
-            in_specs=[
-                pl.BlockSpec((step, states, channels), lambda i, s: (i, 0, 0)),
-                pl.BlockSpec(memory_space=VMEM),
-            ],
-            out_specs=pl.BlockSpec((step, states, channels), lambda i, s: (i, 0, 0)),
-            scratch_shapes=[VMEM((rows, LANES), F32)],
-        ),
-        out_shape=jax.ShapeDtypeStruct((slots, states, channels), F32),
+        in_specs=in_smem(1) + in_hbm(1) + in_vmem(2),
+        out_specs=in_hbm(1) + in_vmem(1),
+        out_shape=[
+            jax.ShapeDtypeStruct((slots, states, channels), F32),
+            jax.ShapeDtypeStruct(conv_rows.shape, BF),
+        ],
+        scratch_shapes=[
+            SMEM((slots,), I32),
+            VMEM((2, states * groups, LANES), F32),
+            VMEM((slots, states, channels), F32),
+            VMEM((slots * 3 * groups, LANES), F32),
+            pltpu.SemaphoreType.DMA((slots,)),
+        ],
         compiler_params=params(24),
-    )(source, store_state, back)
+    )(asked, store_state, conv_rows, back)
 
 
 def exchange(blocks, axis):
@@ -456,17 +671,16 @@
     groups = channels // LANES
     tokens = x_in.shape[0]
     lengths = seg_lengths[0]
-    owners = hit_entry // slot_count
-    slots = hit_entry - owners * slot_count
-    owner_ids = jnp.arange(owner_count, dtype=I32)
-    served = owner_ids[:, None] == owners[None, :]
-    table = jnp.sum(jnp.where(served, slots[None, :] + 1, 0), axis=1, dtype=I32) - 1
-    asked = exchange(table[:, None], "cache")[:, 0]
+    request_count = lengths.shape[0]
+    table, owners = ask(hit_entry, hit_blocks, lengths, slot_count, owner_count)
+    asked = exchange(table, "cache")[:, 0, :]
+    all_rows = lax.all_gather(
+        jnp.concatenate([queries, new_keys, new_values], axis=1), "cache", tiled=True
+    )
 
     conv_tiles = store_conv.reshape(slot_count, 3 * groups, LANES)
     got_conv = exchange(pick(asked, conv_tiles), "cache")
     got_state = exchange(pick(asked, state_tiles(store_state)), "cache")
-    got_prefix = exchange(pick(asked, store_keys, store_values), "cache")
 
     width = tokens + -(-3 * owner_count // LANES) * LANES
     choose = choose_matrix(lengths, owners, tokens, owner_count, width)
@@ -479,6 +693,10 @@
 
     parts = [parts[0]] + [turned(step, parts[step]) for step in range(1, tp_count)]
     summed = sum_parts(parts)
+    attended, summed = attend(
+        asked, all_rows, store_keys, store_values, summed, request_count, tokens
+    )
+    got_attended = exchange(attended, "cache")
     pieces = [summed] + [turned(step, summed) for step in range(1, tp_count)]
 
     mixer_out, back = scan(
@@ -486,18 +704,9 @@
         got_state, tails.reshape(owner_count, 3 * groups, LANES),
     )
     back = exchange(back, "cache")
-    attn_out = attend(lengths, owners, hit_blocks, queries, new_keys, new_values, got_prefix)
-
-    slot_ids = jnp.arange(slot_count, dtype=I32)
-    landing = asked[None, :] == slot_ids[:, None]
-    source = jnp.sum(jnp.where(landing, owner_ids[None, :] + 1, 0), axis=1, dtype=I32) - 1
-    new_state = write_state(source, store_state, back)
-    back_conv = back[:, states * groups :, :]
-    placed_conv = jnp.take(back_conv, jnp.maximum(source, 0), axis=0, mode="clip")
-    new_conv = jnp.where(
-        (source >= 0)[:, None, None], placed_conv.reshape(store_conv.shape), store_conv
-    )
-    return (mixer_out, attn_out, new_state, new_conv)
+    attn_out = settle(lengths, owners, got_attended)
+    new_state, conv_rows = write_store(asked, store_state, store_conv.transpose(1, 0, 2), back)
+    return (mixer_out, attn_out, new_state, conv_rows.transpose(1, 0, 2))
 
 
 def solution(mesh):

time: 192 us -> 217 us (1.13)
  between operations: 1.2 us -> 14.4 us
  waiting for transfers between devices: 50.9 us -> 57.3 us
  Pallas kernels: 46.5 us -> 50.6 us
  starting transfers between devices: 61 us -> 64.3 us
    pallas_call x4 -> x6, Pallas kernels: 31.9 us -> 42.2 us  [the longest x1 16.8 us: attend(): pl.pallas_call(attend_kernel, in_specs=in_smem(1) + in_hbm(3) + in_vmem(1...]
    all_gather x0 -> x1, waiting for transfers between devices: none -> 10.2 us  [shards(): lax.all_gather(jnp.concatenate([queries, new_keys, new_values], axis=1),...]
    pallas_call x3 -> x2, Pallas kernels: 12.1 us -> 5.81 us  [pick(): pl.pallas_call(functools.partial(pick_kernel, len(sources)), in_specs=[pl...]
    ppermute x14, starting transfers between devices: 27.8 us -> 32.5 us  [turned(): lax.ppermute(value, 'tp', [(k, (k + step) % tp_count) for k in range(tp_c...]
    all_to_all x5, waiting for transfers between devices: 44 us -> 39.5 us  [exchange(): return lax.all_to_all(blocks, axis, split_axis=0, concat_axis=0, tiled=True)]
    unnamed x90 -> x77, local copies, waits for them, and re-layouts: 22.1 us -> 26.2 us
    gather x1 -> x0, local copies, waits for them, and re-layouts: 2.28 us -> none  [shards(): jnp.take(back_conv, jnp.maximum(source, 0), axis=0, mode='clip')]
  transfers between devices with their start and end apart: 19 -> 20, of which waited for: 8 -> 9; matrix products, arithmetic and copies ran while one was open for 1% -> 1% of each run, Pallas kernels for 22% -> 21%
where the time goes in v1:
time: 217 us; the launch traced here: 216 us
  starting transfers between devices  64.3 us (30%)
  waiting for transfers between devices  57.3 us (26%)
  Pallas kernels  50.6 us (23%)
  local copies, waits for them, and re-layouts  26.7 us (12%)
  between operations  14.4 us (7%)
  other arithmetic  2.44 us (1%)
    all_to_all x5, waiting for transfers between devices, exchange(): return lax.all_to_all(blocks, axis, split_axis=0, concat_axis=0, tiled=True)  39.5 us
    ppermute x14, starting transfers between devices, turned(): lax.ppermute(value, 'tp', [(k, (k + step) % tp_count) for k in range(tp_c...  32.5 us
    all_to_all x5, starting transfers between devices, exchange(): return lax.all_to_all(blocks, axis, split_axis=0, concat_axis=0, tiled=True)  31.7 us
    unnamed x77, local copies, waits for them, and re-layouts  26.2 us
    pallas_call x1, Pallas kernels, attend(): pl.pallas_call(attend_kernel, in_specs=in_smem(1) + in_hbm(3) + in_vmem(1...  16.8 us
    pallas_call x1, Pallas kernels, scan(): pl.pallas_call(functools.partial(scan_kernel, states), grid=(1,), in_spec...  15 us
    all_gather x1, waiting for transfers between devices, shards(): lax.all_gather(jnp.concatenate([queries, new_keys, new_values], axis=1),...  10.2 us
    ppermute x14, waiting for transfers between devices, turned(): lax.ppermute(value, 'tp', [(k, (k + step) % tp_count) for k in range(tp_c...  7.64 us
  transfers between devices with their start and end apart: 20, of which 9 were waited for; matrix products, arithmetic and copies ran while one was open for 1% of the time, Pallas kernels for 21%

profile of v1, /device:TPU:1, one launch (start us, length us, event | category | flops | bytes accessed | tf_op | source)
XLA Modules:
  0.0 215.8 jit_solution(8865898092947538605)
XLA Ops:
  7.2 1.8 pad_maximum_fusion
  12.3 8.6 %all-to-all-start = ((s32[32,1,128]{2,1,0:T(1,128)}), s32[32,1,128]{2,1,0:T(1,128)S(1)}, u32[]{:S(2)}, u32[]{:S(2)}) async-start(s32[32,1,128]{2,1,0:T(1,128)} %get-tuple-element.23), calls=%async_computation | async-start | bytes 32768 | tf_op jit(solution)/shard_map/all_to_all | solution.py:618
  22.4 5.4 %all-to-all-done = s32[32,1,128]{2,1,0:T(1,128)S(1)} async-done(((s32[32,1,128]{2,1,0:T(1,128)}), s32[32,1,128]{2,1,0:T(1,128)S(1)}, u32[]{:S(2)}, u32[]{:S(2)}) %all-to-all-start) | async-done | bytes 16416 | tf_op jit(solution)/shard_map/all_to_all | solution.py:618
  27.8 1.8 shard_map.202
  29.6 4.2 %all-to-all-start.1 = ((bf16[32,48,128]{2,1,0:T(8,128)(2,1)}), bf16[32,48,128]{2,1,0:T(8,128)(2,1)S(1)}, u32[]{:S(2)}, u32[]{:S(2)}) async-start(bf16[32,48,128]{2,1,0:T(8,128)(2,1)} %shard_map.202), calls=%async_computation.1 | async-start | bytes 786432 | tf_op jit(solution)/shard_map/all_to_all | solution.py:618
  35.1 4.0 %shard_map.207 = bf16[32,256,128]{2,1,0:T(8,128)(2,1)S(1)} custom-call(s32[32,128]{1,0:T(8,128)S(1)} %bitcast.21, bf16[20,256,128]{2,1,0:T(8,128)(2,1)S(1)} %shard_map.206.refs_0_), custom_call_target="tpu_custom_call" | custom-call | tf_op jit(solution)/shard_map/pallas_call | solution.py:132
  40.4 4.3 %all-to-all-done.1 = bf16[32,48,128]{2,1,0:T(8,128)(2,1)S(1)} async-done(((bf16[32,48,128]{2,1,0:T(8,128)(2,1)}), bf16[32,48,128]{2,1,0:T(8,128)(2,1)S(1)}, u32[]{:S(2)}, u32[]{:S(2)}) %all-to-all-start.1) | async-done | bytes 393248 | tf_op jit(solution)/shard_map/all_to_all | solution.py:618
  44.7 4.6 %all-to-all-start.2 = ((bf16[32,256,128]{2,1,0:T(8,128)(2,1)}), bf16[32,256,128]{2,1,0:T(8,128)(2,1)}, u32[]{:S(2)}, u32[]{:S(2)}) async-start(bf16[32,256,128]{2,1,0:T(8,128)(2,1)} %copy-done.1), calls=%async_computation.2 | async-start | bytes 4194304 | tf_op jit(solution)/shard_map/all_to_all | solution.py:618
  49.9 1.6 copy-done.5
  54.2 2.0 shard_map.203
  57.6 1.6 collective-permute-start
  59.2 2.9 %collective-permute-start.1 = (f32[16,640]{1,0:T(8,128)S(1)}, f32[16,640]{1,0:T(8,128)S(1)}, u32[]{:S(2)}, u32[]{:S(2)}) collective-permute-start(f32[16,640]{1,0:T(8,128)S(1)} %get-tuple-element.26), channel_id=1, source_target_pairs={{0,2},{1,3},{2,4},{3,5},{4,6},{5,7},{6,0},{7,1},{8,10},{9,11},{10,... | collective-permute-start | bytes 122888 | tf_op jit(solution)/shard_map/ppermute | solution.py:692
  62.0 3.5 %collective-permute-start.2 = (f32[16,640]{1,0:T(8,128)S(1)}, f32[16,640]{1,0:T(8,128)S(1)}, u32[]{:S(2)}, u32[]{:S(2)}) collective-permute-start(f32[16,640]{1,0:T(8,128)S(1)} %get-tuple-element.27), channel_id=1, source_target_pairs={{0,3},{1,4},{2,5},{3,6},{4,7},{5,0},{6,1},{7,2},{8,11},{9,12},{10,... | collective-permute-start | bytes 122888 | tf_op jit(solution)/shard_map/ppermute | solution.py:692
  66.1 4.5 %collective-permute-start.4 = (f32[16,640]{1,0:T(8,128)S(1)}, f32[16,640]{1,0:T(8,128)S(1)}, u32[]{:S(2)}, u32[]{:S(2)}) collective-permute-start(f32[16,640]{1,0:T(8,128)S(1)} %get-tuple-element.29), channel_id=1, source_target_pairs={{0,5},{1,6},{2,7},{3,0},{4,1},{5,2},{6,3},{7,4},{8,13},{9,14},{10,... | collective-permute-start | bytes 122888 | tf_op jit(solution)/shard_map/ppermute | solution.py:692
  70.6 2.4 %collective-permute-start.5 = (f32[16,640]{1,0:T(8,128)S(1)}, f32[16,640]{1,0:T(8,128)S(1)}, u32[]{:S(2)}, u32[]{:S(2)}) collective-permute-start(f32[16,640]{1,0:T(8,128)S(1)} %get-tuple-element.30), channel_id=1, source_target_pairs={{0,6},{1,7},{2,0},{3,1},{4,2},{5,3},{6,4},{7,5},{8,14},{9,15},{10,... | collective-permute-start | bytes 122888 | tf_op jit(solution)/shard_map/ppermute | solution.py:692
  74.4 3.4 %collective-permute-done.5.refs_6_ = f32[16,640]{1,0:T(8,128)S(1)} collective-permute-done((f32[16,640]{1,0:T(8,128)S(1)}, f32[16,640]{1,0:T(8,128)S(1)}, u32[]{:S(2)}, u32[]{:S(2)}) %collective-permute-start.5) | collective-permute-done | bytes 40992 | tf_op jit(solution)/shard_map/ppermute | solution.py:692
  78.8 1.6 shard_map.204.pass_ref
  80.4 10.2 %all-gather.2.cloned.1.call-done.rows_ref = bf16[4096,768]{1,0:T(8,128)(2,1)} async-done(((bf16[128,768]{1,0:T(8,128)(2,1)}), bf16[4096,768]{1,0:T(8,128)(2,1)}) %all-gather.2.cloned.1.call-update) | async-done | bytes 6291472 | tf_op jit(solution)/shard_map/all_gather | solution.py:677
  90.6 2.8 %copy-done.2 = bf16[4096,768]{1,0:T(8,128)(2,1)S(1)} copy-done((bf16[4096,768]{1,0:T(8,128)(2,1)S(1)}, bf16[4096,768]{1,0:T(8,128)(2,1)}, u32[]{:S(2)}) %copy-start.2) | copy-done | bytes 6291480
  96.8 16.8 %shard_map.205 = (bf16[32,64,512]{2,1,0:T(8,128)(2,1)S(1)}, bf16[16,768]{1,0:T(8,128)(2,1)S(1)}) custom-call(s32[32,128]{1,0:T(8,128)S(1)} %bitcast.22, bf16[4096,768]{1,0:T(8,128)(2,1)S(1)} %copy-done.2, bf16[20,256,128]{2,1,0:T(8,128)(2,1)S(1)} %copy-done.7, bf16[20,256,128]{2,1,0:T(8,128)(2,1)S(1)} %copy-done.8, bf16[16,768]{1,0:T(8,128)(2,1)S(1)} %copy-done.15), custom_call_target="tpu_custom_call" | custom-call | tf_op jit(solution)/shard_map/pallas_call | solution.py:485
  115.5 5.3 %all-to-all-start.3 = ((bf16[32,64,512]{2,1,0:T(8,128)(2,1)}), bf16[32,64,512]{2,1,0:T(8,128)(2,1)}, u32[]{:S(2)}, u32[]{:S(2)}) async-start(bf16[32,64,512]{2,1,0:T(8,128)(2,1)} %copy-done.6), calls=%async_computation.3 | async-start | bytes 4194304 | tf_op jit(solution)/shard_map/all_to_all | solution.py:618
  120.9 5.0 %collective-permute-start.13 = (bf16[16,768]{1,0:T(8,128)(2,1)}, bf16[16,768]{1,0:T(8,128)(2,1)S(1)}, u32[]{:S(2)}, u32[]{:S(2)}) collective-permute-start(bf16[16,768]{1,0:T(8,128)(2,1)} %copy-done.18), channel_id=1, source_target_pairs={{0,7},{1,0},{2,1},{3,2},{4,3},{5,4},{6,5},{7,6},{8,15},{9,8},{10,9... | collective-permute-start | bytes 73736 | tf_op jit(solution)/shard_map/ppermute | solution.py:692
  127.1 1.5 collective-permute-start.11
  128.6 3.4 %collective-permute-start.10 = (bf16[16,768]{1,0:T(8,128)(2,1)}, bf16[16,768]{1,0:T(8,128)(2,1)S(1)}, u32[]{:S(2)}, u32[]{:S(2)}) collective-permute-start(bf16[16,768]{1,0:T(8,128)(2,1)} %copy-done.18), channel_id=1, source_target_pairs={{0,4},{1,5},{2,6},{3,7},{4,0},{5,1},{6,2},{7,3},{8,12},{9,13},{10,... | collective-permute-start | bytes 73736 | tf_op jit(solution)/shard_map/ppermute | solution.py:692
  132.0 3.2 %collective-permute-start.8 = (bf16[16,768]{1,0:T(8,128)(2,1)}, bf16[16,768]{1,0:T(8,128)(2,1)S(1)}, u32[]{:S(2)}, u32[]{:S(2)}) collective-permute-start(bf16[16,768]{1,0:T(8,128)(2,1)} %copy-done.18), channel_id=1, source_target_pairs={{0,2},{1,3},{2,4},{3,5},{4,6},{5,7},{6,0},{7,1},{8,10},{9,11},{10,... | collective-permute-start | bytes 73736 | tf_op jit(solution)/shard_map/ppermute | solution.py:692
  136.7 1.7 collective-permute-done.9.refs_6_
  140.4 1.6 copy-done.4
  146.4 15.0 %shard_map.208 = (bf16[128,2048]{1,0:T(8,128)(2,1)}, bf16[32,304,128]{2,1,0:T(8,128)(2,1)S(1)}) custom-call(s32[1]{0:T(128)} %bitcast.rank_ref.refs_0_, s32[16]{0:T(128)S(1)} %bitcast.30, s32[16]{0:T(128)S(1)} %copy-done.27, bf16[16,768]{1,0:T(8,128)(2,1)S(1)} %copy-done.19, bf16[16,768]{1,0:T(8,128)(2,1)S(1)} %collective-permute-done.7.refs_4_, ...), custom_call_target="tpu_custom_call" | custom-call | tf_op jit(solution)/shard_map/pallas_call | solution.py:338
  162.9 9.0 %all-to-all-start.4 = ((bf16[32,304,128]{2,1,0:T(8,128)(2,1)}), bf16[32,304,128]{2,1,0:T(8,128)(2,1)}, u32[]{:S(2)}, u32[]{:S(2)}) async-start(bf16[32,304,128]{2,1,0:T(8,128)(2,1)} %copy-done.3), calls=%async_computation.4 | async-start | bytes 4980736 | tf_op jit(solution)/shard_map/all_to_all | solution.py:618
  172.0 2.7 %shard_map.209 = bf16[128,512]{1,0:T(8,128)(2,1)} custom-call(s32[16]{0:T(128)S(1)} %bitcast.31, s32[16]{0:T(128)S(1)} %copy-done.28, bf16[32,64,512]{2,1,0:T(8,128)(2,1)} %all-to-all-done.3.got_ref), custom_call_target="tpu_custom_call" | custom-call | tf_op jit(solution)/shard_map/pallas_call | solution.py:531
  174.7 29.8 %all-to-all-done.4.back_ref = bf16[32,304,128]{2,1,0:T(8,128)(2,1)} async-done(((bf16[32,304,128]{2,1,0:T(8,128)(2,1)}), bf16[32,304,128]{2,1,0:T(8,128)(2,1)}, u32[]{:S(2)}, u32[]{:S(2)}) %all-to-all-start.4) | async-done | bytes 2490400 | tf_op jit(solution)/shard_map/all_to_all | solution.py:618
  204.5 4.4 %shard_map.210 = (f32[20,16,2048]{2,1,0:T(8,128)}, bf16[3,20,2048]{2,1,0:T(8,128)(2,1)}) custom-call(s32[32,128]{1,0:T(8,128)S(1)} %bitcast.23, f32[20,16,2048]{2,1,0:T(8,128)S(1)} %copy-done, bf16[3,20,2048]{2,1,0:T(8,128)(2,1)S(1)} %bitcast.19, bf16[32,304,128]{2,1,0:T(8,128)(2,1)} %all-to-all-done.4.back_ref), custom_call_target="tpu_custom_call" | custom-call | tf_op jit(solution)/shard_map/pallas_call | solution.py:598
  (113 shorter events, 30.9 us)
Async XLA Ops:
  7.2 26.9 %copy-start = (f32[20,16,2048]{2,1,0:T(8,128)S(1)}, f32[20,16,2048]{2,1,0:T(8,128)}, u32[]{:S(2)}) copy-start(f32[20,16,2048]{2,1,0:T(8,128)} %store_ref.1) | copy-start | bytes 7864324
  7.2 83.4 %all-gather.2.cloned.1.call-start = ((), (), s32[]{:S(2)}) async-start(), calls=%async_computation.5 | async-start | bytes 6488064 | tf_op jit(solution)/shard_map/all_gather | solution.py:677
  11.0 22.9 %copy-start.23 = (s32[1,16]{1,0:T(1,128)S(1)}, s32[1,16]{1,0:T(1,128)}, u32[]{:S(2)}) copy-start(s32[1,16]{1,0:T(1,128)} %param.35) | copy-start | bytes 196
  12.3 37.3 %copy-start.26 = (s32[16]{0:T(128)}, s32[16]{0:T(128)S(1)}, u32[]{:S(2)}) copy-start(s32[16]{0:T(128)S(1)} %get-tuple-element.22.refs_2_.owner_ref) | copy-start | bytes 196
  12.3 15.5 %all-to-all-start = ((s32[32,1,128]{2,1,0:T(1,128)}), s32[32,1,128]{2,1,0:T(1,128)S(1)}, u32[]{:S(2)}, u32[]{:S(2)}) async-start(s32[32,1,128]{2,1,0:T(1,128)} %get-tuple-element.23), calls=%async_computation | async-start | bytes 32768 | tf_op jit(solution)/shard_map/all_to_all | solution.py:618
  29.6 15.0 %all-to-all-start.1 = ((bf16[32,48,128]{2,1,0:T(8,128)(2,1)}), bf16[32,48,128]{2,1,0:T(8,128)(2,1)S(1)}, u32[]{:S(2)}, u32[]{:S(2)}) async-start(bf16[32,48,128]{2,1,0:T(8,128)(2,1)} %shard_map.202), calls=%async_computation.1 | async-start | bytes 786432 | tf_op jit(solution)/shard_map/all_to_all | solution.py:618
  44.7 70.9 %all-to-all-start.2 = ((bf16[32,256,128]{2,1,0:T(8,128)(2,1)}), bf16[32,256,128]{2,1,0:T(8,128)(2,1)}, u32[]{:S(2)}, u32[]{:S(2)}) async-start(bf16[32,256,128]{2,1,0:T(8,128)(2,1)} %copy-done.1), calls=%async_computation.2 | async-start | bytes 4194304 | tf_op jit(solution)/shard_map/all_to_all | solution.py:618
  57.6 13.0 %collective-permute-start = (f32[16,640]{1,0:T(8,128)S(1)}, f32[16,640]{1,0:T(8,128)S(1)}, u32[]{:S(2)}, u32[]{:S(2)}) collective-permute-start(f32[16,640]{1,0:T(8,128)S(1)} %get-tuple-element.25), channel_id=1, source_target_pairs={{0,1},{1,2},{2,3},{3,4},{4,5},{5,6},{6,7},{7,0},{8,9},{9,10},{10,1... | collective-permute-start | bytes 122888 | tf_op jit(solution)/shard_map/ppermute | solution.py:692
  59.2 13.8 %collective-permute-start.1 = (f32[16,640]{1,0:T(8,128)S(1)}, f32[16,640]{1,0:T(8,128)S(1)}, u32[]{:S(2)}, u32[]{:S(2)}) collective-permute-start(f32[16,640]{1,0:T(8,128)S(1)} %get-tuple-element.26), channel_id=1, source_target_pairs={{0,2},{1,3},{2,4},{3,5},{4,6},{5,7},{6,0},{7,1},{8,10},{9,11},{10,... | collective-permute-start | bytes 122888 | tf_op jit(solution)/shard_map/ppermute | solution.py:692
  62.0 12.3 %collective-permute-start.2 = (f32[16,640]{1,0:T(8,128)S(1)}, f32[16,640]{1,0:T(8,128)S(1)}, u32[]{:S(2)}, u32[]{:S(2)}) collective-permute-start(f32[16,640]{1,0:T(8,128)S(1)} %get-tuple-element.27), channel_id=1, source_target_pairs={{0,3},{1,4},{2,5},{3,6},{4,7},{5,0},{6,1},{7,2},{8,11},{9,12},{10,... | collective-permute-start | bytes 122888 | tf_op jit(solution)/shard_map/ppermute | solution.py:692
  65.5 8.8 %collective-permute-start.3 = (f32[16,640]{1,0:T(8,128)S(1)}, f32[16,640]{1,0:T(8,128)S(1)}, u32[]{:S(2)}, u32[]{:S(2)}) collective-permute-start(f32[16,640]{1,0:T(8,128)S(1)} %get-tuple-element.28), channel_id=1, source_target_pairs={{0,4},{1,5},{2,6},{3,7},{4,0},{5,1},{6,2},{7,3},{8,12},{9,13},{10,... | collective-permute-start | bytes 122888 | tf_op jit(solution)/shard_map/ppermute | solution.py:692
  66.1 8.3 %collective-permute-start.4 = (f32[16,640]{1,0:T(8,128)S(1)}, f32[16,640]{1,0:T(8,128)S(1)}, u32[]{:S(2)}, u32[]{:S(2)}) collective-permute-start(f32[16,640]{1,0:T(8,128)S(1)} %get-tuple-element.29), channel_id=1, source_target_pairs={{0,5},{1,6},{2,7},{3,0},{4,1},{5,2},{6,3},{7,4},{8,13},{9,14},{10,... | collective-permute-start | bytes 122888 | tf_op jit(solution)/shard_map/ppermute | solution.py:692
  70.5 7.7 %copy-start.31 = (f32[16,640]{1,0:T(8,128)}, f32[16,640]{1,0:T(8,128)S(1)}, u32[]{:S(2)}) copy-start(f32[16,640]{1,0:T(8,128)S(1)} %collective-permute-done.refs_1_) | copy-start | bytes 122884
  70.6 7.2 %collective-permute-start.5 = (f32[16,640]{1,0:T(8,128)S(1)}, f32[16,640]{1,0:T(8,128)S(1)}, u32[]{:S(2)}, u32[]{:S(2)}) collective-permute-start(f32[16,640]{1,0:T(8,128)S(1)} %get-tuple-element.30), channel_id=1, source_target_pairs={{0,6},{1,7},{2,0},{3,1},{4,2},{5,3},{6,4},{7,5},{8,14},{9,15},{10,... | collective-permute-start | bytes 122888 | tf_op jit(solution)/shard_map/ppermute | solution.py:692
  72.9 5.3 %copy-start.32 = (f32[16,640]{1,0:T(8,128)}, f32[16,640]{1,0:T(8,128)S(1)}, u32[]{:S(2)}) copy-start(f32[16,640]{1,0:T(8,128)S(1)} %collective-permute-done.1.refs_2_) | copy-start | bytes 122884
  72.9 5.3 %collective-permute-start.6 = (f32[16,640]{1,0:T(8,128)S(1)}, f32[16,640]{1,0:T(8,128)S(1)}, u32[]{:S(2)}, u32[]{:S(2)}) collective-permute-start(f32[16,640]{1,0:T(8,128)S(1)} %get-tuple-element.31), channel_id=1, source_target_pairs={{0,7},{1,0},{2,1},{3,2},{4,3},{5,4},{6,5},{7,6},{8,15},{9,8},{10,9... | collective-permute-start | bytes 122888 | tf_op jit(solution)/shard_map/ppermute | solution.py:692
  74.3 3.9 %copy-start.33 = (f32[16,640]{1,0:T(8,128)}, f32[16,640]{1,0:T(8,128)S(1)}, u32[]{:S(2)}) copy-start(f32[16,640]{1,0:T(8,128)S(1)} %collective-permute-done.2.refs_3_) | copy-start | bytes 122884
  74.3 3.9 %copy-start.34 = (f32[16,640]{1,0:T(8,128)}, f32[16,640]{1,0:T(8,128)S(1)}, u32[]{:S(2)}) copy-start(f32[16,640]{1,0:T(8,128)S(1)} %collective-permute-done.3.refs_4_) | copy-start | bytes 122884
  74.4 3.9 %copy-start.35 = (f32[16,640]{1,0:T(8,128)}, f32[16,640]{1,0:T(8,128)S(1)}, u32[]{:S(2)}) copy-start(f32[16,640]{1,0:T(8,128)S(1)} %collective-permute-done.4.refs_5_) | copy-start | bytes 122884
  115.5 24.9 %copy-start.12 = (bf16[1536,128]{1,0:T(8,128)(2,1)S(1)}, bf16[1536,128]{1,0:T(8,128)(2,1)}, u32[]{:S(2)}) copy-start(bf16[1536,128]{1,0:T(8,128)(2,1)} %copy-done.11) | copy-start | bytes 1179652
  115.5 47.3 %all-to-all-start.3 = ((bf16[32,64,512]{2,1,0:T(8,128)(2,1)}), bf16[32,64,512]{2,1,0:T(8,128)(2,1)}, u32[]{:S(2)}, u32[]{:S(2)}) async-start(bf16[32,64,512]{2,1,0:T(8,128)(2,1)} %copy-done.6), calls=%async_computation.3 | async-start | bytes 4194304 | tf_op jit(solution)/shard_map/all_to_all | solution.py:618
  120.9 11.2 %collective-permute-start.13 = (bf16[16,768]{1,0:T(8,128)(2,1)}, bf16[16,768]{1,0:T(8,128)(2,1)S(1)}, u32[]{:S(2)}, u32[]{:S(2)}) collective-permute-start(bf16[16,768]{1,0:T(8,128)(2,1)} %copy-done.18), channel_id=1, source_target_pairs={{0,7},{1,0},{2,1},{3,2},{4,3},{5,4},{6,5},{7,6},{8,15},{9,8},{10,9... | collective-permute-start | bytes 73736 | tf_op jit(solution)/shard_map/ppermute | solution.py:692
  125.9 9.4 %collective-permute-start.12 = (bf16[16,768]{1,0:T(8,128)(2,1)}, bf16[16,768]{1,0:T(8,128)(2,1)S(1)}, u32[]{:S(2)}, u32[]{:S(2)}) collective-permute-start(bf16[16,768]{1,0:T(8,128)(2,1)} %copy-done.18), channel_id=1, source_target_pairs={{0,6},{1,7},{2,0},{3,1},{4,2},{5,3},{6,4},{7,5},{8,14},{9,15},{10,... | collective-permute-start | bytes 73736 | tf_op jit(solution)/shard_map/ppermute | solution.py:692
  127.1 9.6 %collective-permute-start.11 = (bf16[16,768]{1,0:T(8,128)(2,1)}, bf16[16,768]{1,0:T(8,128)(2,1)S(1)}, u32[]{:S(2)}, u32[]{:S(2)}) collective-permute-start(bf16[16,768]{1,0:T(8,128)(2,1)} %copy-done.18), channel_id=1, source_target_pairs={{0,5},{1,6},{2,7},{3,0},{4,1},{5,2},{6,3},{7,4},{8,13},{9,14},{10,... | collective-permute-start | bytes 73736 | tf_op jit(solution)/shard_map/ppermute | solution.py:692
  128.6 8.0 %collective-permute-start.10 = (bf16[16,768]{1,0:T(8,128)(2,1)}, bf16[16,768]{1,0:T(8,128)(2,1)S(1)}, u32[]{:S(2)}, u32[]{:S(2)}) collective-permute-start(bf16[16,768]{1,0:T(8,128)(2,1)} %copy-done.18), channel_id=1, source_target_pairs={{0,4},{1,5},{2,6},{3,7},{4,0},{5,1},{6,2},{7,3},{8,12},{9,13},{10,... | collective-permute-start | bytes 73736 | tf_op jit(solution)/shard_map/ppermute | solution.py:692
  132.0 6.3 %collective-permute-start.9 = (bf16[16,768]{1,0:T(8,128)(2,1)}, bf16[16,768]{1,0:T(8,128)(2,1)S(1)}, u32[]{:S(2)}, u32[]{:S(2)}) collective-permute-start(bf16[16,768]{1,0:T(8,128)(2,1)} %copy-done.18), channel_id=1, source_target_pairs={{0,3},{1,4},{2,5},{3,6},{4,7},{5,0},{6,1},{7,2},{8,11},{9,12},{10,... | collective-permute-start | bytes 73736 | tf_op jit(solution)/shard_map/ppermute | solution.py:692
  132.0 7.0 %collective-permute-start.8 = (bf16[16,768]{1,0:T(8,128)(2,1)}, bf16[16,768]{1,0:T(8,128)(2,1)S(1)}, u32[]{:S(2)}, u32[]{:S(2)}) collective-permute-start(bf16[16,768]{1,0:T(8,128)(2,1)} %copy-done.18), channel_id=1, source_target_pairs={{0,2},{1,3},{2,4},{3,5},{4,6},{5,7},{6,0},{7,1},{8,10},{9,11},{10,... | collective-permute-start | bytes 73736 | tf_op jit(solution)/shard_map/ppermute | solution.py:692
  135.3 5.2 %collective-permute-start.7 = (bf16[16,768]{1,0:T(8,128)(2,1)}, bf16[16,768]{1,0:T(8,128)(2,1)S(1)}, u32[]{:S(2)}, u32[]{:S(2)}) collective-permute-start(bf16[16,768]{1,0:T(8,128)(2,1)} %copy-done.18), channel_id=1, source_target_pairs={{0,1},{1,2},{2,3},{3,4},{4,5},{5,6},{6,7},{7,0},{8,9},{9,10},{10,1... | collective-permute-start | bytes 73736 | tf_op jit(solution)/shard_map/ppermute | solution.py:692
  162.9 9.1 %copy-start.25 = (s32[1,16]{1,0:T(1,128)S(1)}, s32[1,16]{1,0:T(1,128)}, u32[]{:S(2)}) copy-start(s32[1,16]{1,0:T(1,128)} %param.35) | copy-start | bytes 196
  162.9 9.1 %copy-start.28 = (s32[16]{0:T(128)S(1)}, s32[16]{0:T(128)}, u32[]{:S(2)}) copy-start(s32[16]{0:T(128)} %copy-done.26) | copy-start | bytes 196
  162.9 41.6 %all-to-all-start.4 = ((bf16[32,304,128]{2,1,0:T(8,128)(2,1)}), bf16[32,304,128]{2,1,0:T(8,128)(2,1)}, u32[]{:S(2)}, u32[]{:S(2)}) async-start(bf16[32,304,128]{2,1,0:T(8,128)(2,1)} %copy-done.3), calls=%async_computation.4 | async-start | bytes 4980736 | tf_op jit(solution)/shard_map/all_to_all | solution.py:618
  172.0 32.6 %copy-start.9 = (bf16[20,3,2048]{2,0,1:T(8,128)(2,1)S(1)}, bf16[20,3,2048]{2,0,1:T(8,128)(2,1)}, u32[]{:S(2)}) copy-start(bf16[20,3,2048]{2,0,1:T(8,128)(2,1)} %param.30) | copy-start | bytes 737284
  (26 other events, 25.7 us)
Sparse Core Ops, SparseCore 0:
  11.1 79.4 all-gather.1

commit v2 on v0

v2 whole, which is shorter than its diff:
```python
import functools
import math

import jax
import jax.numpy as jnp
from jax import lax
from jax.experimental import pallas as pl
from jax.experimental.pallas import tpu as pltpu
from jax.sharding import PartitionSpec as P

HEAD_DIM = 128
KVB = 128
LANES = 128
BF = jnp.bfloat16
F32 = jnp.float32
I32 = jnp.int32
VMEM = pltpu.VMEM
SMEM = pltpu.SMEM
MIB = 1 << 20


def params(mib=58):
    return pltpu.CompilerParams(vmem_limit_bytes=mib * MIB)


def in_vmem(count):
    return [pl.BlockSpec(memory_space=VMEM) for _ in range(count)]


def in_smem(count):
    return [pl.BlockSpec(memory_space=SMEM) for _ in range(count)]


def in_hbm(count):
    return [pl.BlockSpec(memory_space=pltpu.HBM) for _ in range(count)]


def pin(*arrays):
    return [pltpu.with_memory_space_constraint(a, pltpu.HBM) for a in arrays]


def whole(*arrays):
    return [
        pl.BlockSpec(a.shape, lambda i, n=len(a.shape): (0,) * n, pipeline_mode=pl.Buffered(1))
        for a in arrays
    ]


def ask_kernel(entry_ref, block_ref, length_ref, rank_ref, out_ref, plan_ref, *, slots):
    shape = out_ref.shape
    count = entry_ref.shape[0]
    owner_of = lax.broadcasted_iota(I32, shape, 0)
    table = jnp.full(shape, -1, I32)
    for r in range(count):
        owner = lax.div(entry_ref[r], slots)
        plan_ref[r] = owner
        plan_ref[count + r] = length_ref[0, r]
        plan_ref[2 * count + r] = block_ref[r]
        table = jnp.where(owner_of == owner, entry_ref[r] - owner * slots, table)
    plan_ref[3 * count] = rank_ref[0]
    out_ref[...] = table


def ask(hit_entry, hit_blocks, seg_lengths, rank, slots, owner_count):
    return pl.pallas_call(
        functools.partial(ask_kernel, slots=slots),
        in_specs=in_smem(4),
        out_specs=in_vmem(1) + in_smem(1),
        out_shape=[
            jax.ShapeDtypeStruct((owner_count, 1, LANES), I32),
            jax.ShapeDtypeStruct((3 * hit_entry.shape[0] + 1,), I32),
        ],
        compiler_params=params(),
    )(hit_entry, hit_blocks, seg_lengths, rank)


def tiles_kernel(state_ref, out_ref, hold):
    entries, states, channels = state_ref.shape
    groups = channels // LANES
    for e in range(entries):
        for low in range(0, states, 8):
            for j in range(groups):
                hold[pl.ds(low * groups + j, 8, stride=groups), :] = state_ref[
                    e, low : low + 8, j * LANES : (j + 1) * LANES
                ]
        out_ref[e] = hold[...].astype(BF)


def state_tiles(store_state):
    slots, states, channels = store_state.shape
    rows = states * channels // LANES
    step = 4
    return pl.pallas_call(
        tiles_kernel,
        grid=(slots // step,),
        in_specs=[pl.BlockSpec((step, states, channels), lambda i: (i, 0, 0))],
        out_specs=pl.BlockSpec((step, rows, LANES), lambda i: (i, 0, 0)),
        out_shape=jax.ShapeDtypeStruct((slots, rows, LANES), BF),
        scratch_shapes=[VMEM((rows, LANES), F32)],
        compiler_params=params(16),
    )(*pin(store_state))


def pick_kernel(count, always, asked_ref, *refs):
    sources, (out_ref, stage, sems) = refs[:count], refs[count:]
    blocks = out_ref.shape[0]
    lows = [sum(s.shape[1] for s in sources[:n]) for n in range(count + 1)]

    def load(i, n):
        return pltpu.make_async_copy(
            sources[n].at[jnp.maximum(asked_ref[i, 0], 0)],
            stage.at[i, pl.ds(lows[n], sources[n].shape[1])],
            sems.at[0, i, n],
        )

    def store(i, n):
        part = pl.ds(lows[n], sources[n].shape[1])
        return pltpu.make_async_copy(stage.at[i, part], out_ref.at[i, part], sems.at[1, i, n])

    def each(act):
        for i in range(blocks):
            for n in range(always):
                act(i, n)

            @pl.when(asked_ref[i, 0] >= 0)
            def _():
                for n in range(always, count):
                    act(i, n)

    def turn(i, n):
        load(i, n).wait()
        store(i, n).start()

    each(lambda i, n: load(i, n).start())
    each(turn)
    each(lambda i, n: store(i, n).wait())


def pick(asked, always, *sources):
    blocks = asked.shape[0]
    rows = sum(s.shape[1] for s in sources)
    return pl.pallas_call(
        functools.partial(pick_kernel, len(sources), always),
        in_specs=in_smem(1) + in_hbm(len(sources)),
        out_specs=in_hbm(1)[0],
        out_shape=pltpu.HBM((blocks, rows, LANES), BF),
        scratch_shapes=[
            VMEM((blocks, rows, LANES), BF),
            pltpu.SemaphoreType.DMA((2, blocks, len(sources))),
        ],
        compiler_params=params(32),
    )(asked, *sources)


def conv_kernel(plan_ref, x_ref, got_ref, choose_ref, weight_ref, in_ref, bc_ref, *refs):
    parts, (mixed_ref, tail_ref), (source, wide, total, tails) = refs[:8], refs[8:10], refs[10:]
    tokens, chunk = x_ref.shape
    step, last = pl.program_id(0), pl.num_programs(0) - 1
    groups = got_ref.shape[1] // 3
    olds = got_ref.shape[0] * 3
    rank_dim = in_ref.shape[1]

    @pl.when(step == 0)
    def _():
        wide[...] = got_ref[...].reshape(olds * groups, LANES).astype(F32)
        source[tokens + olds :, :] = jnp.zeros((source.shape[0] - tokens - olds, chunk), BF)
        total[...] = jnp.zeros(total.shape, F32)

    source[0:tokens, :] = x_ref[...]
    low = step * (chunk // LANES)
    for j in range(chunk // LANES):
        source[tokens : tokens + olds, j * LANES : (j + 1) * LANES] = wide[
            pl.ds(low + j, olds, stride=groups), :
        ].astype(BF)
    taken = jnp.dot(choose_ref[...], source[...], preferred_element_type=F32)
    running = weight_ref[3:4, :] * x_ref[...].astype(F32)
    for lag in range(1, 4):
        running = (
            running + weight_ref[3 - lag : 4 - lag, :] * taken[(lag - 1) * tokens : lag * tokens]
        )
    mixed = (running / (1.0 + jnp.exp(-running))).astype(BF)
    mixed_ref[...] = mixed
    for j in range(chunk // LANES):
        tails[pl.ds(low + j, olds, stride=groups), :] = taken[
            3 * tokens :, j * LANES : (j + 1) * LANES
        ]
    maps = lax.dot_general(
        mixed, bc_ref[...], (((1,), (1,)), ((), ())), preferred_element_type=F32
    )
    total[:, 0:rank_dim] += jnp.dot(mixed, in_ref[...], preferred_element_type=F32)
    total[:, rank_dim : rank_dim + maps.shape[1]] += maps

    @pl.when(step == last)
    def _():
        tail_ref[...] = tails[...].astype(BF)
        share = tokens // 8
        for turn, part in enumerate(parts):
            place = lax.rem(plan_ref[plan_ref.shape[0] - 1] + turn, 8) * share
            part[...] = total[pl.ds(pl.multiple_of(place, share), share), :]


def conv_project(plan, x_rows, got, choose, conv_weight, dt_in_weight, bc_weight):
    tokens, channels = x_rows.shape
    rank_dim = dt_in_weight.shape[1]
    width = rank_dim + LANES
    conv_rows = 3 * channels // LANES
    tail_rows = got.shape[0] * conv_rows
    chunk = min(512, channels)
    once = pl.Buffered(1)
    return pl.pallas_call(
        conv_kernel,
        grid=(channels // chunk,),
        in_specs=in_smem(1)
        + [
            pl.BlockSpec((tokens, chunk), lambda i: (0, i)),
            pl.BlockSpec((got.shape[0], conv_rows, LANES), lambda i: (0, 0, 0), pipeline_mode=once),
            pl.BlockSpec(choose.shape, lambda i: (0, 0), pipeline_mode=once),
            pl.BlockSpec((4, chunk), lambda i: (0, i)),
            pl.BlockSpec((chunk, rank_dim), lambda i: (i, 0)),
            pl.BlockSpec((bc_weight.shape[0], chunk), lambda i: (0, i)),
        ],
        out_specs=[pl.BlockSpec((tokens // 8, width), lambda i: (0, 0), pipeline_mode=once)] * 8
        + [
            pl.BlockSpec((tokens, chunk), lambda i: (0, i)),
            pl.BlockSpec((tail_rows, LANES), lambda i: (0, 0), pipeline_mode=once),
        ],
        out_shape=[jax.ShapeDtypeStruct((tokens // 8, width), F32)] * 8
        + [
            jax.ShapeDtypeStruct((tokens, channels), BF),
            jax.ShapeDtypeStruct((tail_rows, LANES), BF),
        ],
        scratch_shapes=[
            VMEM((choose.shape[1], chunk), BF),
            VMEM((tail_rows, LANES), F32),
            VMEM((tokens, width), F32),
            VMEM((tail_rows, LANES), F32),
        ],
        compiler_params=params(),
    )(plan, *pin(x_rows, got, choose, conv_weight, dt_in_weight, bc_weight))


def sum_kernel(*refs):
    out_ref = refs[-1]
    total = refs[0][...]
    for part in refs[1:-1]:
        total = total + part[...]
    width = total.shape[1]
    rank_dim = width - LANES
    out_ref[:, 0:rank_dim] = total[:, 0:rank_dim].astype(BF)
    maps = total[:, rank_dim:]
    high = maps.astype(BF)
    out_ref[:, rank_dim:width] = high
    out_ref[:, width:] = (maps - high.astype(F32)).astype(BF)


def sum_parts(parts):
    rows, width = parts[0].shape
    return pl.pallas_call(
        sum_kernel,
        in_specs=in_vmem(len(parts)),
        out_specs=in_vmem(1)[0],
        out_shape=jax.ShapeDtypeStruct((rows, width + LANES), BF),
        compiler_params=params(8),
    )(*parts)


def scan_kernel(states, count, plan_ref, *refs):
    pieces = refs[0:8]
    brought, (start_ref, tail_hbm, out_ref, back_ref) = refs[8:13], refs[13:17]
    mixed_ref, weight_ref, bias_ref, decay_ref, skip_ref, tail_ref = refs[17:23]
    low_dt, maps, map_smem, rates, drives, sums, decays, begun, ready, sem, sems, own = refs[23:]
    fetches = [
        pltpu.make_async_copy(source, target, own.at[n])
        for n, (source, target) in enumerate(zip((*brought, tail_hbm), refs[17:23]))
    ]
    for n in (1, 2, 0, 3, 4, 5):
        fetches[n].start()
    tokens, channels = mixed_ref.shape
    groups = channels // LANES
    share = tokens // 8
    rank_dim = weight_ref.shape[0]
    rank = plan_ref[3 * count]
    conv_rows = 3 * groups
    state_rows = states * groups

    def receive(r):
        return pltpu.make_async_copy(
            start_ref.at[plan_ref[r], pl.ds(conv_rows, state_rows)], begun.at[r], sems.at[r, 0]
        )

    def send_tail(r):
        owner = plan_ref[r]
        return pltpu.make_async_copy(
            tail_ref.at[owner], back_ref.at[owner, pl.ds(0, conv_rows)], sems.at[r, 1]
        )

    def send_state(r):
        return pltpu.make_async_copy(
            ready.at[r], back_ref.at[plan_ref[r], pl.ds(conv_rows, state_rows)], sems.at[r, 2]
        )

    for r in range(count):
        receive(r).start()
    for step, piece in enumerate(pieces):
        place = pl.multiple_of(lax.rem(rank + 8 - step, 8) * share, share)
        low_dt[pl.ds(place, share), :] = piece[:, 0:rank_dim]
        maps[pl.ds(place, share), :] = piece[:, rank_dim : rank_dim + LANES].astype(F32) + piece[
            :, rank_dim + LANES :
        ].astype(F32)
    copy = pltpu.make_async_copy(maps, map_smem, sem)
    copy.start()
    fetches[3].wait()
    for low in range(0, states, 8):
        for j in range(groups):
            decays[pl.ds(low * groups + j, 8, stride=groups), :] = decay_ref[
                low : low + 8, j * LANES : (j + 1) * LANES
            ] * (-math.log2(math.e))
    for n in (0, 1, 2):
        fetches[n].wait()
    chunk = min(512, channels)
    for low in range(0, channels, chunk):
        cut = slice(low, low + chunk)
        raw = (
            jnp.dot(low_dt[...], weight_ref[:, cut], preferred_element_type=F32) + bias_ref[:, cut]
        )
        rate = jnp.maximum(raw, 0.0) + jnp.log1p(jnp.exp(-jnp.abs(raw)))
        drive = rate * mixed_ref[:, cut].astype(F32)
        for j in range(chunk // LANES):
            rows = pl.ds(low // LANES + j, tokens, stride=groups)
            rates[rows, :] = rate[:, j * LANES : (j + 1) * LANES]
            drives[rows, :] = drive[:, j * LANES : (j + 1) * LANES]
    fetches[5].wait()
    for r in range(count):
        send_tail(r).start()
    copy.wait()

    def segment(r, begin):
        finish = begin + plan_ref[count + r]
        receive(r).wait()
        held = tuple(
            begun[r, n * groups : (n + 1) * groups, :].astype(F32) for n in range(states)
        )

        def token(t, held):
            place = pl.ds(pl.multiple_of(t * groups, groups), groups)
            rate, drive = rates[place, :], drives[place, :]
            total, later = None, []
            for n in range(states):
                decay = jnp.exp2(rate * decays[n * groups : (n + 1) * groups, :])
                value = decay * held[n] + drive * map_smem[t, n]
                term = value * map_smem[t, states + n]
                total = term if total is None else total + term
                later.append(value)
            sums[place, :] = total
            return tuple(later)

        held = lax.fori_loop(begin, finish, token, held)
        for n in range(states):
            ready[r, n * groups : (n + 1) * groups, :] = held[n].astype(BF)
        send_state(r).start()
        return finish

    lax.fori_loop(0, count, segment, jnp.int32(0))
    fetches[4].wait()
    for j in range(groups):
        cut = slice(j * LANES, (j + 1) * LANES)
        out_ref[:, cut] = (
            sums[pl.ds(j, tokens, stride=groups), :]
            + skip_ref[:, cut] * mixed_ref[:, cut].astype(F32)
        ).astype(BF)
    for r in range(count):
        send_tail(r).wait()
        send_state(r).wait()


def scan(plan, pieces, mixed, dt_weight, dt_bias, decay_rates, skip_gain, got, tails):
    tokens, channels = mixed.shape
    states = decay_rates.shape[0]
    groups = channels // LANES
    count = (plan.shape[0] - 1) // 3
    brought = (mixed, dt_weight, dt_bias[None, :], decay_rates, skip_gain[None, :])
    return pl.pallas_call(
        functools.partial(scan_kernel, states, count),
        in_specs=in_smem(1) + in_vmem(8) + in_hbm(7),
        out_specs=in_vmem(1) + in_hbm(1),
        out_shape=[
            jax.ShapeDtypeStruct((tokens, channels), BF),
            pltpu.HBM(got.shape, BF),
        ],
        scratch_shapes=[VMEM(a.shape, a.dtype) for a in (*brought, tails)]
        + [
            VMEM((tokens, dt_weight.shape[0]), BF),
            VMEM((tokens, LANES), F32),
            SMEM((tokens, LANES), F32),
            VMEM((tokens * groups, LANES), F32),
            VMEM((tokens * groups, LANES), F32),
            VMEM((tokens * groups, LANES), F32),
            VMEM((states * groups, LANES), F32),
            VMEM((count, states * groups, LANES), BF),
            VMEM((count, states * groups, LANES), BF),
            pltpu.SemaphoreType.DMA,
            pltpu.SemaphoreType.DMA((count, 3)),
            pltpu.SemaphoreType.DMA((6,)),
        ],
        compiler_params=params(32),
    )(plan, *pieces, *pin(*brought, got, tails))


def attend_kernel(count, plan_ref, q_ref, k_ref, v_ref, got_ref, out_ref, rows_q, rows_o, prefix_ref, sems):
    tokens = q_ref.shape[0]
    heads = q_ref.shape[1] // HEAD_DIM
    prefix = prefix_ref.shape[1] // 2

    def receive(r):
        return pltpu.make_async_copy(got_ref.at[plan_ref[r]], prefix_ref.at[r], sems.at[r])

    for r in range(count):
        receive(r).start()
    for h in range(heads):
        rows_q[h * tokens : (h + 1) * tokens, :] = q_ref[:, h * HEAD_DIM : (h + 1) * HEAD_DIM]
    contract = (((1,), (1,)), ((), ()))
    scale = HEAD_DIM**-0.5
    many = heads * tokens
    new_scores = lax.dot_general(
        rows_q[...], k_ref[...], contract, preferred_element_type=F32
    ) * scale
    query_of = lax.rem(lax.broadcasted_iota(I32, (many, tokens), 0), tokens)
    key_of = lax.broadcasted_iota(I32, (many, tokens), 1)
    new_scores = jnp.where(key_of <= query_of, new_scores, -1e30)
    token_of = lax.rem(lax.broadcasted_iota(I32, (many, HEAD_DIM), 0), tokens)
    place_of = lax.broadcasted_iota(I32, (many, prefix), 1)
    rows_o[...] = jnp.zeros((many, HEAD_DIM), F32)

    def request(r, begin):
        finish = begin + plan_ref[count + r]
        live = plan_ref[2 * count + r] * KVB
        receive(r).wait()
        old = lax.dot_general(
            rows_q[...], prefix_ref[r, 0:prefix, :], contract, preferred_element_type=F32
        ) * scale
        old = jnp.where(place_of < live, old, -1e30)
        new = jnp.where(key_of >= begin, new_scores, -1e30)
        highest = jnp.maximum(
            jnp.max(old, axis=1, keepdims=True), jnp.max(new, axis=1, keepdims=True)
        )
        old, new = jnp.exp(old - highest), jnp.exp(new - highest)
        total = jnp.sum(old, axis=1, keepdims=True) + jnp.sum(new, axis=1, keepdims=True)
        inverse = 1.0 / total
        result = jnp.dot(
            (old * inverse).astype(BF), prefix_ref[r, prefix:, :], preferred_element_type=F32
        ) + jnp.dot((new * inverse).astype(BF), v_ref[...], preferred_element_type=F32)
        mine = (token_of >= begin) & (token_of < finish)
        rows_o[...] = jnp.where(mine, result, rows_o[...])
        return finish

    lax.fori_loop(0, count, request, jnp.int32(0))
    for h in range(heads):
        out_ref[:, h * HEAD_DIM : (h + 1) * HEAD_DIM] = rows_o[
            h * tokens : (h + 1) * tokens, :
        ].astype(BF)


def attend(plan, queries, new_keys, new_values, got):
    tokens, width = queries.shape
    many = tokens * width // HEAD_DIM
    count = (plan.shape[0] - 1) // 3
    return pl.pallas_call(
        functools.partial(attend_kernel, count),
        grid=(1,),
        in_specs=in_smem(1) + whole(queries, new_keys, new_values) + in_hbm(1),
        out_specs=pl.BlockSpec((tokens, width), lambda i: (0, 0)),
        out_shape=jax.ShapeDtypeStruct((tokens, width), BF),
        scratch_shapes=[
            VMEM((many, HEAD_DIM), BF),
            VMEM((many, HEAD_DIM), F32),
            VMEM((count,) + got.shape[1:], BF),
            pltpu.SemaphoreType.DMA((count,)),
        ],
        compiler_params=params(),
    )(plan, *pin(queries, new_keys, new_values, got))


def write_kernel(
    asked_ref, conv_ref, store_ref, back_ref, conv_out, out_ref, source, hold, came, stage, tails, sems
):
    slots, states, channels = out_ref.shape
    groups = channels // LANES
    rows = states * groups
    conv_rows = 3 * groups
    for s in range(slots):
        source[s] = -1
    for row in range(asked_ref.shape[0]):
        slot = asked_ref[row, 0]

        @pl.when(slot >= 0)
        def _():
            source[slot] = row

    def kept(s):
        return pltpu.make_async_copy(store_ref.at[s], stage.at[s], sems.at[slots + s])

    def changed(s):
        return pltpu.make_async_copy(stage.at[s], out_ref.at[s], sems.at[s])

    def arrival(s):
        return pltpu.make_async_copy(
            back_ref.at[jnp.maximum(source[s], 0)], came.at[s], sems.at[slots + s]
        )

    for s in range(slots):

        @pl.when(source[s] < 0)
        def _():
            kept(s).start()
            tails[s * conv_rows : (s + 1) * conv_rows, :] = jnp.zeros((conv_rows, LANES), F32)

        @pl.when(source[s] >= 0)
        def _():
            arrival(s).start()

    landed = jnp.zeros((slots, LANES), I32)
    slot_of = lax.broadcasted_iota(I32, (slots, LANES), 0)
    for s in range(slots):
        row = source[s]
        landed = jnp.where(slot_of == s, row + 1, landed)

        @pl.when(row >= 0)
        def _():
            arrival(s).wait()
            hold[s % 2] = came[s, conv_rows:, :].astype(F32)
            for low in range(0, states, 8):
                for j in range(groups):
                    stage[s, low : low + 8, j * LANES : (j + 1) * LANES] = hold[
                        s % 2, pl.ds(low * groups + j, 8, stride=groups), :
                    ]
            changed(s).start()
            tails[s * conv_rows : (s + 1) * conv_rows, :] = came[s, 0:conv_rows, :].astype(F32)

    for i in range(3):
        for j in range(groups):
            cut = slice(j * LANES, (j + 1) * LANES)
            fresh = tails[pl.ds(i * groups + j, slots, stride=3 * groups), :]
            conv_out[i, :, cut] = jnp.where(
                landed > 0, fresh, conv_ref[i, :, cut].astype(F32)
            ).astype(BF)
    for s in range(slots):

        @pl.when(source[s] < 0)
        def _():
            kept(s).wait()
            changed(s).start()

    for s in range(slots):
        changed(s).wait()


def write_store(asked, store_state, conv_rows, back):
    slots, states, channels = store_state.shape
    groups = channels // LANES
    return pl.pallas_call(
        write_kernel,
        grid=(1,),
        in_specs=in_smem(1) + whole(conv_rows) + in_hbm(2),
        out_specs=whole(conv_rows) + in_hbm(1),
        out_shape=[
            jax.ShapeDtypeStruct(conv_rows.shape, BF),
            jax.ShapeDtypeStruct((slots, states, channels), F32),
        ],
        scratch_shapes=[
            SMEM((slots,), I32),
            VMEM((2, states * groups, LANES), F32),
            VMEM((slots,) + back.shape[1:], BF),
            VMEM((slots, states, channels), F32),
            VMEM((slots * 3 * groups, LANES), F32),
            pltpu.SemaphoreType.DMA((2 * slots,)),
        ],
        compiler_params=params(),
    )(asked, *pin(conv_rows, store_state, back))


def exchange(blocks, axis):
    return lax.all_to_all(blocks, axis, split_axis=0, concat_axis=0, tiled=True)


def choose_matrix(lengths, owners, tokens, owner_count, width):
    ends = jnp.cumsum(lengths, dtype=I32)
    starts = ends - lengths
    places = jnp.arange(tokens, dtype=I32)
    member = (places[:, None] >= starts[None, :]) & (places[:, None] < ends[None, :])
    offset = places - jnp.sum(jnp.where(member, starts[None, :], 0), axis=1, dtype=I32)
    owner = jnp.sum(jnp.where(member, owners[None, :], 0), axis=1, dtype=I32)
    lags = jnp.arange(1, 4, dtype=I32)[:, None]
    lagged = jnp.where(
        offset[None, :] >= lags,
        places[None, :] - lags,
        tokens + owner[None, :] * 3 + 3 + offset[None, :] - lags,
    )
    owner_ids = jnp.arange(owner_count, dtype=I32)
    served = owner_ids[:, None] == owners[None, :]
    ends_of = jnp.sum(jnp.where(served, ends[None, :], 0), axis=1, dtype=I32)[:, None]
    length_of = jnp.sum(jnp.where(served, lengths[None, :], 0), axis=1, dtype=I32)[:, None]
    rows = jnp.arange(3, dtype=I32)[None, :]
    tails = jnp.where(
        length_of + rows >= 3, ends_of - 3 + rows, tokens + owner_ids[:, None] * 3 + length_of + rows
    )
    tails = jnp.where(length_of > 0, tails, width)
    column = jnp.concatenate([lagged.reshape(-1), tails.reshape(-1)])
    return (column[:, None] == jnp.arange(width, dtype=I32)[None, :]).astype(BF)


def shards(
    x_in,
    conv_weight,
    dt_in_weight,
    bc_weight,
    dt_weight,
    dt_bias,
    decay_rates,
    skip_gain,
    queries,
    new_keys,
    new_values,
    store_state,
    store_conv,
    store_keys,
    store_values,
    hit_entry,
    hit_blocks,
    seg_lengths,
):
    owner_count = lax.axis_size("cache")
    tp_count = lax.axis_size("tp")
    rank = lax.axis_index("tp").astype(I32)[None]
    slot_count, states, channels = store_state.shape
    groups = channels // LANES
    tokens = x_in.shape[0]
    lengths = seg_lengths[0]
    table, plan = ask(hit_entry, hit_blocks, seg_lengths, rank, slot_count, owner_count)
    asked = exchange(table, "cache")[:, 0, :]

    conv_tiles = store_conv.reshape(slot_count, 3 * groups, LANES)
    got = exchange(pick(asked, 1, conv_tiles, state_tiles(store_state)), "cache")

    width = tokens + -(-3 * owner_count // LANES) * LANES
    choose = choose_matrix(lengths, hit_entry // slot_count, tokens, owner_count, width)
    *parts, mixed, tails = conv_project(
        plan, x_in, got, choose, conv_weight, dt_in_weight, bc_weight
    )

    def turned(step, value):
        return lax.ppermute(value, "tp", [(k, (k + step) % tp_count) for k in range(tp_count)])

    parts = [parts[0]] + [turned(step, parts[step]) for step in range(1, tp_count)]
    summed = sum_parts(parts)
    pieces = [summed] + [turned(step, summed) for step in range(1, tp_count)]
    got_prefix = exchange(pick(asked, 0, store_keys, store_values), "cache")

    mixer_out, back = scan(
        plan, pieces, mixed, dt_weight, dt_bias, decay_rates, skip_gain, got,
        tails.reshape(owner_count, 3 * groups, LANES),
    )
    back = exchange(back, "cache")
    attn_out = attend(plan, queries, new_keys, new_values, got_prefix)
    conv_rows, new_state = write_store(asked, store_state, store_conv.transpose(1, 0, 2), back)
    return (mixer_out, attn_out, new_state, conv_rows.transpose(1, 0, 2))


def solution(mesh):
    placed = (
        P("cache", "tp"),
        P(None, "tp"),
        P("tp", None),
        P(None, "tp"),
        P(None, "tp"),
        P("tp"),
        P(None, "tp"),
        P("tp"),
        P("cache", "tp"),
        P("cache", "tp"),
        P("cache", "tp"),
        P("cache", None, "tp"),
        P("cache", None, "tp"),
        P("cache", None, "tp"),
        P("cache", None, "tp"),
        P("cache"),
        P("cache"),
        P("cache", None),
    )
    return jax.shard_map(
        shards,
        mesh=mesh,
        in_specs=placed,
        out_specs=(
            P("cache", "tp"),
            P("cache", "tp"),
            P("cache", None, "tp"),
            P("cache", None, "tp"),
        ),
        check_vma=False,
    )
```

time: 192 us -> 174 us (0.906)
  local copies, waits for them, and re-layouts: 27.9 us -> 3.93 us
  Pallas kernels: 46.5 us -> 54.5 us
  waiting for transfers between devices: 50.9 us -> 53.5 us
  starting transfers between devices: 61 us -> 58.6 us
  other arithmetic: 3.75 us -> 1.37 us
    unnamed x90 -> x17, local copies, waits for them, and re-layouts: 22.1 us -> 3.46 us
    pallas_call x8, Pallas kernels: 45.5 us -> 50.8 us  [the longest x1 14.1 us: attend(): pl.pallas_call(functools.partial(attend_kernel, count), grid=(1,), in_spe...]
    pallas_call x1, Pallas kernels: 0.97 us -> 3.71 us  [state_tiles(): pl.pallas_call(tiles_kernel, grid=(slots // step,), in_specs=[pl.BlockSpe...]
    gather x1 -> x0, local copies, waits for them, and re-layouts: 2.28 us -> none  [shards(): jnp.take(back_conv, jnp.maximum(source, 0), axis=0, mode='clip')]
    all_to_all x5 -> x4, starting transfers between devices: 33.2 us -> 31 us  [exchange(): return lax.all_to_all(blocks, axis, split_axis=0, concat_axis=0, tiled=True)]
    all_to_all x5 -> x4, waiting for transfers between devices: 44 us -> 46.2 us  [exchange(): return lax.all_to_all(blocks, axis, split_axis=0, concat_axis=0, tiled=True)]
  transfers between devices with their start and end apart: 19 -> 18, of which waited for: 8 -> 8; matrix products, arithmetic and copies ran while one was open for 1% -> 2% of each run, Pallas kernels for 22% -> 25%
where the time goes in v2:
time: 174 us; the launch traced here: 173 us
  starting transfers between devices  58.6 us (34%)
  Pallas kernels  54.5 us (31%)
  waiting for transfers between devices  53.5 us (31%)
  local copies, waits for them, and re-layouts  3.93 us (2%)
    all_to_all x4, waiting for transfers between devices, exchange(): return lax.all_to_all(blocks, axis, split_axis=0, concat_axis=0, tiled=True)  46.2 us
    all_to_all x4, starting transfers between devices, exchange(): return lax.all_to_all(blocks, axis, split_axis=0, concat_axis=0, tiled=True)  31 us
    ppermute x14, starting transfers between devices, turned(): lax.ppermute(value, 'tp', [(k, (k + step) % tp_count) for k in range(tp_c...  27.6 us
    pallas_call x1, Pallas kernels, attend(): pl.pallas_call(functools.partial(attend_kernel, count), grid=(1,), in_spe...  14.1 us
    pallas_call x1, Pallas kernels, scan(): pl.pallas_call(functools.partial(scan_kernel, states, count), in_specs=in...  12.9 us
    pallas_call x2, Pallas kernels, pick(): pl.pallas_call(functools.partial(pick_kernel, len(sources), always), in_s...  11.7 us
    ppermute x14, waiting for transfers between devices, turned(): lax.ppermute(value, 'tp', [(k, (k + step) % tp_count) for k in range(tp_c...  7.29 us
    pallas_call x1, Pallas kernels, conv_project(): pl.pallas_call(conv_kernel, grid=(channels // chunk,), in_specs=in_smem(1...  5.6 us
  transfers between devices with their start and end apart: 18, of which 8 were waited for; matrix products, arithmetic and copies ran while one was open for 2% of the time, Pallas kernels for 25%

profile of v2, /device:TPU:1, one launch (start us, length us, event | category | flops | bytes accessed | tf_op | source)
XLA Modules:
  0.0 172.9 jit_solution(16891986071455030979)
XLA Ops:
  0.6 1.4 shard_map.201
  2.1 8.6 %all-to-all-start = ((s32[32,1,128]{2,1,0:T(1,128)}), s32[32,1,128]{2,1,0:T(1,128)S(1)}, u32[]{:S(2)}, u32[]{:S(2)}) async-start(s32[32,1,128]{2,1,0:T(1,128)} %get-tuple-element.21), calls=%async_computation | async-start | bytes 32768 | tf_op jit(solution)/shard_map/all_to_all | solution.py:582
  10.7 1.2 copy.30
  12.2 3.7 %shard_map.202.refs_1_ = bf16[20,256,128]{2,1,0:T(8,128)(2,1)S(1)} custom-call(f32[20,16,2048]{2,1,0:T(8,128)} %store_ref.1), custom_call_target="tpu_custom_call" | custom-call | tf_op jit(solution)/shard_map/pallas_call | solution.py:93
  15.9 1.7 all-to-all-done
  17.6 5.3 %shard_map.203 = bf16[32,304,128]{2,1,0:T(8,128)(2,1)} custom-call(s32[32,128]{1,0:T(8,128)S(1)} %bitcast.17, bf16[20,48,128]{2,1,0:T(8,128)(2,1)S(1)} %reshape.95.refs_0_, bf16[20,256,128]{2,1,0:T(8,128)(2,1)S(1)} %shard_map.202.refs_1_), custom_call_target="tpu_custom_call" | custom-call | tf_op jit(solution)/shard_map/pallas_call | solution.py:142
  22.9 5.9 %all-to-all-start.1 = ((bf16[32,304,128]{2,1,0:T(8,128)(2,1)}), bf16[32,304,128]{2,1,0:T(8,128)(2,1)}, u32[]{:S(2)}, u32[]{:S(2)}) async-start(bf16[32,304,128]{2,1,0:T(8,128)(2,1)} %shard_map.203), calls=%async_computation.1 | async-start | bytes 4980736 | tf_op jit(solution)/shard_map/all_to_all | solution.py:582
  28.9 6.3 %shard_map.207 = bf16[32,512,128]{2,1,0:T(8,128)(2,1)} custom-call(s32[32,128]{1,0:T(8,128)S(1)} %bitcast.18, bf16[20,256,128]{2,1,0:T(8,128)(2,1)S(1)} %copy-done, bf16[20,256,128]{2,1,0:T(8,128)(2,1)S(1)} %copy-done.1), custom_call_target="tpu_custom_call" | custom-call | tf_op jit(solution)/shard_map/pallas_call | solution.py:142
  35.2 26.2 %all-to-all-done.1.got_ref.refs_13_ = bf16[32,304,128]{2,1,0:T(8,128)(2,1)} async-done(((bf16[32,304,128]{2,1,0:T(8,128)(2,1)}), bf16[32,304,128]{2,1,0:T(8,128)(2,1)}, u32[]{:S(2)}, u32[]{:S(2)}) %all-to-all-start.1) | async-done | bytes 2490400 | tf_op jit(solution)/shard_map/all_to_all | solution.py:582
  61.4 5.4 %all-to-all-start.2 = ((bf16[32,512,128]{2,1,0:T(8,128)(2,1)}), bf16[32,512,128]{2,1,0:T(8,128)(2,1)}, u32[]{:S(2)}, u32[]{:S(2)}) async-start(bf16[32,512,128]{2,1,0:T(8,128)(2,1)} %shard_map.207), calls=%async_computation.2 | async-start | bytes 8388608 | tf_op jit(solution)/shard_map/all_to_all | solution.py:582
  67.6 0.8 fusion.choose_ref
  68.4 5.6 %shard_map.204 = (f32[16,640]{1,0:T(8,128)}, f32[16,640]{1,0:T(8,128)}, f32[16,640]{1,0:T(8,128)}, f32[16,640]{1,0:T(8,128)}, f32[16,640]{1,0:T(8,128)}, /*index...) custom-call(s32[49]{0:T(128)} %get-tuple-element.20.plan_ref, ...), custom_call_target="tpu_custom_call" | custom-call | tf_op jit(solution)/shard_map/pallas_call | solution.py:210
  74.0 1.7 collective-permute-start
  75.8 3.0 %collective-permute-start.1 = (f32[16,640]{1,0:T(8,128)}, f32[16,640]{1,0:T(8,128)S(1)}, u32[]{:S(2)}, u32[]{:S(2)}) collective-permute-start(f32[16,640]{1,0:T(8,128)} %get-tuple-element.24), channel_id=1, source_target_pairs={{0,2},{1,3},{2,4},{3,5},{4,6},{5,7},{6,0},{7,1},{8,10},{9,11},{10,... | collective-permute-start | bytes 122888 | tf_op jit(solution)/shard_map/ppermute | solution.py:651
  78.8 3.8 %collective-permute-start.2 = (f32[16,640]{1,0:T(8,128)}, f32[16,640]{1,0:T(8,128)S(1)}, u32[]{:S(2)}, u32[]{:S(2)}) collective-permute-start(f32[16,640]{1,0:T(8,128)} %get-tuple-element.25), channel_id=1, source_target_pairs={{0,3},{1,4},{2,5},{3,6},{4,7},{5,0},{6,1},{7,2},{8,11},{9,12},{10,... | collective-permute-start | bytes 122888 | tf_op jit(solution)/shard_map/ppermute | solution.py:651
  83.0 4.5 %collective-permute-start.4 = (f32[16,640]{1,0:T(8,128)}, f32[16,640]{1,0:T(8,128)S(1)}, u32[]{:S(2)}, u32[]{:S(2)}) collective-permute-start(f32[16,640]{1,0:T(8,128)} %get-tuple-element.27), channel_id=1, source_target_pairs={{0,5},{1,6},{2,7},{3,0},{4,1},{5,2},{6,3},{7,4},{8,13},{9,14},{10,... | collective-permute-start | bytes 122888 | tf_op jit(solution)/shard_map/ppermute | solution.py:651
  87.4 2.4 %collective-permute-start.5 = (f32[16,640]{1,0:T(8,128)}, f32[16,640]{1,0:T(8,128)S(1)}, u32[]{:S(2)}, u32[]{:S(2)}) collective-permute-start(f32[16,640]{1,0:T(8,128)} %get-tuple-element.28), channel_id=1, source_target_pairs={{0,6},{1,7},{2,0},{3,1},{4,2},{5,3},{6,4},{7,5},{8,14},{9,15},{10,... | collective-permute-start | bytes 122888 | tf_op jit(solution)/shard_map/ppermute | solution.py:651
  89.8 0.7 collective-permute-start.6
  90.6 4.4 %collective-permute-done.5.refs_6_ = f32[16,640]{1,0:T(8,128)S(1)} collective-permute-done((f32[16,640]{1,0:T(8,128)}, f32[16,640]{1,0:T(8,128)S(1)}, u32[]{:S(2)}, u32[]{:S(2)}) %collective-permute-start.5) | collective-permute-done | bytes 40992 | tf_op jit(solution)/shard_map/ppermute | solution.py:651
  95.3 0.8 copy-done.3
  96.1 0.9 collective-permute-start.7
  97.0 3.3 %collective-permute-start.9 = (bf16[16,768]{1,0:T(8,128)(2,1)S(1)}, bf16[16,768]{1,0:T(8,128)(2,1)S(1)}, u32[]{:S(2)}, u32[]{:S(2)}) collective-permute-start(bf16[16,768]{1,0:T(8,128)(2,1)S(1)} %shard_map.205.refs_0_), channel_id=1, source_target_pairs={{0,3},{1,4},{2,5},{3,6},{4,7},{5,0},{6,1},{7,2},{8,11},{9,12},{10,... | collective-permute-start | bytes 73736 | tf_op jit(solution)/shard_map/ppermute | solution.py:651
  100.3 2.3 %collective-permute-start.10 = (bf16[16,768]{1,0:T(8,128)(2,1)S(1)}, bf16[16,768]{1,0:T(8,128)(2,1)S(1)}, u32[]{:S(2)}, u32[]{:S(2)}) collective-permute-start(bf16[16,768]{1,0:T(8,128)(2,1)S(1)} %shard_map.205.refs_0_), channel_id=1, source_target_pairs={{0,4},{1,5},{2,6},{3,7},{4,0},{5,1},{6,2},{7,3},{8,12},{9,13},{10,... | collective-permute-start | bytes 73736 | tf_op jit(solution)/shard_map/ppermute | solution.py:651
  102.6 2.9 %collective-permute-start.11 = (bf16[16,768]{1,0:T(8,128)(2,1)S(1)}, bf16[16,768]{1,0:T(8,128)(2,1)S(1)}, u32[]{:S(2)}, u32[]{:S(2)}) collective-permute-start(bf16[16,768]{1,0:T(8,128)(2,1)S(1)} %shard_map.205.refs_0_), channel_id=1, source_target_pairs={{0,5},{1,6},{2,7},{3,0},{4,1},{5,2},{6,3},{7,4},{8,13},{9,14},{10,... | collective-permute-start | bytes 73736 | tf_op jit(solution)/shard_map/ppermute | solution.py:651
  106.0 1.2 collective-permute-start.13
  107.5 2.0 %collective-permute-done.12.refs_6_ = bf16[16,768]{1,0:T(8,128)(2,1)S(1)} collective-permute-done((bf16[16,768]{1,0:T(8,128)(2,1)S(1)}, bf16[16,768]{1,0:T(8,128)(2,1)S(1)}, u32[]{:S(2)}, u32[]{:S(2)}) %collective-permute-start.12) | collective-permute-done | bytes 24608 | tf_op jit(solution)/shard_map/ppermute | solution.py:651
  109.8 12.9 %shard_map.206 = (bf16[128,2048]{1,0:T(8,128)(2,1)}, bf16[32,304,128]{2,1,0:T(8,128)(2,1)}) custom-call(s32[49]{0:T(128)S(1)} %copy-done.4, bf16[16,768]{1,0:T(8,128)(2,1)S(1)} %shard_map.205.refs_0_, bf16[16,768]{1,0:T(8,128)(2,1)S(1)} %collective-permute-done.7.refs_1_, bf16[16,768]{1,0:T(8,128)(2,1)S(1)} %collective-permute-done.8.refs_2_, ...), custom_call_target="tpu_custom_call" | custom-call | tf_op jit(solution)/shard_map/pallas_call | solution.py:382
  122.7 11.1 %all-to-all-start.3 = ((bf16[32,304,128]{2,1,0:T(8,128)(2,1)}), bf16[32,304,128]{2,1,0:T(8,128)(2,1)S(1)}, u32[]{:S(2)}, u32[]{:S(2)}) async-start(bf16[32,304,128]{2,1,0:T(8,128)(2,1)} %get-tuple-element.33), calls=%async_computation.3 | async-start | bytes 4980736 | tf_op jit(solution)/shard_map/all_to_all | solution.py:582
  133.8 14.1 %shard_map.208 = bf16[128,512]{1,0:T(8,128)(2,1)} custom-call(s32[49]{0:T(128)} %get-tuple-element.20.plan_ref, bf16[128,512]{1,0:T(8,128)(2,1)} %q_ref.1, bf16[128,128]{1,0:T(8,128)(2,1)} %k_ref.1, bf16[128,128]{1,0:T(8,128)(2,1)} %v_ref.1, bf16[32,512,128]{2,1,0:T(8,128)(2,1)} %all-to-all-done.2.got_ref), custom_call_target="tpu_custom_call" | custom-call | tf_op jit(solution)/shard_map/pallas_call | solution.py:467
  147.9 18.4 %all-to-all-done.3.back_ref = bf16[32,304,128]{2,1,0:T(8,128)(2,1)S(1)} async-done(((bf16[32,304,128]{2,1,0:T(8,128)(2,1)}), bf16[32,304,128]{2,1,0:T(8,128)(2,1)S(1)}, u32[]{:S(2)}, u32[]{:S(2)}) %all-to-all-start.3) | async-done | bytes 2490400 | tf_op jit(solution)/shard_map/all_to_all | solution.py:582
  166.3 1.5 copy-done.5
  167.8 5.0 %shard_map.209 = (bf16[3,20,2048]{2,1,0:T(8,128)(2,1)}, f32[20,16,2048]{2,1,0:T(8,128)}) custom-call(s32[32,128]{1,0:T(8,128)} %bitcast.19, bf16[3,20,2048]{2,1,0:T(8,128)(2,1)} %bitcast.20, f32[20,16,2048]{2,1,0:T(8,128)} %store_ref.1, bf16[32,304,128]{2,1,0:T(8,128)(2,1)} %copy-done.5), custom_call_target="tpu_custom_call" | custom-call | tf_op jit(solution)/shard_map/pallas_call | solution.py:560
  (47 shorter events, 3.0 us)
Async XLA Ops:
  2.1 15.5 %all-to-all-start = ((s32[32,1,128]{2,1,0:T(1,128)}), s32[32,1,128]{2,1,0:T(1,128)S(1)}, u32[]{:S(2)}, u32[]{:S(2)}) async-start(s32[32,1,128]{2,1,0:T(1,128)} %get-tuple-element.21), calls=%async_computation | async-start | bytes 32768 | tf_op jit(solution)/shard_map/all_to_all | solution.py:582
  17.6 11.3 %copy-start.2 = (s32[32,1,128]{2,1,0:T(1,128)}, s32[32,1,128]{2,1,0:T(1,128)S(1)}, u32[]{:S(2)}) copy-start(s32[32,1,128]{2,1,0:T(1,128)S(1)} %all-to-all-done) | copy-start | bytes 49156
  22.9 6.0 %copy-start = (bf16[20,256,128]{2,1,0:T(8,128)(2,1)S(1)}, bf16[20,256,128]{2,1,0:T(8,128)(2,1)}, u32[]{:S(2)}) copy-start(bf16[20,256,128]{2,1,0:T(8,128)(2,1)} %refs_0_.1) | copy-start | bytes 3932164
  22.9 5.9 %copy-start.1 = (bf16[20,256,128]{2,1,0:T(8,128)(2,1)S(1)}, bf16[20,256,128]{2,1,0:T(8,128)(2,1)}, u32[]{:S(2)}) copy-start(bf16[20,256,128]{2,1,0:T(8,128)(2,1)} %refs_1_.1) | copy-start | bytes 3932164
  22.9 38.5 %all-to-all-start.1 = ((bf16[32,304,128]{2,1,0:T(8,128)(2,1)}), bf16[32,304,128]{2,1,0:T(8,128)(2,1)}, u32[]{:S(2)}, u32[]{:S(2)}) async-start(bf16[32,304,128]{2,1,0:T(8,128)(2,1)} %shard_map.203), calls=%async_computation.1 | async-start | bytes 4980736 | tf_op jit(solution)/shard_map/all_to_all | solution.py:582
  35.2 31.6 %copy-start.6 = (s32[1,16]{1,0:T(1,128)S(1)}, s32[1,16]{1,0:T(1,128)}, u32[]{:S(2)}) copy-start(s32[1,16]{1,0:T(1,128)} %length_ref.1) | copy-start | bytes 196
  35.2 31.8 %copy-start.7 = (s32[16]{0:T(128)S(1)}, s32[16]{0:T(128)}, u32[]{:S(2)}) copy-start(s32[16]{0:T(128)} %entry_ref.1) | copy-start | bytes 196
  61.4 61.3 %all-to-all-start.2 = ((bf16[32,512,128]{2,1,0:T(8,128)(2,1)}), bf16[32,512,128]{2,1,0:T(8,128)(2,1)}, u32[]{:S(2)}, u32[]{:S(2)}) async-start(bf16[32,512,128]{2,1,0:T(8,128)(2,1)} %shard_map.207), calls=%async_computation.2 | async-start | bytes 8388608 | tf_op jit(solution)/shard_map/all_to_all | solution.py:582
  68.4 41.3 %copy-start.4 = (s32[49]{0:T(128)S(1)}, s32[49]{0:T(128)}, u32[]{:S(2)}) copy-start(s32[49]{0:T(128)} %get-tuple-element.20.plan_ref) | copy-start | bytes 592
  74.0 13.4 %collective-permute-start = (f32[16,640]{1,0:T(8,128)}, f32[16,640]{1,0:T(8,128)S(1)}, u32[]{:S(2)}, u32[]{:S(2)}) collective-permute-start(f32[16,640]{1,0:T(8,128)} %get-tuple-element.23), channel_id=1, source_target_pairs={{0,1},{1,2},{2,3},{3,4},{4,5},{5,6},{6,7},{7,0},{8,9},{9,10},{10,1... | collective-permute-start | bytes 122888 | tf_op jit(solution)/shard_map/ppermute | solution.py:651
  75.8 14.1 %collective-permute-start.1 = (f32[16,640]{1,0:T(8,128)}, f32[16,640]{1,0:T(8,128)S(1)}, u32[]{:S(2)}, u32[]{:S(2)}) collective-permute-start(f32[16,640]{1,0:T(8,128)} %get-tuple-element.24), channel_id=1, source_target_pairs={{0,2},{1,3},{2,4},{3,5},{4,6},{5,7},{6,0},{7,1},{8,10},{9,11},{10,... | collective-permute-start | bytes 122888 | tf_op jit(solution)/shard_map/ppermute | solution.py:651
  78.8 11.8 %collective-permute-start.2 = (f32[16,640]{1,0:T(8,128)}, f32[16,640]{1,0:T(8,128)S(1)}, u32[]{:S(2)}, u32[]{:S(2)}) collective-permute-start(f32[16,640]{1,0:T(8,128)} %get-tuple-element.25), channel_id=1, source_target_pairs={{0,3},{1,4},{2,5},{3,6},{4,7},{5,0},{6,1},{7,2},{8,11},{9,12},{10,... | collective-permute-start | bytes 122888 | tf_op jit(solution)/shard_map/ppermute | solution.py:651
  82.5 8.1 %collective-permute-start.3 = (f32[16,640]{1,0:T(8,128)}, f32[16,640]{1,0:T(8,128)S(1)}, u32[]{:S(2)}, u32[]{:S(2)}) collective-permute-start(f32[16,640]{1,0:T(8,128)} %get-tuple-element.26), channel_id=1, source_target_pairs={{0,4},{1,5},{2,6},{3,7},{4,0},{5,1},{6,2},{7,3},{8,12},{9,13},{10,... | collective-permute-start | bytes 122888 | tf_op jit(solution)/shard_map/ppermute | solution.py:651
  83.0 7.6 %collective-permute-start.4 = (f32[16,640]{1,0:T(8,128)}, f32[16,640]{1,0:T(8,128)S(1)}, u32[]{:S(2)}, u32[]{:S(2)}) collective-permute-start(f32[16,640]{1,0:T(8,128)} %get-tuple-element.27), channel_id=1, source_target_pairs={{0,5},{1,6},{2,7},{3,0},{4,1},{5,2},{6,3},{7,4},{8,13},{9,14},{10,... | collective-permute-start | bytes 122888 | tf_op jit(solution)/shard_map/ppermute | solution.py:651
  87.4 7.5 %collective-permute-start.5 = (f32[16,640]{1,0:T(8,128)}, f32[16,640]{1,0:T(8,128)S(1)}, u32[]{:S(2)}, u32[]{:S(2)}) collective-permute-start(f32[16,640]{1,0:T(8,128)} %get-tuple-element.28), channel_id=1, source_target_pairs={{0,6},{1,7},{2,0},{3,1},{4,2},{5,3},{6,4},{7,5},{8,14},{9,15},{10,... | collective-permute-start | bytes 122888 | tf_op jit(solution)/shard_map/ppermute | solution.py:651
  89.8 5.4 %collective-permute-start.6 = (f32[16,640]{1,0:T(8,128)}, f32[16,640]{1,0:T(8,128)S(1)}, u32[]{:S(2)}, u32[]{:S(2)}) collective-permute-start(f32[16,640]{1,0:T(8,128)} %get-tuple-element.29), channel_id=1, source_target_pairs={{0,7},{1,0},{2,1},{3,2},{4,3},{5,4},{6,5},{7,6},{8,15},{9,8},{10,9... | collective-permute-start | bytes 122888 | tf_op jit(solution)/shard_map/ppermute | solution.py:651
  95.3 0.8 copy-start.3
  96.1 9.4 %collective-permute-start.7 = (bf16[16,768]{1,0:T(8,128)(2,1)S(1)}, bf16[16,768]{1,0:T(8,128)(2,1)S(1)}, u32[]{:S(2)}, u32[]{:S(2)}) collective-permute-start(bf16[16,768]{1,0:T(8,128)(2,1)S(1)} %shard_map.205.refs_0_), channel_id=1, source_target_pairs={{0,1},{1,2},{2,3},{3,4},{4,5},{5,6},{6,7},{7,0},{8,9},{9,10},{10,1... | collective-permute-start | bytes 73736 | tf_op jit(solution)/shard_map/ppermute | solution.py:651
  97.0 9.0 %collective-permute-start.8 = (bf16[16,768]{1,0:T(8,128)(2,1)S(1)}, bf16[16,768]{1,0:T(8,128)(2,1)S(1)}, u32[]{:S(2)}, u32[]{:S(2)}) collective-permute-start(bf16[16,768]{1,0:T(8,128)(2,1)S(1)} %shard_map.205.refs_0_), channel_id=1, source_target_pairs={{0,2},{1,3},{2,4},{3,5},{4,6},{5,7},{6,0},{7,1},{8,10},{9,11},{10,... | collective-permute-start | bytes 73736 | tf_op jit(solution)/shard_map/ppermute | solution.py:651
  97.0 10.2 %collective-permute-start.9 = (bf16[16,768]{1,0:T(8,128)(2,1)S(1)}, bf16[16,768]{1,0:T(8,128)(2,1)S(1)}, u32[]{:S(2)}, u32[]{:S(2)}) collective-permute-start(bf16[16,768]{1,0:T(8,128)(2,1)S(1)} %shard_map.205.refs_0_), channel_id=1, source_target_pairs={{0,3},{1,4},{2,5},{3,6},{4,7},{5,0},{6,1},{7,2},{8,11},{9,12},{10,... | collective-permute-start | bytes 73736 | tf_op jit(solution)/shard_map/ppermute | solution.py:651
  100.3 6.9 %collective-permute-start.10 = (bf16[16,768]{1,0:T(8,128)(2,1)S(1)}, bf16[16,768]{1,0:T(8,128)(2,1)S(1)}, u32[]{:S(2)}, u32[]{:S(2)}) collective-permute-start(bf16[16,768]{1,0:T(8,128)(2,1)S(1)} %shard_map.205.refs_0_), channel_id=1, source_target_pairs={{0,4},{1,5},{2,6},{3,7},{4,0},{5,1},{6,2},{7,3},{8,12},{9,13},{10,... | collective-permute-start | bytes 73736 | tf_op jit(solution)/shard_map/ppermute | solution.py:651
  102.6 4.9 %collective-permute-start.11 = (bf16[16,768]{1,0:T(8,128)(2,1)S(1)}, bf16[16,768]{1,0:T(8,128)(2,1)S(1)}, u32[]{:S(2)}, u32[]{:S(2)}) collective-permute-start(bf16[16,768]{1,0:T(8,128)(2,1)S(1)} %shard_map.205.refs_0_), channel_id=1, source_target_pairs={{0,5},{1,6},{2,7},{3,0},{4,1},{5,2},{6,3},{7,4},{8,13},{9,14},{10,... | collective-permute-start | bytes 73736 | tf_op jit(solution)/shard_map/ppermute | solution.py:651
  105.5 4.0 %collective-permute-start.12 = (bf16[16,768]{1,0:T(8,128)(2,1)S(1)}, bf16[16,768]{1,0:T(8,128)(2,1)S(1)}, u32[]{:S(2)}, u32[]{:S(2)}) collective-permute-start(bf16[16,768]{1,0:T(8,128)(2,1)S(1)} %shard_map.205.refs_0_), channel_id=1, source_target_pairs={{0,6},{1,7},{2,0},{3,1},{4,2},{5,3},{6,4},{7,5},{8,14},{9,15},{10,... | collective-permute-start | bytes 73736 | tf_op jit(solution)/shard_map/ppermute | solution.py:651
  106.0 3.8 %collective-permute-start.13 = (bf16[16,768]{1,0:T(8,128)(2,1)S(1)}, bf16[16,768]{1,0:T(8,128)(2,1)S(1)}, u32[]{:S(2)}, u32[]{:S(2)}) collective-permute-start(bf16[16,768]{1,0:T(8,128)(2,1)S(1)} %shard_map.205.refs_0_), channel_id=1, source_target_pairs={{0,7},{1,0},{2,1},{3,2},{4,3},{5,4},{6,5},{7,6},{8,15},{9,8},{10,9... | collective-permute-start | bytes 73736 | tf_op jit(solution)/shard_map/ppermute | solution.py:651
  122.7 43.6 %all-to-all-start.3 = ((bf16[32,304,128]{2,1,0:T(8,128)(2,1)}), bf16[32,304,128]{2,1,0:T(8,128)(2,1)S(1)}, u32[]{:S(2)}, u32[]{:S(2)}) async-start(bf16[32,304,128]{2,1,0:T(8,128)(2,1)} %get-tuple-element.33), calls=%async_computation.3 | async-start | bytes 4980736 | tf_op jit(solution)/shard_map/all_to_all | solution.py:582
  166.3 1.5 copy-start.5

commit v3 on v2

--- a/solution.py
+++ b/solution.py
@@ -74,34 +74,50 @@
     )(hit_entry, hit_blocks, seg_lengths, rank)
 
 
-def tiles_kernel(state_ref, out_ref, hold):
+def tiles_kernel(conv_ref, state_ref, out_ref, hold, tails):
     entries, states, channels = state_ref.shape
+    slots = conv_ref.shape[1]
     groups = channels // LANES
+    conv_rows = 3 * groups
+    first = pl.program_id(0) * entries
+
+    @pl.when(first == 0)
+    def _():
+        for i in range(3):
+            for j in range(groups):
+                tails[pl.ds(i * groups + j, slots, stride=conv_rows), :] = conv_ref[
+                    i, :, j * LANES : (j + 1) * LANES
+                ].astype(F32)
+
     for e in range(entries):
         for low in range(0, states, 8):
             for j in range(groups):
                 hold[pl.ds(low * groups + j, 8, stride=groups), :] = state_ref[
                     e, low : low + 8, j * LANES : (j + 1) * LANES
                 ]
-        out_ref[e] = hold[...].astype(BF)
-
-
-def state_tiles(store_state):
+        place = pl.multiple_of((first + e) * conv_rows, conv_rows)
+        out_ref[e, 0:conv_rows, :] = tails[pl.ds(place, conv_rows), :].astype(BF)
+        out_ref[e, conv_rows:, :] = hold[...].astype(BF)
+
+
+def entry_tiles(conv_rows, store_state):
     slots, states, channels = store_state.shape
     rows = states * channels // LANES
+    tail_rows = 3 * channels // LANES
     step = 4
     return pl.pallas_call(
         tiles_kernel,
         grid=(slots // step,),
-        in_specs=[pl.BlockSpec((step, states, channels), lambda i: (i, 0, 0))],
-        out_specs=pl.BlockSpec((step, rows, LANES), lambda i: (i, 0, 0)),
-        out_shape=jax.ShapeDtypeStruct((slots, rows, LANES), BF),
-        scratch_shapes=[VMEM((rows, LANES), F32)],
+        in_specs=whole(conv_rows)
+        + [pl.BlockSpec((step, states, channels), lambda i: (i, 0, 0))],
+        out_specs=pl.BlockSpec((step, tail_rows + rows, LANES), lambda i: (i, 0, 0)),
+        out_shape=jax.ShapeDtypeStruct((slots, tail_rows + rows, LANES), BF),
+        scratch_shapes=[VMEM((rows, LANES), F32), VMEM((slots * tail_rows, LANES), F32)],
         compiler_params=params(16),
-    )(*pin(store_state))
-
-
-def pick_kernel(count, always, asked_ref, *refs):
+    )(*pin(conv_rows, store_state))
+
+
+def pick_kernel(count, asked_ref, *refs):
     sources, (out_ref, stage, sems) = refs[:count], refs[count:]
     blocks = out_ref.shape[0]
     lows = [sum(s.shape[1] for s in sources[:n]) for n in range(count + 1)]
@@ -119,12 +135,10 @@
 
     def each(act):
         for i in range(blocks):
-            for n in range(always):
-                act(i, n)
 
             @pl.when(asked_ref[i, 0] >= 0)
             def _():
-                for n in range(always, count):
+                for n in range(count):
                     act(i, n)
 
     def turn(i, n):
@@ -136,11 +150,11 @@
     each(lambda i, n: store(i, n).wait())
 
 
-def pick(asked, always, *sources):
+def pick(asked, *sources):
     blocks = asked.shape[0]
     rows = sum(s.shape[1] for s in sources)
     return pl.pallas_call(
-        functools.partial(pick_kernel, len(sources), always),
+        functools.partial(pick_kernel, len(sources)),
         in_specs=in_smem(1) + in_hbm(len(sources)),
         out_specs=in_hbm(1)[0],
         out_shape=pltpu.HBM((blocks, rows, LANES), BF),
@@ -150,6 +164,38 @@
         ],
         compiler_params=params(32),
     )(asked, *sources)
+
+
+def pick_tiles_kernel(part, asked_ref, tiles_ref, out_ref, sems):
+    def act(name):
+        for i in range(out_ref.shape[0]):
+            slot = asked_ref[i, 0]
+
+            @pl.when(slot >= 0)
+            def _():
+                getattr(pltpu.make_async_copy(tiles_ref.at[slot], out_ref.at[i], sems.at[i]), name)()
+
+            @pl.when(slot < 0)
+            def _():
+                few = pl.ds(0, part)
+                getattr(
+                    pltpu.make_async_copy(tiles_ref.at[0, few], out_ref.at[i, few], sems.at[i]), name
+                )()
+
+    act("start")
+    act("wait")
+
+
+def pick_tiles(asked, tiles, part):
+    blocks = asked.shape[0]
+    return pl.pallas_call(
+        functools.partial(pick_tiles_kernel, part),
+        in_specs=in_smem(1) + in_vmem(1),
+        out_specs=in_hbm(1)[0],
+        out_shape=pltpu.HBM((blocks,) + tiles.shape[1:], BF),
+        scratch_shapes=[pltpu.SemaphoreType.DMA((blocks,))],
+        compiler_params=params(4),
+    )(asked, tiles)
 
 
 def conv_kernel(plan_ref, x_ref, got_ref, choose_ref, weight_ref, in_ref, bc_ref, *refs):
@@ -193,10 +239,13 @@
     @pl.when(step == last)
     def _():
         tail_ref[...] = tails[...].astype(BF)
-        share = tokens // 8
+        share, width = tokens // 8, total.shape[1]
         for turn, part in enumerate(parts):
             place = lax.rem(plan_ref[plan_ref.shape[0] - 1] + turn, 8) * share
-            part[...] = total[pl.ds(pl.multiple_of(place, share), share), :]
+            rows = total[pl.ds(pl.multiple_of(place, share), share), :]
+            high = rows.astype(BF)
+            part[:, 0:width] = high
+            part[:, width:] = (rows[:, rank_dim:] - high[:, rank_dim:].astype(F32)).astype(BF)
 
 
 def conv_project(plan, x_rows, got, choose, conv_weight, dt_in_weight, bc_weight):
@@ -219,12 +268,12 @@
             pl.BlockSpec((chunk, rank_dim), lambda i: (i, 0)),
             pl.BlockSpec((bc_weight.shape[0], chunk), lambda i: (0, i)),
         ],
-        out_specs=[pl.BlockSpec((tokens // 8, width), lambda i: (0, 0), pipeline_mode=once)] * 8
+        out_specs=in_vmem(8)
         + [
             pl.BlockSpec((tokens, chunk), lambda i: (0, i)),
             pl.BlockSpec((tail_rows, LANES), lambda i: (0, 0), pipeline_mode=once),
         ],
-        out_shape=[jax.ShapeDtypeStruct((tokens // 8, width), F32)] * 8
+        out_shape=[jax.ShapeDtypeStruct((tokens // 8, width + LANES), BF)] * 8
         + [
             jax.ShapeDtypeStruct((tokens, channels), BF),
             jax.ShapeDtypeStruct((tail_rows, LANES), BF),
@@ -235,22 +284,22 @@
             VMEM((tokens, width), F32),
             VMEM((tail_rows, LANES), F32),
         ],
-        compiler_params=params(),
+        compiler_params=params(24),
     )(plan, *pin(x_rows, got, choose, conv_weight, dt_in_weight, bc_weight))
 
 
 def sum_kernel(*refs):
     out_ref = refs[-1]
-    total = refs[0][...]
-    for part in refs[1:-1]:
-        total = total + part[...]
-    width = total.shape[1]
-    rank_dim = width - LANES
+    total, rest = (
+        functools.reduce(jnp.add, [part[:, cut].astype(F32) for part in refs[:-1]])
+        for cut in (slice(0, -LANES), slice(-LANES, None))
+    )
+    rank_dim = total.shape[1] - LANES
+    maps = total[:, rank_dim:] + rest
+    high = maps.astype(BF)
     out_ref[:, 0:rank_dim] = total[:, 0:rank_dim].astype(BF)
-    maps = total[:, rank_dim:]
-    high = maps.astype(BF)
-    out_ref[:, rank_dim:width] = high
-    out_ref[:, width:] = (maps - high.astype(F32)).astype(BF)
+    out_ref[:, rank_dim : rank_dim + LANES] = high
+    out_ref[:, rank_dim + LANES :] = (maps - high.astype(F32)).astype(BF)
 
 
 def sum_parts(parts):
@@ -259,7 +308,7 @@
         sum_kernel,
         in_specs=in_vmem(len(parts)),
         out_specs=in_vmem(1)[0],
-        out_shape=jax.ShapeDtypeStruct((rows, width + LANES), BF),
+        out_shape=jax.ShapeDtypeStruct((rows, width), BF),
         compiler_params=params(8),
     )(*parts)
 
@@ -481,7 +530,7 @@
 
 
 def write_kernel(
-    asked_ref, conv_ref, store_ref, back_ref, conv_out, out_ref, source, hold, came, stage, tails, sems
+    asked_ref, conv_ref, store_ref, back_ref, conv_out, out_ref, source, hold, stage, tails, sems
 ):
     slots, states, channels = out_ref.shape
     groups = channels // LANES
@@ -502,22 +551,12 @@
     def changed(s):
         return pltpu.make_async_copy(stage.at[s], out_ref.at[s], sems.at[s])
 
-    def arrival(s):
-        return pltpu.make_async_copy(
-            back_ref.at[jnp.maximum(source[s], 0)], came.at[s], sems.at[slots + s]
-        )
-
     for s in range(slots):
 
         @pl.when(source[s] < 0)
         def _():
             kept(s).start()
             tails[s * conv_rows : (s + 1) * conv_rows, :] = jnp.zeros((conv_rows, LANES), F32)
-
-        @pl.when(source[s] >= 0)
-        def _():
-            arrival(s).start()
-
     landed = jnp.zeros((slots, LANES), I32)
     slot_of = lax.broadcasted_iota(I32, (slots, LANES), 0)
     for s in range(slots):
@@ -526,15 +565,14 @@
 
         @pl.when(row >= 0)
         def _():
-            arrival(s).wait()
-            hold[s % 2] = came[s, conv_rows:, :].astype(F32)
+            hold[s % 2] = back_ref[row, conv_rows:, :].astype(F32)
             for low in range(0, states, 8):
                 for j in range(groups):
                     stage[s, low : low + 8, j * LANES : (j + 1) * LANES] = hold[
                         s % 2, pl.ds(low * groups + j, 8, stride=groups), :
                     ]
             changed(s).start()
-            tails[s * conv_rows : (s + 1) * conv_rows, :] = came[s, 0:conv_rows, :].astype(F32)
+            tails[s * conv_rows : (s + 1) * conv_rows, :] = back_ref[row, 0:conv_rows, :].astype(F32)
 
     for i in range(3):
         for j in range(groups):
@@ -560,7 +598,7 @@
     return pl.pallas_call(
         write_kernel,
         grid=(1,),
-        in_specs=in_smem(1) + whole(conv_rows) + in_hbm(2),
+        in_specs=in_smem(1) + whole(conv_rows) + in_hbm(1) + in_vmem(1),
         out_specs=whole(conv_rows) + in_hbm(1),
         out_shape=[
             jax.ShapeDtypeStruct(conv_rows.shape, BF),
@@ -569,13 +607,12 @@
         scratch_shapes=[
             SMEM((slots,), I32),
             VMEM((2, states * groups, LANES), F32),
-            VMEM((slots,) + back.shape[1:], BF),
             VMEM((slots, states, channels), F32),
             VMEM((slots * 3 * groups, LANES), F32),
             pltpu.SemaphoreType.DMA((2 * slots,)),
         ],
-        compiler_params=params(),
-    )(asked, *pin(conv_rows, store_state, back))
+        compiler_params=params(24),
+    )(asked, *pin(conv_rows, store_state), back)
 
 
 def exchange(blocks, axis):
@@ -638,8 +675,9 @@
     table, plan = ask(hit_entry, hit_blocks, seg_lengths, rank, slot_count, owner_count)
     asked = exchange(table, "cache")[:, 0, :]
 
-    conv_tiles = store_conv.reshape(slot_count, 3 * groups, LANES)
-    got = exchange(pick(asked, 1, conv_tiles, state_tiles(store_state)), "cache")
+    conv_store = store_conv.transpose(1, 0, 2)
+    tiles = entry_tiles(conv_store, store_state)
+    got = exchange(pick_tiles(asked, tiles, 3 * groups), "cache")
 
     width = tokens + -(-3 * owner_count // LANES) * LANES
     choose = choose_matrix(lengths, hit_entry // slot_count, tokens, owner_count, width)
@@ -653,7 +691,7 @@
     parts = [parts[0]] + [turned(step, parts[step]) for step in range(1, tp_count)]
     summed = sum_parts(parts)
     pieces = [summed] + [turned(step, summed) for step in range(1, tp_count)]
-    got_prefix = exchange(pick(asked, 0, store_keys, store_values), "cache")
+    got_prefix = exchange(pick(asked, *pin(store_keys, store_values)), "cache")
 
     mixer_out, back = scan(
         plan, pieces, mixed, dt_weight, dt_bias, decay_rates, skip_gain, got,
@@ -661,7 +699,7 @@
     )
     back = exchange(back, "cache")
     attn_out = attend(plan, queries, new_keys, new_values, got_prefix)
-    conv_rows, new_state = write_store(asked, store_state, store_conv.transpose(1, 0, 2), back)
+    conv_rows, new_state = write_store(asked, store_state, conv_store, back)
     return (mixer_out, attn_out, new_state, conv_rows.transpose(1, 0, 2))
 
 

time: 174 us -> 167 us (0.960)
  Pallas kernels: 54.5 us -> 47.8 us
  waiting for transfers between devices: 53.5 us -> 55.3 us
    pallas_call x3, Pallas kernels: 15.4 us -> 10.4 us  [the longest x1 4.2 us: pick(): pl.pallas_call(functools.partial(pick_kernel, len(sources)), in_specs=in_...]
    all_to_all x4, waiting for transfers between devices: 46.2 us -> 49.5 us  [exchange(): return lax.all_to_all(blocks, axis, split_axis=0, concat_axis=0, tiled=True)]
  transfers between devices with their start and end apart: 18 -> 18, of which waited for: 8 -> 7; matrix products, arithmetic and copies ran while one was open for 2% -> 1% of each run, Pallas kernels for 25% -> 24%
where the time goes in v3:
time: 167 us; the launch traced here: 166 us
  starting transfers between devices  57.6 us (34%)
  waiting for transfers between devices  55.3 us (33%)
  Pallas kernels  47.8 us (29%)
  local copies, waits for them, and re-layouts  3.19 us (2%)
    all_to_all x4, waiting for transfers between devices, exchange(): return lax.all_to_all(blocks, axis, split_axis=0, concat_axis=0, tiled=True)  49.5 us
    all_to_all x4, starting transfers between devices, exchange(): return lax.all_to_all(blocks, axis, split_axis=0, concat_axis=0, tiled=True)  30.3 us
    ppermute x14, starting transfers between devices, turned(): lax.ppermute(value, 'tp', [(k, (k + step) % tp_count) for k in range(tp_c...  27.3 us
    pallas_call x1, Pallas kernels, attend(): pl.pallas_call(functools.partial(attend_kernel, count), grid=(1,), in_spe...  14.1 us
    pallas_call x1, Pallas kernels, scan(): pl.pallas_call(functools.partial(scan_kernel, states, count), in_specs=in...  12.9 us
    ppermute x14, waiting for transfers between devices, turned(): lax.ppermute(value, 'tp', [(k, (k + step) % tp_count) for k in range(tp_c...  5.78 us
    pallas_call x1, Pallas kernels, conv_project(): pl.pallas_call(conv_kernel, grid=(channels // chunk,), in_specs=in_smem(1...  4.69 us
    pallas_call x1, Pallas kernels, write_store(): pl.pallas_call(write_kernel, grid=(1,), in_specs=in_smem(1) + whole(conv_...  4.21 us
  transfers between devices with their start and end apart: 18, of which 7 were waited for; matrix products, arithmetic and copies ran while one was open for 1% of the time, Pallas kernels for 24%

profile of v3, /device:TPU:1, one launch (start us, length us, event | category | flops | bytes accessed | tf_op | source)
XLA Modules:
  0.0 166.3 jit_solution(5906730686218016334)
XLA Ops:
  0.6 1.4 shard_map.201
  2.1 8.6 %all-to-all-start = ((s32[32,1,128]{2,1,0:T(1,128)}), s32[32,1,128]{2,1,0:T(1,128)S(1)}, u32[]{:S(2)}, u32[]{:S(2)}) async-start(s32[32,1,128]{2,1,0:T(1,128)} %get-tuple-element.21), calls=%async_computation | async-start | bytes 32768 | tf_op jit(solution)/shard_map/all_to_all | solution.py:619
  10.7 4.0 %shard_map.202.tiles_ref = bf16[20,304,128]{2,1,0:T(8,128)(2,1)S(1)} custom-call(bf16[3,20,2048]{2,1,0:T(8,128)(2,1)} %bitcast.21, f32[20,16,2048]{2,1,0:T(8,128)} %store_ref.1), custom_call_target="tpu_custom_call" | custom-call | tf_op jit(solution)/shard_map/pallas_call | solution.py:108
  14.7 2.9 %all-to-all-done = s32[32,1,128]{2,1,0:T(1,128)S(1)} async-done(((s32[32,1,128]{2,1,0:T(1,128)}), s32[32,1,128]{2,1,0:T(1,128)S(1)}, u32[]{:S(2)}, u32[]{:S(2)}) %all-to-all-start) | async-done | bytes 16416 | tf_op jit(solution)/shard_map/all_to_all | solution.py:619
  17.6 2.2 %shard_map.203 = bf16[32,304,128]{2,1,0:T(8,128)(2,1)} custom-call(s32[32,128]{1,0:T(8,128)S(1)} %bitcast.18, bf16[20,304,128]{2,1,0:T(8,128)(2,1)S(1)} %shard_map.202.tiles_ref), custom_call_target="tpu_custom_call" | custom-call | tf_op jit(solution)/shard_map/pallas_call | solution.py:191
  19.7 4.5 %all-to-all-start.1 = ((bf16[32,304,128]{2,1,0:T(8,128)(2,1)}), bf16[32,304,128]{2,1,0:T(8,128)(2,1)S(1)}, u32[]{:S(2)}, u32[]{:S(2)}) async-start(bf16[32,304,128]{2,1,0:T(8,128)(2,1)} %shard_map.203), calls=%async_computation.1 | async-start | bytes 4980736 | tf_op jit(solution)/shard_map/all_to_all | solution.py:619
  24.3 4.2 %shard_map.207 = bf16[32,512,128]{2,1,0:T(8,128)(2,1)} custom-call(s32[32,128]{1,0:T(8,128)S(1)} %bitcast.19, bf16[20,256,128]{2,1,0:T(8,128)(2,1)} %refs_0_.1, bf16[20,256,128]{2,1,0:T(8,128)(2,1)} %refs_1_.1), custom_call_target="tpu_custom_call" | custom-call | tf_op jit(solution)/shard_map/pallas_call | solution.py:156
  28.5 28.3 %all-to-all-done.1.got_ref.refs_13_ = bf16[32,304,128]{2,1,0:T(8,128)(2,1)S(1)} async-done(((bf16[32,304,128]{2,1,0:T(8,128)(2,1)}), bf16[32,304,128]{2,1,0:T(8,128)(2,1)S(1)}, u32[]{:S(2)}, u32[]{:S(2)}) %all-to-all-start.1) | async-done | bytes 2490400 | tf_op jit(solution)/shard_map/all_to_all | solution.py:619
  56.8 1.4 copy-done.3
  58.3 5.4 %all-to-all-start.2 = ((bf16[32,512,128]{2,1,0:T(8,128)(2,1)}), bf16[32,512,128]{2,1,0:T(8,128)(2,1)}, u32[]{:S(2)}, u32[]{:S(2)}) async-start(bf16[32,512,128]{2,1,0:T(8,128)(2,1)} %shard_map.207), calls=%async_computation.2 | async-start | bytes 8388608 | tf_op jit(solution)/shard_map/all_to_all | solution.py:619
  64.5 0.8 fusion.choose_ref
  65.3 4.7 %shard_map.204 = (bf16[16,768]{1,0:T(8,128)(2,1)S(1)}, bf16[16,768]{1,0:T(8,128)(2,1)S(1)}, bf16[16,768]{1,0:T(8,128)(2,1)S(1)}, bf16[16,768]{1,0:T(8,128)(2,1)S...) custom-call(s32[49]{0:T(128)S(1)} %copy-done.2, ...), custom_call_target="tpu_custom_call" | custom-call | tf_op jit(solution)/shard_map/pallas_call | solution.py:259
  70.0 0.8 copy-done
  70.8 0.7 copy-done.1
  71.5 1.6 collective-permute-start
  73.2 3.0 %collective-permute-start.1 = (bf16[16,768]{1,0:T(8,128)(2,1)S(1)}, bf16[16,768]{1,0:T(8,128)(2,1)S(1)}, u32[]{:S(2)}, u32[]{:S(2)}) collective-permute-start(bf16[16,768]{1,0:T(8,128)(2,1)S(1)} %get-tuple-element.24), channel_id=1, source_target_pairs={{0,2},{1,3},{2,4},{3,5},{4,6},{5,7},{6,0},{7,1},{8,10},{9,11},{10,... | collective-permute-start | bytes 73736 | tf_op jit(solution)/shard_map/ppermute | solution.py:689
  76.2 3.8 %collective-permute-start.2 = (bf16[16,768]{1,0:T(8,128)(2,1)S(1)}, bf16[16,768]{1,0:T(8,128)(2,1)S(1)}, u32[]{:S(2)}, u32[]{:S(2)}) collective-permute-start(bf16[16,768]{1,0:T(8,128)(2,1)S(1)} %get-tuple-element.25), channel_id=1, source_target_pairs={{0,3},{1,4},{2,5},{3,6},{4,7},{5,0},{6,1},{7,2},{8,11},{9,12},{10,... | collective-permute-start | bytes 73736 | tf_op jit(solution)/shard_map/ppermute | solution.py:689
  80.4 4.5 %collective-permute-start.4 = (bf16[16,768]{1,0:T(8,128)(2,1)S(1)}, bf16[16,768]{1,0:T(8,128)(2,1)S(1)}, u32[]{:S(2)}, u32[]{:S(2)}) collective-permute-start(bf16[16,768]{1,0:T(8,128)(2,1)S(1)} %get-tuple-element.27), channel_id=1, source_target_pairs={{0,5},{1,6},{2,7},{3,0},{4,1},{5,2},{6,3},{7,4},{8,13},{9,14},{10,... | collective-permute-start | bytes 73736 | tf_op jit(solution)/shard_map/ppermute | solution.py:689
  84.9 2.4 %collective-permute-start.5 = (bf16[16,768]{1,0:T(8,128)(2,1)S(1)}, bf16[16,768]{1,0:T(8,128)(2,1)S(1)}, u32[]{:S(2)}, u32[]{:S(2)}) collective-permute-start(bf16[16,768]{1,0:T(8,128)(2,1)S(1)} %get-tuple-element.28), channel_id=1, source_target_pairs={{0,6},{1,7},{2,0},{3,1},{4,2},{5,3},{6,4},{7,5},{8,14},{9,15},{10,... | collective-permute-start | bytes 73736 | tf_op jit(solution)/shard_map/ppermute | solution.py:689
  88.0 1.8 %collective-permute-done.5.refs_6_ = bf16[16,768]{1,0:T(8,128)(2,1)S(1)} collective-permute-done((bf16[16,768]{1,0:T(8,128)(2,1)S(1)}, bf16[16,768]{1,0:T(8,128)(2,1)S(1)}, u32[]{:S(2)}, u32[]{:S(2)}) %collective-permute-start.5) | collective-permute-done | bytes 24608 | tf_op jit(solution)/shard_map/ppermute | solution.py:689
  90.5 1.3 collective-permute-start.8
  91.8 3.7 %collective-permute-start.9 = (bf16[16,768]{1,0:T(8,128)(2,1)S(1)}, bf16[16,768]{1,0:T(8,128)(2,1)S(1)}, u32[]{:S(2)}, u32[]{:S(2)}) collective-permute-start(bf16[16,768]{1,0:T(8,128)(2,1)S(1)} %shard_map.205.refs_0_), channel_id=1, source_target_pairs={{0,3},{1,4},{2,5},{3,6},{4,7},{5,0},{6,1},{7,2},{8,11},{9,12},{10,... | collective-permute-start | bytes 73736 | tf_op jit(solution)/shard_map/ppermute | solution.py:689
  95.4 1.2 collective-permute-start.10
  96.6 3.6 %collective-permute-start.11 = (bf16[16,768]{1,0:T(8,128)(2,1)S(1)}, bf16[16,768]{1,0:T(8,128)(2,1)S(1)}, u32[]{:S(2)}, u32[]{:S(2)}) collective-permute-start(bf16[16,768]{1,0:T(8,128)(2,1)S(1)} %shard_map.205.refs_0_), channel_id=1, source_target_pairs={{0,5},{1,6},{2,7},{3,0},{4,1},{5,2},{6,3},{7,4},{8,13},{9,14},{10,... | collective-permute-start | bytes 73736 | tf_op jit(solution)/shard_map/ppermute | solution.py:689
  100.2 0.9 collective-permute-start.12
  101.3 1.3 collective-permute-done.10.refs_4_
  102.6 2.1 %collective-permute-done.12.refs_6_ = bf16[16,768]{1,0:T(8,128)(2,1)S(1)} collective-permute-done((bf16[16,768]{1,0:T(8,128)(2,1)S(1)}, bf16[16,768]{1,0:T(8,128)(2,1)S(1)}, u32[]{:S(2)}, u32[]{:S(2)}) %collective-permute-start.12) | collective-permute-done | bytes 24608 | tf_op jit(solution)/shard_map/ppermute | solution.py:689
  104.7 12.9 %shard_map.206 = (bf16[128,2048]{1,0:T(8,128)(2,1)}, bf16[32,304,128]{2,1,0:T(8,128)(2,1)}) custom-call(s32[49]{0:T(128)S(1)} %copy-done.2, bf16[16,768]{1,0:T(8,128)(2,1)S(1)} %shard_map.205.refs_0_, bf16[16,768]{1,0:T(8,128)(2,1)S(1)} %collective-permute-done.7.refs_1_, bf16[16,768]{1,0:T(8,128)(2,1)S(1)} %collective-permute-done.8.refs_2_, ...), custom_call_target="tpu_custom_call" | custom-call | tf_op jit(solution)/shard_map/pallas_call | solution.py:431
  117.6 11.8 %all-to-all-start.3 = ((bf16[32,304,128]{2,1,0:T(8,128)(2,1)}), bf16[32,304,128]{2,1,0:T(8,128)(2,1)S(1)}, u32[]{:S(2)}, u32[]{:S(2)}) async-start(bf16[32,304,128]{2,1,0:T(8,128)(2,1)} %get-tuple-element.33), calls=%async_computation.3 | async-start | bytes 4980736 | tf_op jit(solution)/shard_map/all_to_all | solution.py:619
  129.4 14.1 %shard_map.208 = bf16[128,512]{1,0:T(8,128)(2,1)} custom-call(s32[49]{0:T(128)} %get-tuple-element.20.plan_ref, bf16[128,512]{1,0:T(8,128)(2,1)} %q_ref.1, bf16[128,128]{1,0:T(8,128)(2,1)} %k_ref.1, bf16[128,128]{1,0:T(8,128)(2,1)} %v_ref.1, bf16[32,512,128]{2,1,0:T(8,128)(2,1)} %all-to-all-done.2.got_ref), custom_call_target="tpu_custom_call" | custom-call | tf_op jit(solution)/shard_map/pallas_call | solution.py:516
  143.5 18.4 %all-to-all-done.3.back_ref = bf16[32,304,128]{2,1,0:T(8,128)(2,1)S(1)} async-done(((bf16[32,304,128]{2,1,0:T(8,128)(2,1)}), bf16[32,304,128]{2,1,0:T(8,128)(2,1)S(1)}, u32[]{:S(2)}, u32[]{:S(2)}) %all-to-all-start.3) | async-done | bytes 2490400 | tf_op jit(solution)/shard_map/all_to_all | solution.py:619
  161.9 4.2 %shard_map.209 = (bf16[3,20,2048]{2,1,0:T(8,128)(2,1)}, f32[20,16,2048]{2,1,0:T(8,128)}) custom-call(s32[32,128]{1,0:T(8,128)S(1)} %bitcast.20, bf16[3,20,2048]{2,1,0:T(8,128)(2,1)} %bitcast.22, f32[20,16,2048]{2,1,0:T(8,128)} %store_ref.1, bf16[32,304,128]{2,1,0:T(8,128)(2,1)S(1)} %all-to-all-done.3.back_ref), custom_call_target="tpu_custom_call" | custom-call | tf_op jit(solution)/shard_map/pallas_call | solution.py:598
  (41 shorter events, 2.8 us)
Async XLA Ops:
  2.1 15.5 %all-to-all-start = ((s32[32,1,128]{2,1,0:T(1,128)}), s32[32,1,128]{2,1,0:T(1,128)S(1)}, u32[]{:S(2)}, u32[]{:S(2)}) async-start(s32[32,1,128]{2,1,0:T(1,128)} %get-tuple-element.21), calls=%async_computation | async-start | bytes 32768 | tf_op jit(solution)/shard_map/all_to_all | solution.py:619
  19.7 37.1 %all-to-all-start.1 = ((bf16[32,304,128]{2,1,0:T(8,128)(2,1)}), bf16[32,304,128]{2,1,0:T(8,128)(2,1)S(1)}, u32[]{:S(2)}, u32[]{:S(2)}) async-start(bf16[32,304,128]{2,1,0:T(8,128)(2,1)} %shard_map.203), calls=%async_computation.1 | async-start | bytes 4980736 | tf_op jit(solution)/shard_map/all_to_all | solution.py:619
  28.5 35.2 %copy-start.4 = (s32[1,16]{1,0:T(1,128)S(1)}, s32[1,16]{1,0:T(1,128)}, u32[]{:S(2)}) copy-start(s32[1,16]{1,0:T(1,128)} %length_ref.1) | copy-start | bytes 196
  28.5 35.4 %copy-start.5 = (s32[16]{0:T(128)S(1)}, s32[16]{0:T(128)}, u32[]{:S(2)}) copy-start(s32[16]{0:T(128)} %entry_ref.1) | copy-start | bytes 196
  28.5 36.8 %copy-start.2 = (s32[49]{0:T(128)S(1)}, s32[49]{0:T(128)}, u32[]{:S(2)}) copy-start(s32[49]{0:T(128)} %get-tuple-element.20.plan_ref) | copy-start | bytes 592
  56.8 1.4 copy-start.3
  58.3 59.4 %all-to-all-start.2 = ((bf16[32,512,128]{2,1,0:T(8,128)(2,1)}), bf16[32,512,128]{2,1,0:T(8,128)(2,1)}, u32[]{:S(2)}, u32[]{:S(2)}) async-start(bf16[32,512,128]{2,1,0:T(8,128)(2,1)} %shard_map.207), calls=%async_computation.2 | async-start | bytes 8388608 | tf_op jit(solution)/shard_map/all_to_all | solution.py:619
  70.0 0.8 copy-start
  70.8 0.7 copy-start.1
  71.5 13.3 %collective-permute-start = (bf16[16,768]{1,0:T(8,128)(2,1)S(1)}, bf16[16,768]{1,0:T(8,128)(2,1)S(1)}, u32[]{:S(2)}, u32[]{:S(2)}) collective-permute-start(bf16[16,768]{1,0:T(8,128)(2,1)S(1)} %get-tuple-element.23), channel_id=1, source_target_pairs={{0,1},{1,2},{2,3},{3,4},{4,5},{5,6},{6,7},{7,0},{8,9},{9,10},{10,1... | collective-permute-start | bytes 73736 | tf_op jit(solution)/shard_map/ppermute | solution.py:689
  73.2 14.1 %collective-permute-start.1 = (bf16[16,768]{1,0:T(8,128)(2,1)S(1)}, bf16[16,768]{1,0:T(8,128)(2,1)S(1)}, u32[]{:S(2)}, u32[]{:S(2)}) collective-permute-start(bf16[16,768]{1,0:T(8,128)(2,1)S(1)} %get-tuple-element.24), channel_id=1, source_target_pairs={{0,2},{1,3},{2,4},{3,5},{4,6},{5,7},{6,0},{7,1},{8,10},{9,11},{10,... | collective-permute-start | bytes 73736 | tf_op jit(solution)/shard_map/ppermute | solution.py:689
  76.2 11.8 %collective-permute-start.2 = (bf16[16,768]{1,0:T(8,128)(2,1)S(1)}, bf16[16,768]{1,0:T(8,128)(2,1)S(1)}, u32[]{:S(2)}, u32[]{:S(2)}) collective-permute-start(bf16[16,768]{1,0:T(8,128)(2,1)S(1)} %get-tuple-element.25), channel_id=1, source_target_pairs={{0,3},{1,4},{2,5},{3,6},{4,7},{5,0},{6,1},{7,2},{8,11},{9,12},{10,... | collective-permute-start | bytes 73736 | tf_op jit(solution)/shard_map/ppermute | solution.py:689
  79.9 8.1 %collective-permute-start.3 = (bf16[16,768]{1,0:T(8,128)(2,1)S(1)}, bf16[16,768]{1,0:T(8,128)(2,1)S(1)}, u32[]{:S(2)}, u32[]{:S(2)}) collective-permute-start(bf16[16,768]{1,0:T(8,128)(2,1)S(1)} %get-tuple-element.26), channel_id=1, source_target_pairs={{0,4},{1,5},{2,6},{3,7},{4,0},{5,1},{6,2},{7,3},{8,12},{9,13},{10,... | collective-permute-start | bytes 73736 | tf_op jit(solution)/shard_map/ppermute | solution.py:689
  80.4 7.6 %collective-permute-start.4 = (bf16[16,768]{1,0:T(8,128)(2,1)S(1)}, bf16[16,768]{1,0:T(8,128)(2,1)S(1)}, u32[]{:S(2)}, u32[]{:S(2)}) collective-permute-start(bf16[16,768]{1,0:T(8,128)(2,1)S(1)} %get-tuple-element.27), channel_id=1, source_target_pairs={{0,5},{1,6},{2,7},{3,0},{4,1},{5,2},{6,3},{7,4},{8,13},{9,14},{10,... | collective-permute-start | bytes 73736 | tf_op jit(solution)/shard_map/ppermute | solution.py:689
  84.9 4.9 %collective-permute-start.5 = (bf16[16,768]{1,0:T(8,128)(2,1)S(1)}, bf16[16,768]{1,0:T(8,128)(2,1)S(1)}, u32[]{:S(2)}, u32[]{:S(2)}) collective-permute-start(bf16[16,768]{1,0:T(8,128)(2,1)S(1)} %get-tuple-element.28), channel_id=1, source_target_pairs={{0,6},{1,7},{2,0},{3,1},{4,2},{5,3},{6,4},{7,5},{8,14},{9,15},{10,... | collective-permute-start | bytes 73736 | tf_op jit(solution)/shard_map/ppermute | solution.py:689
  87.2 3.1 %collective-permute-start.6 = (bf16[16,768]{1,0:T(8,128)(2,1)S(1)}, bf16[16,768]{1,0:T(8,128)(2,1)S(1)}, u32[]{:S(2)}, u32[]{:S(2)}) collective-permute-start(bf16[16,768]{1,0:T(8,128)(2,1)S(1)} %get-tuple-element.29), channel_id=1, source_target_pairs={{0,7},{1,0},{2,1},{3,2},{4,3},{5,4},{6,5},{7,6},{8,15},{9,8},{10,9... | collective-permute-start | bytes 73736 | tf_op jit(solution)/shard_map/ppermute | solution.py:689
  90.4 9.8 %collective-permute-start.7 = (bf16[16,768]{1,0:T(8,128)(2,1)S(1)}, bf16[16,768]{1,0:T(8,128)(2,1)S(1)}, u32[]{:S(2)}, u32[]{:S(2)}) collective-permute-start(bf16[16,768]{1,0:T(8,128)(2,1)S(1)} %shard_map.205.refs_0_), channel_id=1, source_target_pairs={{0,1},{1,2},{2,3},{3,4},{4,5},{5,6},{6,7},{7,0},{8,9},{9,10},{10,1... | collective-permute-start | bytes 73736 | tf_op jit(solution)/shard_map/ppermute | solution.py:689
  90.5 10.7 %collective-permute-start.8 = (bf16[16,768]{1,0:T(8,128)(2,1)S(1)}, bf16[16,768]{1,0:T(8,128)(2,1)S(1)}, u32[]{:S(2)}, u32[]{:S(2)}) collective-permute-start(bf16[16,768]{1,0:T(8,128)(2,1)S(1)} %shard_map.205.refs_0_), channel_id=1, source_target_pairs={{0,2},{1,3},{2,4},{3,5},{4,6},{5,7},{6,0},{7,1},{8,10},{9,11},{10,... | collective-permute-start | bytes 73736 | tf_op jit(solution)/shard_map/ppermute | solution.py:689
  91.8 9.5 %collective-permute-start.9 = (bf16[16,768]{1,0:T(8,128)(2,1)S(1)}, bf16[16,768]{1,0:T(8,128)(2,1)S(1)}, u32[]{:S(2)}, u32[]{:S(2)}) collective-permute-start(bf16[16,768]{1,0:T(8,128)(2,1)S(1)} %shard_map.205.refs_0_), channel_id=1, source_target_pairs={{0,3},{1,4},{2,5},{3,6},{4,7},{5,0},{6,1},{7,2},{8,11},{9,12},{10,... | collective-permute-start | bytes 73736 | tf_op jit(solution)/shard_map/ppermute | solution.py:689
  95.4 7.2 %collective-permute-start.10 = (bf16[16,768]{1,0:T(8,128)(2,1)S(1)}, bf16[16,768]{1,0:T(8,128)(2,1)S(1)}, u32[]{:S(2)}, u32[]{:S(2)}) collective-permute-start(bf16[16,768]{1,0:T(8,128)(2,1)S(1)} %shard_map.205.refs_0_), channel_id=1, source_target_pairs={{0,4},{1,5},{2,6},{3,7},{4,0},{5,1},{6,2},{7,3},{8,12},{9,13},{10,... | collective-permute-start | bytes 73736 | tf_op jit(solution)/shard_map/ppermute | solution.py:689
  96.6 6.0 %collective-permute-start.11 = (bf16[16,768]{1,0:T(8,128)(2,1)S(1)}, bf16[16,768]{1,0:T(8,128)(2,1)S(1)}, u32[]{:S(2)}, u32[]{:S(2)}) collective-permute-start(bf16[16,768]{1,0:T(8,128)(2,1)S(1)} %shard_map.205.refs_0_), channel_id=1, source_target_pairs={{0,5},{1,6},{2,7},{3,0},{4,1},{5,2},{6,3},{7,4},{8,13},{9,14},{10,... | collective-permute-start | bytes 73736 | tf_op jit(solution)/shard_map/ppermute | solution.py:689
  100.2 4.5 %collective-permute-start.12 = (bf16[16,768]{1,0:T(8,128)(2,1)S(1)}, bf16[16,768]{1,0:T(8,128)(2,1)S(1)}, u32[]{:S(2)}, u32[]{:S(2)}) collective-permute-start(bf16[16,768]{1,0:T(8,128)(2,1)S(1)} %shard_map.205.refs_0_), channel_id=1, source_target_pairs={{0,6},{1,7},{2,0},{3,1},{4,2},{5,3},{6,4},{7,5},{8,14},{9,15},{10,... | collective-permute-start | bytes 73736 | tf_op jit(solution)/shard_map/ppermute | solution.py:689
  101.1 3.6 %collective-permute-start.13 = (bf16[16,768]{1,0:T(8,128)(2,1)S(1)}, bf16[16,768]{1,0:T(8,128)(2,1)S(1)}, u32[]{:S(2)}, u32[]{:S(2)}) collective-permute-start(bf16[16,768]{1,0:T(8,128)(2,1)S(1)} %shard_map.205.refs_0_), channel_id=1, source_target_pairs={{0,7},{1,0},{2,1},{3,2},{4,3},{5,4},{6,5},{7,6},{8,15},{9,8},{10,9... | collective-permute-start | bytes 73736 | tf_op jit(solution)/shard_map/ppermute | solution.py:689
  117.6 44.3 %all-to-all-start.3 = ((bf16[32,304,128]{2,1,0:T(8,128)(2,1)}), bf16[32,304,128]{2,1,0:T(8,128)(2,1)S(1)}, u32[]{:S(2)}, u32[]{:S(2)}) async-start(bf16[32,304,128]{2,1,0:T(8,128)(2,1)} %get-tuple-element.33), calls=%async_computation.3 | async-start | bytes 4980736 | tf_op jit(solution)/shard_map/all_to_all | solution.py:619

commit v4 on v3

--- a/solution.py
+++ b/solution.py
@@ -198,94 +198,113 @@
     )(asked, tiles)
 
 
-def conv_kernel(plan_ref, x_ref, got_ref, choose_ref, weight_ref, in_ref, bc_ref, *refs):
-    parts, (mixed_ref, tail_ref), (source, wide, total, tails) = refs[:8], refs[8:10], refs[10:]
-    tokens, chunk = x_ref.shape
-    step, last = pl.program_id(0), pl.num_programs(0) - 1
-    groups = got_ref.shape[1] // 3
+def bring_kernel(count, after_ref, *refs):
+    sources, targets = refs[:count], refs[count + 1 : 2 * count + 1]
+    decay_ref, tile_ref, sems = refs[count], refs[2 * count + 1], refs[2 * count + 2]
+    copies = [
+        pltpu.make_async_copy(source, target, sems.at[n])
+        for n, (source, target) in enumerate(zip(sources, targets))
+    ]
+    for copy in copies:
+        copy.start()
+    states, channels = decay_ref.shape
+    groups = channels // LANES
+    for low in range(0, states, 8):
+        for j in range(groups):
+            tile_ref[pl.ds(low * groups + j, 8, stride=groups), :] = decay_ref[
+                low : low + 8, j * LANES : (j + 1) * LANES
+            ] * (-math.log2(math.e))
+    for copy in copies:
+        copy.wait()
+
+
+def bring(after, decay_rates, *arrays):
+    states, channels = decay_rates.shape
+    return pl.pallas_call(
+        functools.partial(bring_kernel, len(arrays)),
+        in_specs=in_hbm(1 + len(arrays)) + in_vmem(1),
+        out_specs=in_vmem(len(arrays) + 1),
+        out_shape=[jax.ShapeDtypeStruct(a.shape, a.dtype) for a in arrays]
+        + [jax.ShapeDtypeStruct((states * channels // LANES, LANES), F32)],
+        scratch_shapes=[pltpu.SemaphoreType.DMA((len(arrays),))],
+        compiler_params=params(4),
+    )(*pin(after, *arrays), decay_rates)
+
+
+def conv_kernel(plan_ref, x_ref, choose_ref, weight_ref, in_ref, bc_ref, got_ref, *refs):
+    parts, (mixed_ref, tail_ref), (source, wide, total, tails, came, sem) = (
+        refs[:8], refs[8:10], refs[10:]
+    )
+    tokens, channels = x_ref.shape
+    groups = channels // LANES
     olds = got_ref.shape[0] * 3
     rank_dim = in_ref.shape[1]
-
-    @pl.when(step == 0)
-    def _():
-        wide[...] = got_ref[...].reshape(olds * groups, LANES).astype(F32)
-        source[tokens + olds :, :] = jnp.zeros((source.shape[0] - tokens - olds, chunk), BF)
-        total[...] = jnp.zeros(total.shape, F32)
-
-    source[0:tokens, :] = x_ref[...]
-    low = step * (chunk // LANES)
-    for j in range(chunk // LANES):
-        source[tokens : tokens + olds, j * LANES : (j + 1) * LANES] = wide[
-            pl.ds(low + j, olds, stride=groups), :
-        ].astype(BF)
-    taken = jnp.dot(choose_ref[...], source[...], preferred_element_type=F32)
-    running = weight_ref[3:4, :] * x_ref[...].astype(F32)
-    for lag in range(1, 4):
-        running = (
-            running + weight_ref[3 - lag : 4 - lag, :] * taken[(lag - 1) * tokens : lag * tokens]
+    chunk = source.shape[1]
+    copy = pltpu.make_async_copy(got_ref.at[:, pl.ds(0, 3 * groups)], came, sem)
+    copy.start()
+    source[tokens + olds :, :] = jnp.zeros((source.shape[0] - tokens - olds, chunk), BF)
+    total[...] = jnp.zeros(total.shape, F32)
+    copy.wait()
+    wide[...] = came[...].reshape(olds * groups, LANES).astype(F32)
+    for low in range(0, channels, chunk):
+        cut = slice(low, low + chunk)
+        source[0:tokens, :] = x_ref[:, cut]
+        for j in range(chunk // LANES):
+            source[tokens : tokens + olds, j * LANES : (j + 1) * LANES] = wide[
+                pl.ds(low // LANES + j, olds, stride=groups), :
+            ].astype(BF)
+        taken = jnp.dot(choose_ref[...], source[...], preferred_element_type=F32)
+        running = weight_ref[3:4, cut] * x_ref[:, cut].astype(F32)
+        for lag in range(1, 4):
+            running = (
+                running
+                + weight_ref[3 - lag : 4 - lag, cut] * taken[(lag - 1) * tokens : lag * tokens]
+            )
+        mixed = (running / (1.0 + jnp.exp(-running))).astype(BF)
+        mixed_ref[:, cut] = mixed
+        for j in range(chunk // LANES):
+            tails[pl.ds(low // LANES + j, olds, stride=groups), :] = taken[
+                3 * tokens :, j * LANES : (j + 1) * LANES
+            ]
+        maps = lax.dot_general(
+            mixed, bc_ref[:, cut], (((1,), (1,)), ((), ())), preferred_element_type=F32
         )
-    mixed = (running / (1.0 + jnp.exp(-running))).astype(BF)
-    mixed_ref[...] = mixed
-    for j in range(chunk // LANES):
-        tails[pl.ds(low + j, olds, stride=groups), :] = taken[
-            3 * tokens :, j * LANES : (j + 1) * LANES
-        ]
-    maps = lax.dot_general(
-        mixed, bc_ref[...], (((1,), (1,)), ((), ())), preferred_element_type=F32
-    )
-    total[:, 0:rank_dim] += jnp.dot(mixed, in_ref[...], preferred_element_type=F32)
-    total[:, rank_dim : rank_dim + maps.shape[1]] += maps
-
-    @pl.when(step == last)
-    def _():
-        tail_ref[...] = tails[...].astype(BF)
-        share, width = tokens // 8, total.shape[1]
-        for turn, part in enumerate(parts):
-            place = lax.rem(plan_ref[plan_ref.shape[0] - 1] + turn, 8) * share
-            rows = total[pl.ds(pl.multiple_of(place, share), share), :]
-            high = rows.astype(BF)
-            part[:, 0:width] = high
-            part[:, width:] = (rows[:, rank_dim:] - high[:, rank_dim:].astype(F32)).astype(BF)
-
-
-def conv_project(plan, x_rows, got, choose, conv_weight, dt_in_weight, bc_weight):
+        total[:, 0:rank_dim] += jnp.dot(mixed, in_ref[cut, :], preferred_element_type=F32)
+        total[:, rank_dim : rank_dim + maps.shape[1]] += maps
+    tail_ref[...] = tails[...].reshape(tail_ref.shape).astype(BF)
+    share, width = tokens // 8, total.shape[1]
+    for turn, part in enumerate(parts):
+        place = lax.rem(plan_ref[plan_ref.shape[0] - 1] + turn, 8) * share
+        rows = total[pl.ds(pl.multiple_of(place, share), share), :]
+        high = rows.astype(BF)
+        part[:, 0:width] = high
+        part[:, width:] = (rows[:, rank_dim:] - high[:, rank_dim:].astype(F32)).astype(BF)
+
+
+def conv_project(plan, x_rows, choose, conv_weight, dt_in_weight, bc_weight, got):
     tokens, channels = x_rows.shape
-    rank_dim = dt_in_weight.shape[1]
-    width = rank_dim + LANES
+    width = dt_in_weight.shape[1] + LANES
     conv_rows = 3 * channels // LANES
     tail_rows = got.shape[0] * conv_rows
-    chunk = min(512, channels)
-    once = pl.Buffered(1)
     return pl.pallas_call(
         conv_kernel,
-        grid=(channels // chunk,),
-        in_specs=in_smem(1)
-        + [
-            pl.BlockSpec((tokens, chunk), lambda i: (0, i)),
-            pl.BlockSpec((got.shape[0], conv_rows, LANES), lambda i: (0, 0, 0), pipeline_mode=once),
-            pl.BlockSpec(choose.shape, lambda i: (0, 0), pipeline_mode=once),
-            pl.BlockSpec((4, chunk), lambda i: (0, i)),
-            pl.BlockSpec((chunk, rank_dim), lambda i: (i, 0)),
-            pl.BlockSpec((bc_weight.shape[0], chunk), lambda i: (0, i)),
-        ],
-        out_specs=in_vmem(8)
-        + [
-            pl.BlockSpec((tokens, chunk), lambda i: (0, i)),
-            pl.BlockSpec((tail_rows, LANES), lambda i: (0, 0), pipeline_mode=once),
-        ],
+        in_specs=in_smem(1) + in_vmem(5) + [pl.BlockSpec(memory_space=pl.ANY)],
+        out_specs=in_vmem(10),
         out_shape=[jax.ShapeDtypeStruct((tokens // 8, width + LANES), BF)] * 8
         + [
             jax.ShapeDtypeStruct((tokens, channels), BF),
-            jax.ShapeDtypeStruct((tail_rows, LANES), BF),
+            jax.ShapeDtypeStruct((got.shape[0], conv_rows, LANES), BF),
         ],
         scratch_shapes=[
-            VMEM((choose.shape[1], chunk), BF),
+            VMEM((choose.shape[1], min(512, channels)), BF),
             VMEM((tail_rows, LANES), F32),
             VMEM((tokens, width), F32),
             VMEM((tail_rows, LANES), F32),
+            VMEM((got.shape[0], conv_rows, LANES), BF),
+            pltpu.SemaphoreType.DMA,
         ],
         compiler_params=params(24),
-    )(plan, *pin(x_rows, got, choose, conv_weight, dt_in_weight, bc_weight))
+    )(plan, x_rows, choose, conv_weight, dt_in_weight, bc_weight, got)
 
 
 def sum_kernel(*refs):
@@ -315,15 +334,9 @@
 
 def scan_kernel(states, count, plan_ref, *refs):
     pieces = refs[0:8]
-    brought, (start_ref, tail_hbm, out_ref, back_ref) = refs[8:13], refs[13:17]
-    mixed_ref, weight_ref, bias_ref, decay_ref, skip_ref, tail_ref = refs[17:23]
-    low_dt, maps, map_smem, rates, drives, sums, decays, begun, ready, sem, sems, own = refs[23:]
-    fetches = [
-        pltpu.make_async_copy(source, target, own.at[n])
-        for n, (source, target) in enumerate(zip((*brought, tail_hbm), refs[17:23]))
-    ]
-    for n in (1, 2, 0, 3, 4, 5):
-        fetches[n].start()
+    mixed_ref, weight_ref, bias_ref, skip_ref, tail_ref, decays, start_ref = refs[8:15]
+    out_ref, back_ref = refs[15:17]
+    low_dt, maps, map_smem, rates, drives, sums, begun, ready, sem, sems = refs[17:]
     tokens, channels = mixed_ref.shape
     groups = channels // LANES
     share = tokens // 8
@@ -350,6 +363,7 @@
 
     for r in range(count):
         receive(r).start()
+        send_tail(r).start()
     for step, piece in enumerate(pieces):
         place = pl.multiple_of(lax.rem(rank + 8 - step, 8) * share, share)
         low_dt[pl.ds(place, share), :] = piece[:, 0:rank_dim]
@@ -358,14 +372,6 @@
         ].astype(F32)
     copy = pltpu.make_async_copy(maps, map_smem, sem)
     copy.start()
-    fetches[3].wait()
-    for low in range(0, states, 8):
-        for j in range(groups):
-            decays[pl.ds(low * groups + j, 8, stride=groups), :] = decay_ref[
-                low : low + 8, j * LANES : (j + 1) * LANES
-            ] * (-math.log2(math.e))
-    for n in (0, 1, 2):
-        fetches[n].wait()
     chunk = min(512, channels)
     for low in range(0, channels, chunk):
         cut = slice(low, low + chunk)
@@ -378,9 +384,6 @@
             rows = pl.ds(low // LANES + j, tokens, stride=groups)
             rates[rows, :] = rate[:, j * LANES : (j + 1) * LANES]
             drives[rows, :] = drive[:, j * LANES : (j + 1) * LANES]
-    fetches[5].wait()
-    for r in range(count):
-        send_tail(r).start()
     copy.wait()
 
     def segment(r, begin):
@@ -410,7 +413,6 @@
         return finish
 
     lax.fori_loop(0, count, segment, jnp.int32(0))
-    fetches[4].wait()
     for j in range(groups):
         cut = slice(j * LANES, (j + 1) * LANES)
         out_ref[:, cut] = (
@@ -422,37 +424,33 @@
         send_state(r).wait()
 
 
-def scan(plan, pieces, mixed, dt_weight, dt_bias, decay_rates, skip_gain, got, tails):
+def scan(plan, pieces, mixed, dt_weight, dt_bias, skip_gain, tails, decays, got):
     tokens, channels = mixed.shape
-    states = decay_rates.shape[0]
     groups = channels // LANES
+    state_rows = decays.shape[0]
     count = (plan.shape[0] - 1) // 3
-    brought = (mixed, dt_weight, dt_bias[None, :], decay_rates, skip_gain[None, :])
-    return pl.pallas_call(
-        functools.partial(scan_kernel, states, count),
-        in_specs=in_smem(1) + in_vmem(8) + in_hbm(7),
+    return pl.pallas_call(
+        functools.partial(scan_kernel, state_rows // groups, count),
+        in_specs=in_smem(1) + in_vmem(14) + [pl.BlockSpec(memory_space=pl.ANY)],
         out_specs=in_vmem(1) + in_hbm(1),
         out_shape=[
             jax.ShapeDtypeStruct((tokens, channels), BF),
             pltpu.HBM(got.shape, BF),
         ],
-        scratch_shapes=[VMEM(a.shape, a.dtype) for a in (*brought, tails)]
-        + [
+        scratch_shapes=[
             VMEM((tokens, dt_weight.shape[0]), BF),
             VMEM((tokens, LANES), F32),
             SMEM((tokens, LANES), F32),
             VMEM((tokens * groups, LANES), F32),
             VMEM((tokens * groups, LANES), F32),
             VMEM((tokens * groups, LANES), F32),
-            VMEM((states * groups, LANES), F32),
-            VMEM((count, states * groups, LANES), BF),
-            VMEM((count, states * groups, LANES), BF),
+            VMEM((count, state_rows, LANES), BF),
+            VMEM((count, state_rows, LANES), BF),
             pltpu.SemaphoreType.DMA,
             pltpu.SemaphoreType.DMA((count, 3)),
-            pltpu.SemaphoreType.DMA((6,)),
-        ],
-        compiler_params=params(32),
-    )(plan, *pieces, *pin(*brought, got, tails))
+        ],
+        compiler_params=params(24),
+    )(plan, *pieces, mixed, dt_weight, dt_bias, skip_gain, tails, decays, got)
 
 
 def attend_kernel(count, plan_ref, q_ref, k_ref, v_ref, got_ref, out_ref, rows_q, rows_o, prefix_ref, sems):
@@ -677,13 +675,15 @@
 
     conv_store = store_conv.transpose(1, 0, 2)
     tiles = entry_tiles(conv_store, store_state)
-    got = exchange(pick_tiles(asked, tiles, 3 * groups), "cache")
-
+    sent = pick_tiles(asked, tiles, 3 * groups)
     width = tokens + -(-3 * owner_count // LANES) * LANES
     choose = choose_matrix(lengths, hit_entry // slot_count, tokens, owner_count, width)
-    *parts, mixed, tails = conv_project(
-        plan, x_in, got, choose, conv_weight, dt_in_weight, bc_weight
+    x_rows, choose, taps, dt_in, bc_in, dt_out, bias, skip, decays = bring(
+        sent, decay_rates, x_in, choose, conv_weight, dt_in_weight, bc_weight, dt_weight,
+        dt_bias[None, :], skip_gain[None, :],
     )
+    got = exchange(sent, "cache")
+    *parts, mixed, tails = conv_project(plan, x_rows, choose, taps, dt_in, bc_in, got)
 
     def turned(step, value):
         return lax.ppermute(value, "tp", [(k, (k + step) % tp_count) for k in range(tp_count)])
@@ -693,10 +693,7 @@
     pieces = [summed] + [turned(step, summed) for step in range(1, tp_count)]
     got_prefix = exchange(pick(asked, *pin(store_keys, store_values)), "cache")
 
-    mixer_out, back = scan(
-        plan, pieces, mixed, dt_weight, dt_bias, decay_rates, skip_gain, got,
-        tails.reshape(owner_count, 3 * groups, LANES),
-    )
+    mixer_out, back = scan(plan, pieces, mixed, dt_out, bias, skip, tails, decays, got)
     back = exchange(back, "cache")
     attn_out = attend(plan, queries, new_keys, new_values, got_prefix)
     conv_rows, new_state = write_store(asked, store_state, conv_store, back)

time: 167 us -> 166 us (level)
  local copies, waits for them, and re-layouts: 3.19 us -> 0.21 us
  Pallas kernels: 47.8 us -> 49.7 us
    unnamed x12 -> x8, local copies, waits for them, and re-layouts: 3 us -> 0.02 us
    pallas_call x2 -> x3, Pallas kernels: 17.6 us -> 19.5 us  [the longest x1 14 us: scan(): pl.pallas_call(functools.partial(scan_kernel, state_rows // groups, count...]
  transfers between devices with their start and end apart: 18 -> 18, of which waited for: 7 -> 7; matrix products, arithmetic and copies ran while one was open for 1% -> 1% of each run, Pallas kernels for 24% -> 25%
where the time goes in v4:
time: 166 us; the launch traced here: 165 us
  starting transfers between devices  57.6 us (35%)
  waiting for transfers between devices  55.3 us (33%)
  Pallas kernels  49.7 us (30%)
    all_to_all x4, waiting for transfers between devices, exchange(): return lax.all_to_all(blocks, axis, split_axis=0, concat_axis=0, tiled=True)  49.5 us
    all_to_all x4, starting transfers between devices, exchange(): return lax.all_to_all(blocks, axis, split_axis=0, concat_axis=0, tiled=True)  30.2 us
    ppermute x14, starting transfers between devices, turned(): lax.ppermute(value, 'tp', [(k, (k + step) % tp_count) for k in range(tp_c...  27.4 us
    pallas_call x1, Pallas kernels, attend(): pl.pallas_call(functools.partial(attend_kernel, count), grid=(1,), in_spe...  14.1 us
    pallas_call x1, Pallas kernels, scan(): pl.pallas_call(functools.partial(scan_kernel, state_rows // groups, count...  14 us
    ppermute x14, waiting for transfers between devices, turned(): lax.ppermute(value, 'tp', [(k, (k + step) % tp_count) for k in range(tp_c...  5.83 us
    pallas_call x1, Pallas kernels, pick(): pl.pallas_call(functools.partial(pick_kernel, len(sources)), in_specs=in_...  4.22 us
    pallas_call x1, Pallas kernels, write_store(): pl.pallas_call(write_kernel, grid=(1,), in_specs=in_smem(1) + whole(conv_...  4.21 us
  transfers between devices with their start and end apart: 18, of which 7 were waited for; matrix products, arithmetic and copies ran while one was open for 1% of the time, Pallas kernels for 25%

profile of v4, /device:TPU:1, one launch (start us, length us, event | category | flops | bytes accessed | tf_op | source)
XLA Modules:
  0.0 165.2 jit_solution(8725733774830920293)
XLA Ops:
  0.6 1.4 shard_map.201
  2.1 8.6 %all-to-all-start = ((s32[32,1,128]{2,1,0:T(1,128)}), s32[32,1,128]{2,1,0:T(1,128)S(1)}, u32[]{:S(2)}, u32[]{:S(2)}) async-start(s32[32,1,128]{2,1,0:T(1,128)} %get-tuple-element.30), calls=%async_computation | async-start | bytes 32768 | tf_op jit(solution)/shard_map/all_to_all | solution.py:617
  10.7 4.0 %shard_map.202.tiles_ref = bf16[20,304,128]{2,1,0:T(8,128)(2,1)S(1)} custom-call(bf16[3,20,2048]{2,1,0:T(8,128)(2,1)} %bitcast.19, f32[20,16,2048]{2,1,0:T(8,128)} %store_ref.1), custom_call_target="tpu_custom_call" | custom-call | tf_op jit(solution)/shard_map/pallas_call | solution.py:108
  14.7 2.9 %all-to-all-done = s32[32,1,128]{2,1,0:T(1,128)S(1)} async-done(((s32[32,1,128]{2,1,0:T(1,128)}), s32[32,1,128]{2,1,0:T(1,128)S(1)}, u32[]{:S(2)}, u32[]{:S(2)}) %all-to-all-start) | async-done | bytes 16416 | tf_op jit(solution)/shard_map/all_to_all | solution.py:617
  17.6 2.2 %shard_map.203.after_ref = bf16[32,304,128]{2,1,0:T(8,128)(2,1)} custom-call(s32[32,128]{1,0:T(8,128)S(1)} %bitcast.16, bf16[20,304,128]{2,1,0:T(8,128)(2,1)S(1)} %shard_map.202.tiles_ref), custom_call_target="tpu_custom_call" | custom-call | tf_op jit(solution)/shard_map/pallas_call | solution.py:191
  19.7 4.6 %all-to-all-start.1 = ((bf16[32,304,128]{2,1,0:T(8,128)(2,1)}), bf16[32,304,128]{2,1,0:T(8,128)(2,1)S(1)}, u32[]{:S(2)}, u32[]{:S(2)}) async-start(bf16[32,304,128]{2,1,0:T(8,128)(2,1)} %shard_map.203.after_ref), calls=%async_computation.1 | async-start | bytes 4980736 | tf_op jit(solution)/shard_map/all_to_all | solution.py:617
  24.3 4.2 %shard_map.208 = bf16[32,512,128]{2,1,0:T(8,128)(2,1)} custom-call(s32[32,128]{1,0:T(8,128)S(1)} %bitcast.17, bf16[20,256,128]{2,1,0:T(8,128)(2,1)} %refs_0_.3, bf16[20,256,128]{2,1,0:T(8,128)(2,1)} %refs_1_.1), custom_call_target="tpu_custom_call" | custom-call | tf_op jit(solution)/shard_map/pallas_call | solution.py:156
  28.6 28.3 %all-to-all-done.1.got_ref.refs_14_ = bf16[32,304,128]{2,1,0:T(8,128)(2,1)S(1)} async-done(((bf16[32,304,128]{2,1,0:T(8,128)(2,1)}), bf16[32,304,128]{2,1,0:T(8,128)(2,1)S(1)}, u32[]{:S(2)}, u32[]{:S(2)}) %all-to-all-start.1) | async-done | bytes 2490400 | tf_op jit(solution)/shard_map/all_to_all | solution.py:617
  56.8 5.4 %all-to-all-start.2 = ((bf16[32,512,128]{2,1,0:T(8,128)(2,1)}), bf16[32,512,128]{2,1,0:T(8,128)(2,1)}, u32[]{:S(2)}, u32[]{:S(2)}) async-start(bf16[32,512,128]{2,1,0:T(8,128)(2,1)} %shard_map.208), calls=%async_computation.2 | async-start | bytes 8388608 | tf_op jit(solution)/shard_map/all_to_all | solution.py:617
  63.0 0.8 fusion.refs_1_
  63.8 2.6 %shard_map.204 = (bf16[128,2048]{1,0:T(8,128)(2,1)S(1)}, bf16[480,256]{1,0:T(8,128)(2,1)S(1)}, f32[4,2048]{1,0:T(4,128)S(1)}, bf16[2048,512]{1,0:T(8,128)(2,1)S(...) custom-call(bf16[32,304,128]{2,1,0:T(8,128)(2,1)} %shard_map.203.aft, ...), custom_call_target="tpu_custom_call" | custom-call | tf_op jit(solution)/shard_map/pallas_call | solution.py:223
  66.5 2.8 %shard_map.205 = (bf16[16,768]{1,0:T(8,128)(2,1)S(1)}, bf16[16,768]{1,0:T(8,128)(2,1)S(1)}, bf16[16,768]{1,0:T(8,128)(2,1)S(1)}, bf16[16,768]{1,0:T(8,128)(2,1)S...) custom-call(s32[49]{0:T(128)S(1)} %copy-done.1, ...), custom_call_target="tpu_custom_call" | custom-call | tf_op jit(solution)/shard_map/pallas_call | solution.py:289
  69.3 1.7 %collective-permute-start = (bf16[16,768]{1,0:T(8,128)(2,1)S(1)}, bf16[16,768]{1,0:T(8,128)(2,1)S(1)}, u32[]{:S(2)}, u32[]{:S(2)}) collective-permute-start(bf16[16,768]{1,0:T(8,128)(2,1)S(1)} %get-tuple-element.37), channel_id=1, source_target_pairs={{0,1},{1,2},{2,3},{3,4},{4,5},{5,6},{6,7},{7,0},{8,9},{9,10},{10,1... | collective-permute-start | bytes 73736 | tf_op jit(solution)/shard_map/ppermute | solution.py:689
  71.0 3.0 %collective-permute-start.1 = (bf16[16,768]{1,0:T(8,128)(2,1)S(1)}, bf16[16,768]{1,0:T(8,128)(2,1)S(1)}, u32[]{:S(2)}, u32[]{:S(2)}) collective-permute-start(bf16[16,768]{1,0:T(8,128)(2,1)S(1)} %get-tuple-element.38), channel_id=1, source_target_pairs={{0,2},{1,3},{2,4},{3,5},{4,6},{5,7},{6,0},{7,1},{8,10},{9,11},{10,... | collective-permute-start | bytes 73736 | tf_op jit(solution)/shard_map/ppermute | solution.py:689
  74.0 3.8 %collective-permute-start.2 = (bf16[16,768]{1,0:T(8,128)(2,1)S(1)}, bf16[16,768]{1,0:T(8,128)(2,1)S(1)}, u32[]{:S(2)}, u32[]{:S(2)}) collective-permute-start(bf16[16,768]{1,0:T(8,128)(2,1)S(1)} %get-tuple-element.39), channel_id=1, source_target_pairs={{0,3},{1,4},{2,5},{3,6},{4,7},{5,0},{6,1},{7,2},{8,11},{9,12},{10,... | collective-permute-start | bytes 73736 | tf_op jit(solution)/shard_map/ppermute | solution.py:689
  78.2 4.5 %collective-permute-start.4 = (bf16[16,768]{1,0:T(8,128)(2,1)S(1)}, bf16[16,768]{1,0:T(8,128)(2,1)S(1)}, u32[]{:S(2)}, u32[]{:S(2)}) collective-permute-start(bf16[16,768]{1,0:T(8,128)(2,1)S(1)} %get-tuple-element.41), channel_id=1, source_target_pairs={{0,5},{1,6},{2,7},{3,0},{4,1},{5,2},{6,3},{7,4},{8,13},{9,14},{10,... | collective-permute-start | bytes 73736 | tf_op jit(solution)/shard_map/ppermute | solution.py:689
  82.7 2.4 %collective-permute-start.5 = (bf16[16,768]{1,0:T(8,128)(2,1)S(1)}, bf16[16,768]{1,0:T(8,128)(2,1)S(1)}, u32[]{:S(2)}, u32[]{:S(2)}) collective-permute-start(bf16[16,768]{1,0:T(8,128)(2,1)S(1)} %get-tuple-element.42), channel_id=1, source_target_pairs={{0,6},{1,7},{2,0},{3,1},{4,2},{5,3},{6,4},{7,5},{8,14},{9,15},{10,... | collective-permute-start | bytes 73736 | tf_op jit(solution)/shard_map/ppermute | solution.py:689
  85.1 0.7 collective-permute-start.6
  85.8 1.8 %collective-permute-done.5.refs_6_ = bf16[16,768]{1,0:T(8,128)(2,1)S(1)} collective-permute-done((bf16[16,768]{1,0:T(8,128)(2,1)S(1)}, bf16[16,768]{1,0:T(8,128)(2,1)S(1)}, u32[]{:S(2)}, u32[]{:S(2)}) %collective-permute-start.5) | collective-permute-done | bytes 24608 | tf_op jit(solution)/shard_map/ppermute | solution.py:689
  87.6 0.6 collective-permute-done.6.refs_7_
  88.3 1.4 collective-permute-start.8
  89.7 3.6 %collective-permute-start.9 = (bf16[16,768]{1,0:T(8,128)(2,1)S(1)}, bf16[16,768]{1,0:T(8,128)(2,1)S(1)}, u32[]{:S(2)}, u32[]{:S(2)}) collective-permute-start(bf16[16,768]{1,0:T(8,128)(2,1)S(1)} %shard_map.206.refs_0_), channel_id=1, source_target_pairs={{0,3},{1,4},{2,5},{3,6},{4,7},{5,0},{6,1},{7,2},{8,11},{9,12},{10,... | collective-permute-start | bytes 73736 | tf_op jit(solution)/shard_map/ppermute | solution.py:689
  93.3 1.0 collective-permute-start.10
  94.3 3.7 %collective-permute-start.11 = (bf16[16,768]{1,0:T(8,128)(2,1)S(1)}, bf16[16,768]{1,0:T(8,128)(2,1)S(1)}, u32[]{:S(2)}, u32[]{:S(2)}) collective-permute-start(bf16[16,768]{1,0:T(8,128)(2,1)S(1)} %shard_map.206.refs_0_), channel_id=1, source_target_pairs={{0,5},{1,6},{2,7},{3,0},{4,1},{5,2},{6,3},{7,4},{8,13},{9,14},{10,... | collective-permute-start | bytes 73736 | tf_op jit(solution)/shard_map/ppermute | solution.py:689
  98.1 0.9 collective-permute-start.12
  99.1 1.3 collective-permute-done.10.refs_4_
  100.4 2.2 %collective-permute-done.12.refs_6_ = bf16[16,768]{1,0:T(8,128)(2,1)S(1)} collective-permute-done((bf16[16,768]{1,0:T(8,128)(2,1)S(1)}, bf16[16,768]{1,0:T(8,128)(2,1)S(1)}, u32[]{:S(2)}, u32[]{:S(2)}) %collective-permute-start.12) | collective-permute-done | bytes 24608 | tf_op jit(solution)/shard_map/ppermute | solution.py:689
  102.6 14.0 %shard_map.207 = (bf16[128,2048]{1,0:T(8,128)(2,1)}, bf16[32,304,128]{2,1,0:T(8,128)(2,1)}) custom-call(s32[49]{0:T(128)S(1)} %copy-done.1, bf16[16,768]{1,0:T(8,128)(2,1)S(1)} %shard_map.206.refs_0_, bf16[16,768]{1,0:T(8,128)(2,1)S(1)} %collective-permute-done.7.refs_1_, bf16[16,768]{1,0:T(8,128)(2,1)S(1)} %collective-permute-done.8.refs_2_, ...), custom_call_target="tpu_custom_call" | custom-call | tf_op jit(solution)/shard_map/pallas_call | solution.py:432
  116.6 11.7 %all-to-all-start.3 = ((bf16[32,304,128]{2,1,0:T(8,128)(2,1)}), bf16[32,304,128]{2,1,0:T(8,128)(2,1)S(1)}, u32[]{:S(2)}, u32[]{:S(2)}) async-start(bf16[32,304,128]{2,1,0:T(8,128)(2,1)} %get-tuple-element.51), calls=%async_computation.3 | async-start | bytes 4980736 | tf_op jit(solution)/shard_map/all_to_all | solution.py:617
  128.3 14.1 %shard_map.209 = bf16[128,512]{1,0:T(8,128)(2,1)} custom-call(s32[49]{0:T(128)} %get-tuple-element.29.plan_ref, bf16[128,512]{1,0:T(8,128)(2,1)} %q_ref.1, bf16[128,128]{1,0:T(8,128)(2,1)} %k_ref.1, bf16[128,128]{1,0:T(8,128)(2,1)} %v_ref.1, bf16[32,512,128]{2,1,0:T(8,128)(2,1)} %all-to-all-done.2.got_ref), custom_call_target="tpu_custom_call" | custom-call | tf_op jit(solution)/shard_map/pallas_call | solution.py:514
  142.5 18.4 %all-to-all-done.3.back_ref = bf16[32,304,128]{2,1,0:T(8,128)(2,1)S(1)} async-done(((bf16[32,304,128]{2,1,0:T(8,128)(2,1)}), bf16[32,304,128]{2,1,0:T(8,128)(2,1)S(1)}, u32[]{:S(2)}, u32[]{:S(2)}) %all-to-all-start.3) | async-done | bytes 2490400 | tf_op jit(solution)/shard_map/all_to_all | solution.py:617
  160.9 4.2 %shard_map.210 = (bf16[3,20,2048]{2,1,0:T(8,128)(2,1)}, f32[20,16,2048]{2,1,0:T(8,128)}) custom-call(s32[32,128]{1,0:T(8,128)S(1)} %bitcast.18, bf16[3,20,2048]{2,1,0:T(8,128)(2,1)} %bitcast.20, f32[20,16,2048]{2,1,0:T(8,128)} %store_ref.1, bf16[32,304,128]{2,1,0:T(8,128)(2,1)S(1)} %all-to-all-done.3.back_ref), custom_call_target="tpu_custom_call" | custom-call | tf_op jit(solution)/shard_map/pallas_call | solution.py:596
  (38 shorter events, 1.5 us)
Async XLA Ops:
  2.1 15.5 %all-to-all-start = ((s32[32,1,128]{2,1,0:T(1,128)}), s32[32,1,128]{2,1,0:T(1,128)S(1)}, u32[]{:S(2)}, u32[]{:S(2)}) async-start(s32[32,1,128]{2,1,0:T(1,128)} %get-tuple-element.30), calls=%async_computation | async-start | bytes 32768 | tf_op jit(solution)/shard_map/all_to_all | solution.py:617
  19.7 37.1 %all-to-all-start.1 = ((bf16[32,304,128]{2,1,0:T(8,128)(2,1)}), bf16[32,304,128]{2,1,0:T(8,128)(2,1)S(1)}, u32[]{:S(2)}, u32[]{:S(2)}) async-start(bf16[32,304,128]{2,1,0:T(8,128)(2,1)} %shard_map.203.after_ref), calls=%async_computation.1 | async-start | bytes 4980736 | tf_op jit(solution)/shard_map/all_to_all | solution.py:617
  28.5 33.7 %copy-start.2 = (s32[1,16]{1,0:T(1,128)S(1)}, s32[1,16]{1,0:T(1,128)}, u32[]{:S(2)}) copy-start(s32[1,16]{1,0:T(1,128)} %length_ref.1) | copy-start | bytes 196
  28.5 33.9 %copy-start.3 = (s32[16]{0:T(128)S(1)}, s32[16]{0:T(128)}, u32[]{:S(2)}) copy-start(s32[16]{0:T(128)} %entry_ref.1) | copy-start | bytes 196
  28.5 35.3 %copy-start = (f32[16,2048]{1,0:T(8,128)S(1)}, f32[16,2048]{1,0:T(8,128)}, u32[]{:S(2)}) copy-start(f32[16,2048]{1,0:T(8,128)} %refs_8_.1) | copy-start | bytes 393220
  56.8 59.8 %all-to-all-start.2 = ((bf16[32,512,128]{2,1,0:T(8,128)(2,1)}), bf16[32,512,128]{2,1,0:T(8,128)(2,1)}, u32[]{:S(2)}, u32[]{:S(2)}) async-start(bf16[32,512,128]{2,1,0:T(8,128)(2,1)} %shard_map.208), calls=%async_computation.2 | async-start | bytes 8388608 | tf_op jit(solution)/shard_map/all_to_all | solution.py:617
  63.8 2.6 %copy-start.1 = (s32[49]{0:T(128)S(1)}, s32[49]{0:T(128)}, u32[]{:S(2)}) copy-start(s32[49]{0:T(128)} %get-tuple-element.29.plan_ref) | copy-start | bytes 592
  69.3 13.4 %collective-permute-start = (bf16[16,768]{1,0:T(8,128)(2,1)S(1)}, bf16[16,768]{1,0:T(8,128)(2,1)S(1)}, u32[]{:S(2)}, u32[]{:S(2)}) collective-permute-start(bf16[16,768]{1,0:T(8,128)(2,1)S(1)} %get-tuple-element.37), channel_id=1, source_target_pairs={{0,1},{1,2},{2,3},{3,4},{4,5},{5,6},{6,7},{7,0},{8,9},{9,10},{10,1... | collective-permute-start | bytes 73736 | tf_op jit(solution)/shard_map/ppermute | solution.py:689
  71.0 14.1 %collective-permute-start.1 = (bf16[16,768]{1,0:T(8,128)(2,1)S(1)}, bf16[16,768]{1,0:T(8,128)(2,1)S(1)}, u32[]{:S(2)}, u32[]{:S(2)}) collective-permute-start(bf16[16,768]{1,0:T(8,128)(2,1)S(1)} %get-tuple-element.38), channel_id=1, source_target_pairs={{0,2},{1,3},{2,4},{3,5},{4,6},{5,7},{6,0},{7,1},{8,10},{9,11},{10,... | collective-permute-start | bytes 73736 | tf_op jit(solution)/shard_map/ppermute | solution.py:689
  74.0 11.8 %collective-permute-start.2 = (bf16[16,768]{1,0:T(8,128)(2,1)S(1)}, bf16[16,768]{1,0:T(8,128)(2,1)S(1)}, u32[]{:S(2)}, u32[]{:S(2)}) collective-permute-start(bf16[16,768]{1,0:T(8,128)(2,1)S(1)} %get-tuple-element.39), channel_id=1, source_target_pairs={{0,3},{1,4},{2,5},{3,6},{4,7},{5,0},{6,1},{7,2},{8,11},{9,12},{10,... | collective-permute-start | bytes 73736 | tf_op jit(solution)/shard_map/ppermute | solution.py:689
  77.8 8.1 %collective-permute-start.3 = (bf16[16,768]{1,0:T(8,128)(2,1)S(1)}, bf16[16,768]{1,0:T(8,128)(2,1)S(1)}, u32[]{:S(2)}, u32[]{:S(2)}) collective-permute-start(bf16[16,768]{1,0:T(8,128)(2,1)S(1)} %get-tuple-element.40), channel_id=1, source_target_pairs={{0,4},{1,5},{2,6},{3,7},{4,0},{5,1},{6,2},{7,3},{8,12},{9,13},{10,... | collective-permute-start | bytes 73736 | tf_op jit(solution)/shard_map/ppermute | solution.py:689
  78.2 7.6 %collective-permute-start.4 = (bf16[16,768]{1,0:T(8,128)(2,1)S(1)}, bf16[16,768]{1,0:T(8,128)(2,1)S(1)}, u32[]{:S(2)}, u32[]{:S(2)}) collective-permute-start(bf16[16,768]{1,0:T(8,128)(2,1)S(1)} %get-tuple-element.41), channel_id=1, source_target_pairs={{0,5},{1,6},{2,7},{3,0},{4,1},{5,2},{6,3},{7,4},{8,13},{9,14},{10,... | collective-permute-start | bytes 73736 | tf_op jit(solution)/shard_map/ppermute | solution.py:689
  82.7 4.9 %collective-permute-start.5 = (bf16[16,768]{1,0:T(8,128)(2,1)S(1)}, bf16[16,768]{1,0:T(8,128)(2,1)S(1)}, u32[]{:S(2)}, u32[]{:S(2)}) collective-permute-start(bf16[16,768]{1,0:T(8,128)(2,1)S(1)} %get-tuple-element.42), channel_id=1, source_target_pairs={{0,6},{1,7},{2,0},{3,1},{4,2},{5,3},{6,4},{7,5},{8,14},{9,15},{10,... | collective-permute-start | bytes 73736 | tf_op jit(solution)/shard_map/ppermute | solution.py:689
  85.1 3.1 %collective-permute-start.6 = (bf16[16,768]{1,0:T(8,128)(2,1)S(1)}, bf16[16,768]{1,0:T(8,128)(2,1)S(1)}, u32[]{:S(2)}, u32[]{:S(2)}) collective-permute-start(bf16[16,768]{1,0:T(8,128)(2,1)S(1)} %get-tuple-element.43), channel_id=1, source_target_pairs={{0,7},{1,0},{2,1},{3,2},{4,3},{5,4},{6,5},{7,6},{8,15},{9,8},{10,9... | collective-permute-start | bytes 73736 | tf_op jit(solution)/shard_map/ppermute | solution.py:689
  88.2 9.9 %collective-permute-start.7 = (bf16[16,768]{1,0:T(8,128)(2,1)S(1)}, bf16[16,768]{1,0:T(8,128)(2,1)S(1)}, u32[]{:S(2)}, u32[]{:S(2)}) collective-permute-start(bf16[16,768]{1,0:T(8,128)(2,1)S(1)} %shard_map.206.refs_0_), channel_id=1, source_target_pairs={{0,1},{1,2},{2,3},{3,4},{4,5},{5,6},{6,7},{7,0},{8,9},{9,10},{10,1... | collective-permute-start | bytes 73736 | tf_op jit(solution)/shard_map/ppermute | solution.py:689
  88.3 10.7 %collective-permute-start.8 = (bf16[16,768]{1,0:T(8,128)(2,1)S(1)}, bf16[16,768]{1,0:T(8,128)(2,1)S(1)}, u32[]{:S(2)}, u32[]{:S(2)}) collective-permute-start(bf16[16,768]{1,0:T(8,128)(2,1)S(1)} %shard_map.206.refs_0_), channel_id=1, source_target_pairs={{0,2},{1,3},{2,4},{3,5},{4,6},{5,7},{6,0},{7,1},{8,10},{9,11},{10,... | collective-permute-start | bytes 73736 | tf_op jit(solution)/shard_map/ppermute | solution.py:689
  89.7 9.4 %collective-permute-start.9 = (bf16[16,768]{1,0:T(8,128)(2,1)S(1)}, bf16[16,768]{1,0:T(8,128)(2,1)S(1)}, u32[]{:S(2)}, u32[]{:S(2)}) collective-permute-start(bf16[16,768]{1,0:T(8,128)(2,1)S(1)} %shard_map.206.refs_0_), channel_id=1, source_target_pairs={{0,3},{1,4},{2,5},{3,6},{4,7},{5,0},{6,1},{7,2},{8,11},{9,12},{10,... | collective-permute-start | bytes 73736 | tf_op jit(solution)/shard_map/ppermute | solution.py:689
  93.3 7.1 %collective-permute-start.10 = (bf16[16,768]{1,0:T(8,128)(2,1)S(1)}, bf16[16,768]{1,0:T(8,128)(2,1)S(1)}, u32[]{:S(2)}, u32[]{:S(2)}) collective-permute-start(bf16[16,768]{1,0:T(8,128)(2,1)S(1)} %shard_map.206.refs_0_), channel_id=1, source_target_pairs={{0,4},{1,5},{2,6},{3,7},{4,0},{5,1},{6,2},{7,3},{8,12},{9,13},{10,... | collective-permute-start | bytes 73736 | tf_op jit(solution)/shard_map/ppermute | solution.py:689
  94.3 6.1 %collective-permute-start.11 = (bf16[16,768]{1,0:T(8,128)(2,1)S(1)}, bf16[16,768]{1,0:T(8,128)(2,1)S(1)}, u32[]{:S(2)}, u32[]{:S(2)}) collective-permute-start(bf16[16,768]{1,0:T(8,128)(2,1)S(1)} %shard_map.206.refs_0_), channel_id=1, source_target_pairs={{0,5},{1,6},{2,7},{3,0},{4,1},{5,2},{6,3},{7,4},{8,13},{9,14},{10,... | collective-permute-start | bytes 73736 | tf_op jit(solution)/shard_map/ppermute | solution.py:689
  98.1 4.5 %collective-permute-start.12 = (bf16[16,768]{1,0:T(8,128)(2,1)S(1)}, bf16[16,768]{1,0:T(8,128)(2,1)S(1)}, u32[]{:S(2)}, u32[]{:S(2)}) collective-permute-start(bf16[16,768]{1,0:T(8,128)(2,1)S(1)} %shard_map.206.refs_0_), channel_id=1, source_target_pairs={{0,6},{1,7},{2,0},{3,1},{4,2},{5,3},{6,4},{7,5},{8,14},{9,15},{10,... | collective-permute-start | bytes 73736 | tf_op jit(solution)/shard_map/ppermute | solution.py:689
  99.0 3.6 %collective-permute-start.13 = (bf16[16,768]{1,0:T(8,128)(2,1)S(1)}, bf16[16,768]{1,0:T(8,128)(2,1)S(1)}, u32[]{:S(2)}, u32[]{:S(2)}) collective-permute-start(bf16[16,768]{1,0:T(8,128)(2,1)S(1)} %shard_map.206.refs_0_), channel_id=1, source_target_pairs={{0,7},{1,0},{2,1},{3,2},{4,3},{5,4},{6,5},{7,6},{8,15},{9,8},{10,9... | collective-permute-start | bytes 73736 | tf_op jit(solution)/shard_map/ppermute | solution.py:689
  116.6 44.2 %all-to-all-start.3 = ((bf16[32,304,128]{2,1,0:T(8,128)(2,1)}), bf16[32,304,128]{2,1,0:T(8,128)(2,1)S(1)}, u32[]{:S(2)}, u32[]{:S(2)}) async-start(bf16[32,304,128]{2,1,0:T(8,128)(2,1)} %get-tuple-element.51), calls=%async_computation.3 | async-start | bytes 4980736 | tf_op jit(solution)/shard_map/all_to_all | solution.py:617

commit v5 on v4

--- a/solution.py
+++ b/solution.py
@@ -118,7 +118,7 @@
 
 
 def pick_kernel(count, asked_ref, *refs):
-    sources, (out_ref, stage, sems) = refs[:count], refs[count:]
+    sources, (_, out_ref, stage, sems) = refs[:count], refs[count:]
     blocks = out_ref.shape[0]
     lows = [sum(s.shape[1] for s in sources[:n]) for n in range(count + 1)]
 
@@ -150,12 +150,12 @@
     each(lambda i, n: store(i, n).wait())
 
 
-def pick(asked, *sources):
+def pick(asked, after, *sources):
     blocks = asked.shape[0]
     rows = sum(s.shape[1] for s in sources)
     return pl.pallas_call(
         functools.partial(pick_kernel, len(sources)),
-        in_specs=in_smem(1) + in_hbm(len(sources)),
+        in_specs=in_smem(1) + in_hbm(len(sources)) + [pl.BlockSpec(memory_space=pl.ANY)],
         out_specs=in_hbm(1)[0],
         out_shape=pltpu.HBM((blocks, rows, LANES), BF),
         scratch_shapes=[
@@ -163,7 +163,7 @@
             pltpu.SemaphoreType.DMA((2, blocks, len(sources))),
         ],
         compiler_params=params(32),
-    )(asked, *sources)
+    )(asked, *sources, after)
 
 
 def pick_tiles_kernel(part, asked_ref, tiles_ref, out_ref, sems):
@@ -336,7 +336,7 @@
     pieces = refs[0:8]
     mixed_ref, weight_ref, bias_ref, skip_ref, tail_ref, decays, start_ref = refs[8:15]
     out_ref, back_ref = refs[15:17]
-    low_dt, maps, map_smem, rates, drives, sums, begun, ready, sem, sems = refs[17:]
+    low_dt, maps, turned, map_smem, rates, drives, sums, begun, ready, sem, sems = refs[17:]
     tokens, channels = mixed_ref.shape
     groups = channels // LANES
     share = tokens // 8
@@ -361,17 +361,17 @@
             ready.at[r], back_ref.at[plan_ref[r], pl.ds(conv_rows, state_rows)], sems.at[r, 2]
         )
 
-    for r in range(count):
-        receive(r).start()
-        send_tail(r).start()
     for step, piece in enumerate(pieces):
         place = pl.multiple_of(lax.rem(rank + 8 - step, 8) * share, share)
         low_dt[pl.ds(place, share), :] = piece[:, 0:rank_dim]
         maps[pl.ds(place, share), :] = piece[:, rank_dim : rank_dim + LANES].astype(F32) + piece[
             :, rank_dim + LANES :
         ].astype(F32)
-    copy = pltpu.make_async_copy(maps, map_smem, sem)
+    turned[...] = jnp.transpose(maps[...])[0 : 2 * states, :]
+    copy = pltpu.make_async_copy(turned, map_smem, sem)
     copy.start()
+    for r in range(count):
+        receive(r).start()
     chunk = min(512, channels)
     for low in range(0, channels, chunk):
         cut = slice(low, low + chunk)
@@ -399,8 +399,8 @@
             total, later = None, []
             for n in range(states):
                 decay = jnp.exp2(rate * decays[n * groups : (n + 1) * groups, :])
-                value = decay * held[n] + drive * map_smem[t, n]
-                term = value * map_smem[t, states + n]
+                value = decay * held[n] + drive * map_smem[n, t]
+                term = value * map_smem[states + n, t]
                 total = term if total is None else total + term
                 later.append(value)
             sums[place, :] = total
@@ -410,6 +410,7 @@
         for n in range(states):
             ready[r, n * groups : (n + 1) * groups, :] = held[n].astype(BF)
         send_state(r).start()
+        send_tail(r).start()
         return finish
 
     lax.fori_loop(0, count, segment, jnp.int32(0))
@@ -440,7 +441,8 @@
         scratch_shapes=[
             VMEM((tokens, dt_weight.shape[0]), BF),
             VMEM((tokens, LANES), F32),
-            SMEM((tokens, LANES), F32),
+            VMEM((2 * state_rows // groups, tokens), F32),
+            SMEM((2 * state_rows // groups, tokens), F32),
             VMEM((tokens * groups, LANES), F32),
             VMEM((tokens * groups, LANES), F32),
             VMEM((tokens * groups, LANES), F32),
@@ -691,7 +693,7 @@
     parts = [parts[0]] + [turned(step, parts[step]) for step in range(1, tp_count)]
     summed = sum_parts(parts)
     pieces = [summed] + [turned(step, summed) for step in range(1, tp_count)]
-    got_prefix = exchange(pick(asked, *pin(store_keys, store_values)), "cache")
+    got_prefix = exchange(pick(asked, bias, *pin(store_keys, store_values)), "cache")
 
     mixer_out, back = scan(plan, pieces, mixed, dt_out, bias, skip, tails, decays, got)
     back = exchange(back, "cache")

time: 166 us -> 163 us (0.982)
  waiting for transfers between devices: 55.3 us -> 48.1 us
  local copies, waits for them, and re-layouts: 0.21 us -> 7.16 us
  Pallas kernels: 49.7 us -> 47.9 us
    all_to_all x4, waiting for transfers between devices: 49.5 us -> 42.2 us  [exchange(): return lax.all_to_all(blocks, axis, split_axis=0, concat_axis=0, tiled=True)]
    unnamed x8 -> x24, local copies, waits for them, and re-layouts: 0.02 us -> 6.98 us
    pallas_call x1, Pallas kernels: 14 us -> 12.2 us  [scan(): pl.pallas_call(functools.partial(scan_kernel, state_rows // groups, count...]
  transfers between devices with their start and end apart: 18 -> 18, of which waited for: 7 -> 8; matrix products, arithmetic and copies ran while one was open for 1% -> 1% of each run, Pallas kernels for 25% -> 25%
where the time goes in v5:
time: 163 us; the launch traced here: 162 us
  starting transfers between devices  56.7 us (35%)
  waiting for transfers between devices  48.1 us (30%)
  Pallas kernels  47.9 us (29%)
  local copies, waits for them, and re-layouts  7.16 us (4%)
    all_to_all x4, waiting for transfers between devices, exchange(): return lax.all_to_all(blocks, axis, split_axis=0, concat_axis=0, tiled=True)  42.2 us
    all_to_all x4, starting transfers between devices, exchange(): return lax.all_to_all(blocks, axis, split_axis=0, concat_axis=0, tiled=True)  29.3 us
    ppermute x14, starting transfers between devices, turned(): lax.ppermute(value, 'tp', [(k, (k + step) % tp_count) for k in range(tp_c...  27.4 us
    pallas_call x1, Pallas kernels, attend(): pl.pallas_call(functools.partial(attend_kernel, count), grid=(1,), in_spe...  14.1 us
    pallas_call x1, Pallas kernels, scan(): pl.pallas_call(functools.partial(scan_kernel, state_rows // groups, count...  12.2 us
    unnamed x24, local copies, waits for them, and re-layouts  6.98 us
    ppermute x14, waiting for transfers between devices, turned(): lax.ppermute(value, 'tp', [(k, (k + step) % tp_count) for k in range(tp_c...  5.83 us
    pallas_call x1, Pallas kernels, pick(): pl.pallas_call(functools.partial(pick_kernel, len(sources)), in_specs=in_...  4.26 us
  transfers between devices with their start and end apart: 18, of which 8 were waited for; matrix products, arithmetic and copies ran while one was open for 1% of the time, Pallas kernels for 25%

profile of v5, /device:TPU:1, one launch (start us, length us, event | category | flops | bytes accessed | tf_op | source)
XLA Modules:
  0.0 162.2 jit_solution(6497829622987517514)
XLA Ops:
  0.6 1.4 shard_map.201
  2.1 8.6 %all-to-all-start = ((s32[32,1,128]{2,1,0:T(1,128)}), s32[32,1,128]{2,1,0:T(1,128)S(1)}, u32[]{:S(2)}, u32[]{:S(2)}) async-start(s32[32,1,128]{2,1,0:T(1,128)} %get-tuple-element.30), calls=%async_computation | async-start | bytes 32768 | tf_op jit(solution)/shard_map/all_to_all | solution.py:619
  10.7 4.0 %shard_map.202.tiles_ref = bf16[20,304,128]{2,1,0:T(8,128)(2,1)S(1)} custom-call(bf16[3,20,2048]{2,1,0:T(8,128)(2,1)} %bitcast.19, f32[20,16,2048]{2,1,0:T(8,128)} %store_ref.1), custom_call_target="tpu_custom_call" | custom-call | tf_op jit(solution)/shard_map/pallas_call | solution.py:108
  14.7 2.9 %all-to-all-done = s32[32,1,128]{2,1,0:T(1,128)S(1)} async-done(((s32[32,1,128]{2,1,0:T(1,128)}), s32[32,1,128]{2,1,0:T(1,128)S(1)}, u32[]{:S(2)}, u32[]{:S(2)}) %all-to-all-start) | async-done | bytes 16416 | tf_op jit(solution)/shard_map/all_to_all | solution.py:619
  17.6 2.2 %shard_map.203.after_ref = bf16[32,304,128]{2,1,0:T(8,128)(2,1)} custom-call(s32[32,128]{1,0:T(8,128)S(1)} %bitcast.16, bf16[20,304,128]{2,1,0:T(8,128)(2,1)S(1)} %shard_map.202.tiles_ref), custom_call_target="tpu_custom_call" | custom-call | tf_op jit(solution)/shard_map/pallas_call | solution.py:191
  19.8 4.7 %all-to-all-start.1 = ((bf16[32,304,128]{2,1,0:T(8,128)(2,1)}), bf16[32,304,128]{2,1,0:T(8,128)(2,1)S(1)}, u32[]{:S(2)}, u32[]{:S(2)}) async-start(bf16[32,304,128]{2,1,0:T(8,128)(2,1)} %shard_map.203.after_ref), calls=%async_computation.1 | async-start | bytes 4980736 | tf_op jit(solution)/shard_map/all_to_all | solution.py:619
  26.1 2.6 %shard_map.204 = (bf16[128,2048]{1,0:T(8,128)(2,1)S(1)}, bf16[480,256]{1,0:T(8,128)(2,1)S(1)}, f32[4,2048]{1,0:T(4,128)S(1)}, bf16[2048,512]{1,0:T(8,128)(2,1)S(...) custom-call(bf16[32,304,128]{2,1,0:T(8,128)(2,1)} %shard_map.203.aft, ...), custom_call_target="tpu_custom_call" | custom-call | tf_op jit(solution)/shard_map/pallas_call | solution.py:223
  28.7 1.4 copy-done
  30.1 1.3 copy-done.2
  32.7 4.3 %shard_map.208 = bf16[32,512,128]{2,1,0:T(8,128)(2,1)} custom-call(s32[32,128]{1,0:T(8,128)S(1)} %bitcast.17, bf16[20,256,128]{2,1,0:T(8,128)(2,1)} %refs_0_.3, bf16[20,256,128]{2,1,0:T(8,128)(2,1)} %refs_1_.1, f32[1,2048]{1,0:T(1,128)S(1)} %get-tuple-element.46.refs_10_.refs_2_), custom_call_target="tpu_custom_call" | custom-call | tf_op jit(solution)/shard_map/pallas_call | solution.py:156
  37.0 20.0 %all-to-all-done.1.got_ref.refs_14_ = bf16[32,304,128]{2,1,0:T(8,128)(2,1)S(1)} async-done(((bf16[32,304,128]{2,1,0:T(8,128)(2,1)}), bf16[32,304,128]{2,1,0:T(8,128)(2,1)S(1)}, u32[]{:S(2)}, u32[]{:S(2)}) %all-to-all-start.1) | async-done | bytes 2490400 | tf_op jit(solution)/shard_map/all_to_all | solution.py:619
  57.0 5.4 %all-to-all-start.2 = ((bf16[32,512,128]{2,1,0:T(8,128)(2,1)}), bf16[32,512,128]{2,1,0:T(8,128)(2,1)}, u32[]{:S(2)}, u32[]{:S(2)}) async-start(bf16[32,512,128]{2,1,0:T(8,128)(2,1)} %shard_map.208), calls=%async_computation.2 | async-start | bytes 8388608 | tf_op jit(solution)/shard_map/all_to_all | solution.py:619
  62.4 1.6 copy-done.3
  65.3 2.8 %shard_map.205 = (bf16[16,768]{1,0:T(8,128)(2,1)S(1)}, bf16[16,768]{1,0:T(8,128)(2,1)S(1)}, bf16[16,768]{1,0:T(8,128)(2,1)S(1)}, bf16[16,768]{1,0:T(8,128)(2,1)S...) custom-call(s32[49]{0:T(128)S(1)} %copy-done.9, ...), custom_call_target="tpu_custom_call" | custom-call | tf_op jit(solution)/shard_map/pallas_call | solution.py:289
  68.1 1.7 %collective-permute-start = (bf16[16,768]{1,0:T(8,128)(2,1)S(1)}, bf16[16,768]{1,0:T(8,128)(2,1)S(1)}, u32[]{:S(2)}, u32[]{:S(2)}) collective-permute-start(bf16[16,768]{1,0:T(8,128)(2,1)S(1)} %get-tuple-element.37), channel_id=1, source_target_pairs={{0,1},{1,2},{2,3},{3,4},{4,5},{5,6},{6,7},{7,0},{8,9},{9,10},{10,1... | collective-permute-start | bytes 73736 | tf_op jit(solution)/shard_map/ppermute | solution.py:691
  69.8 3.0 %collective-permute-start.1 = (bf16[16,768]{1,0:T(8,128)(2,1)S(1)}, bf16[16,768]{1,0:T(8,128)(2,1)S(1)}, u32[]{:S(2)}, u32[]{:S(2)}) collective-permute-start(bf16[16,768]{1,0:T(8,128)(2,1)S(1)} %get-tuple-element.38), channel_id=1, source_target_pairs={{0,2},{1,3},{2,4},{3,5},{4,6},{5,7},{6,0},{7,1},{8,10},{9,11},{10,... | collective-permute-start | bytes 73736 | tf_op jit(solution)/shard_map/ppermute | solution.py:691
  72.8 3.8 %collective-permute-start.2 = (bf16[16,768]{1,0:T(8,128)(2,1)S(1)}, bf16[16,768]{1,0:T(8,128)(2,1)S(1)}, u32[]{:S(2)}, u32[]{:S(2)}) collective-permute-start(bf16[16,768]{1,0:T(8,128)(2,1)S(1)} %get-tuple-element.39), channel_id=1, source_target_pairs={{0,3},{1,4},{2,5},{3,6},{4,7},{5,0},{6,1},{7,2},{8,11},{9,12},{10,... | collective-permute-start | bytes 73736 | tf_op jit(solution)/shard_map/ppermute | solution.py:691
  77.0 4.5 %collective-permute-start.4 = (bf16[16,768]{1,0:T(8,128)(2,1)S(1)}, bf16[16,768]{1,0:T(8,128)(2,1)S(1)}, u32[]{:S(2)}, u32[]{:S(2)}) collective-permute-start(bf16[16,768]{1,0:T(8,128)(2,1)S(1)} %get-tuple-element.41), channel_id=1, source_target_pairs={{0,5},{1,6},{2,7},{3,0},{4,1},{5,2},{6,3},{7,4},{8,13},{9,14},{10,... | collective-permute-start | bytes 73736 | tf_op jit(solution)/shard_map/ppermute | solution.py:691
  81.5 2.4 %collective-permute-start.5 = (bf16[16,768]{1,0:T(8,128)(2,1)S(1)}, bf16[16,768]{1,0:T(8,128)(2,1)S(1)}, u32[]{:S(2)}, u32[]{:S(2)}) collective-permute-start(bf16[16,768]{1,0:T(8,128)(2,1)S(1)} %get-tuple-element.42), channel_id=1, source_target_pairs={{0,6},{1,7},{2,0},{3,1},{4,2},{5,3},{6,4},{7,5},{8,14},{9,15},{10,... | collective-permute-start | bytes 73736 | tf_op jit(solution)/shard_map/ppermute | solution.py:691
  84.6 1.8 %collective-permute-done.5.refs_6_ = bf16[16,768]{1,0:T(8,128)(2,1)S(1)} collective-permute-done((bf16[16,768]{1,0:T(8,128)(2,1)S(1)}, bf16[16,768]{1,0:T(8,128)(2,1)S(1)}, u32[]{:S(2)}, u32[]{:S(2)}) %collective-permute-start.5) | collective-permute-done | bytes 24608 | tf_op jit(solution)/shard_map/ppermute | solution.py:691
  87.1 1.4 collective-permute-start.8
  88.5 3.6 %collective-permute-start.9 = (bf16[16,768]{1,0:T(8,128)(2,1)S(1)}, bf16[16,768]{1,0:T(8,128)(2,1)S(1)}, u32[]{:S(2)}, u32[]{:S(2)}) collective-permute-start(bf16[16,768]{1,0:T(8,128)(2,1)S(1)} %shard_map.206.refs_0_), channel_id=1, source_target_pairs={{0,3},{1,4},{2,5},{3,6},{4,7},{5,0},{6,1},{7,2},{8,11},{9,12},{10,... | collective-permute-start | bytes 73736 | tf_op jit(solution)/shard_map/ppermute | solution.py:691
  92.1 1.0 collective-permute-start.10
  93.2 3.7 %collective-permute-start.11 = (bf16[16,768]{1,0:T(8,128)(2,1)S(1)}, bf16[16,768]{1,0:T(8,128)(2,1)S(1)}, u32[]{:S(2)}, u32[]{:S(2)}) collective-permute-start(bf16[16,768]{1,0:T(8,128)(2,1)S(1)} %shard_map.206.refs_0_), channel_id=1, source_target_pairs={{0,5},{1,6},{2,7},{3,0},{4,1},{5,2},{6,3},{7,4},{8,13},{9,14},{10,... | collective-permute-start | bytes 73736 | tf_op jit(solution)/shard_map/ppermute | solution.py:691
  97.9 1.3 collective-permute-done.10.refs_4_
  99.2 2.2 %collective-permute-done.12.refs_6_ = bf16[16,768]{1,0:T(8,128)(2,1)S(1)} collective-permute-done((bf16[16,768]{1,0:T(8,128)(2,1)S(1)}, bf16[16,768]{1,0:T(8,128)(2,1)S(1)}, u32[]{:S(2)}, u32[]{:S(2)}) %collective-permute-start.12) | collective-permute-done | bytes 24608 | tf_op jit(solution)/shard_map/ppermute | solution.py:691
  101.4 12.2 %shard_map.207 = (bf16[128,2048]{1,0:T(8,128)(2,1)}, bf16[32,304,128]{2,1,0:T(8,128)(2,1)}) custom-call(s32[49]{0:T(128)S(1)} %copy-done.9, bf16[16,768]{1,0:T(8,128)(2,1)S(1)} %shard_map.206.refs_0_, bf16[16,768]{1,0:T(8,128)(2,1)S(1)} %collective-permute-done.7.refs_1_, bf16[16,768]{1,0:T(8,128)(2,1)S(1)} %collective-permute-done.8.refs_2_, ...), custom_call_target="tpu_custom_call" | custom-call | tf_op jit(solution)/shard_map/pallas_call | solution.py:433
  113.6 1.0 all-to-all-done.2.got_ref
  114.6 10.7 %all-to-all-start.3 = ((bf16[32,304,128]{2,1,0:T(8,128)(2,1)}), bf16[32,304,128]{2,1,0:T(8,128)(2,1)S(1)}, u32[]{:S(2)}, u32[]{:S(2)}) async-start(bf16[32,304,128]{2,1,0:T(8,128)(2,1)} %get-tuple-element.51), calls=%async_computation.3 | async-start | bytes 4980736 | tf_op jit(solution)/shard_map/all_to_all | solution.py:619
  125.3 14.1 %shard_map.209 = bf16[128,512]{1,0:T(8,128)(2,1)} custom-call(s32[49]{0:T(128)} %get-tuple-element.29.plan_ref, bf16[128,512]{1,0:T(8,128)(2,1)} %q_ref.1, bf16[128,128]{1,0:T(8,128)(2,1)} %k_ref.1, bf16[128,128]{1,0:T(8,128)(2,1)} %v_ref.1, bf16[32,512,128]{2,1,0:T(8,128)(2,1)} %all-to-all-done.2.got_ref), custom_call_target="tpu_custom_call" | custom-call | tf_op jit(solution)/shard_map/pallas_call | solution.py:516
  139.5 18.4 %all-to-all-done.3.back_ref = bf16[32,304,128]{2,1,0:T(8,128)(2,1)S(1)} async-done(((bf16[32,304,128]{2,1,0:T(8,128)(2,1)}), bf16[32,304,128]{2,1,0:T(8,128)(2,1)S(1)}, u32[]{:S(2)}, u32[]{:S(2)}) %all-to-all-start.3) | async-done | bytes 2490400 | tf_op jit(solution)/shard_map/all_to_all | solution.py:619
  157.9 4.2 %shard_map.210 = (bf16[3,20,2048]{2,1,0:T(8,128)(2,1)}, f32[20,16,2048]{2,1,0:T(8,128)}) custom-call(s32[32,128]{1,0:T(8,128)S(1)} %bitcast.18, bf16[3,20,2048]{2,1,0:T(8,128)(2,1)} %bitcast.20, f32[20,16,2048]{2,1,0:T(8,128)} %store_ref.1, bf16[32,304,128]{2,1,0:T(8,128)(2,1)S(1)} %all-to-all-done.3.back_ref), custom_call_target="tpu_custom_call" | custom-call | tf_op jit(solution)/shard_map/pallas_call | solution.py:598
  (54 shorter events, 7.1 us)
Async XLA Ops:
  2.1 15.5 %all-to-all-start = ((s32[32,1,128]{2,1,0:T(1,128)}), s32[32,1,128]{2,1,0:T(1,128)S(1)}, u32[]{:S(2)}, u32[]{:S(2)}) async-start(s32[32,1,128]{2,1,0:T(1,128)} %get-tuple-element.30), calls=%async_computation | async-start | bytes 32768 | tf_op jit(solution)/shard_map/all_to_all | solution.py:619
  19.7 4.7 %copy-start.10 = (s32[1,16]{1,0:T(1,128)S(1)}, s32[1,16]{1,0:T(1,128)}, u32[]{:S(2)}) copy-start(s32[1,16]{1,0:T(1,128)} %length_ref.1) | copy-start | bytes 196
  19.7 5.0 %copy-start.11 = (s32[16]{0:T(128)S(1)}, s32[16]{0:T(128)}, u32[]{:S(2)}) copy-start(s32[16]{0:T(128)} %entry_ref.1) | copy-start | bytes 196
  19.8 6.3 %copy-start.4 = (f32[16,2048]{1,0:T(8,128)S(1)}, f32[16,2048]{1,0:T(8,128)}, u32[]{:S(2)}) copy-start(f32[16,2048]{1,0:T(8,128)} %refs_8_.1) | copy-start | bytes 393220
  19.8 37.2 %all-to-all-start.1 = ((bf16[32,304,128]{2,1,0:T(8,128)(2,1)}), bf16[32,304,128]{2,1,0:T(8,128)(2,1)S(1)}, u32[]{:S(2)}, u32[]{:S(2)}) async-start(bf16[32,304,128]{2,1,0:T(8,128)(2,1)} %shard_map.203.after_ref), calls=%async_computation.1 | async-start | bytes 4980736 | tf_op jit(solution)/shard_map/all_to_all | solution.py:619
  28.7 1.4 copy-start
  30.1 1.3 copy-start.2
  31.4 0.7 copy-start.5
  32.1 0.6 copy-start.7
  37.0 25.4 %copy-start.6 = (bf16[32,2048]{1,0:T(8,128)(2,1)S(1)}, bf16[32,2048]{1,0:T(8,128)(2,1)}, u32[]{:S(2)}) copy-start(bf16[32,2048]{1,0:T(8,128)(2,1)} %copy-done.5) | copy-start | bytes 393220
  57.0 57.7 %all-to-all-start.2 = ((bf16[32,512,128]{2,1,0:T(8,128)(2,1)}), bf16[32,512,128]{2,1,0:T(8,128)(2,1)}, u32[]{:S(2)}, u32[]{:S(2)}) async-start(bf16[32,512,128]{2,1,0:T(8,128)(2,1)} %shard_map.208), calls=%async_computation.2 | async-start | bytes 8388608 | tf_op jit(solution)/shard_map/all_to_all | solution.py:619
  62.4 1.6 copy-start.3
  64.0 0.8 copy-start.8
  64.7 0.6 copy-start.9
  65.3 36.1 %copy-start.1 = (bf16[512,2048]{1,0:T(8,128)(2,1)S(1)}, bf16[512,2048]{1,0:T(8,128)(2,1)}, u32[]{:S(2)}) copy-start(bf16[512,2048]{1,0:T(8,128)(2,1)} %copy-done) | copy-start | bytes 6291460
  68.1 13.4 %collective-permute-start = (bf16[16,768]{1,0:T(8,128)(2,1)S(1)}, bf16[16,768]{1,0:T(8,128)(2,1)S(1)}, u32[]{:S(2)}, u32[]{:S(2)}) collective-permute-start(bf16[16,768]{1,0:T(8,128)(2,1)S(1)} %get-tuple-element.37), channel_id=1, source_target_pairs={{0,1},{1,2},{2,3},{3,4},{4,5},{5,6},{6,7},{7,0},{8,9},{9,10},{10,1... | collective-permute-start | bytes 73736 | tf_op jit(solution)/shard_map/ppermute | solution.py:691
  69.8 14.1 %collective-permute-start.1 = (bf16[16,768]{1,0:T(8,128)(2,1)S(1)}, bf16[16,768]{1,0:T(8,128)(2,1)S(1)}, u32[]{:S(2)}, u32[]{:S(2)}) collective-permute-start(bf16[16,768]{1,0:T(8,128)(2,1)S(1)} %get-tuple-element.38), channel_id=1, source_target_pairs={{0,2},{1,3},{2,4},{3,5},{4,6},{5,7},{6,0},{7,1},{8,10},{9,11},{10,... | collective-permute-start | bytes 73736 | tf_op jit(solution)/shard_map/ppermute | solution.py:691
  72.8 11.8 %collective-permute-start.2 = (bf16[16,768]{1,0:T(8,128)(2,1)S(1)}, bf16[16,768]{1,0:T(8,128)(2,1)S(1)}, u32[]{:S(2)}, u32[]{:S(2)}) collective-permute-start(bf16[16,768]{1,0:T(8,128)(2,1)S(1)} %get-tuple-element.39), channel_id=1, source_target_pairs={{0,3},{1,4},{2,5},{3,6},{4,7},{5,0},{6,1},{7,2},{8,11},{9,12},{10,... | collective-permute-start | bytes 73736 | tf_op jit(solution)/shard_map/ppermute | solution.py:691
  76.6 8.0 %collective-permute-start.3 = (bf16[16,768]{1,0:T(8,128)(2,1)S(1)}, bf16[16,768]{1,0:T(8,128)(2,1)S(1)}, u32[]{:S(2)}, u32[]{:S(2)}) collective-permute-start(bf16[16,768]{1,0:T(8,128)(2,1)S(1)} %get-tuple-element.40), channel_id=1, source_target_pairs={{0,4},{1,5},{2,6},{3,7},{4,0},{5,1},{6,2},{7,3},{8,12},{9,13},{10,... | collective-permute-start | bytes 73736 | tf_op jit(solution)/shard_map/ppermute | solution.py:691
  77.0 7.6 %collective-permute-start.4 = (bf16[16,768]{1,0:T(8,128)(2,1)S(1)}, bf16[16,768]{1,0:T(8,128)(2,1)S(1)}, u32[]{:S(2)}, u32[]{:S(2)}) collective-permute-start(bf16[16,768]{1,0:T(8,128)(2,1)S(1)} %get-tuple-element.41), channel_id=1, source_target_pairs={{0,5},{1,6},{2,7},{3,0},{4,1},{5,2},{6,3},{7,4},{8,13},{9,14},{10,... | collective-permute-start | bytes 73736 | tf_op jit(solution)/shard_map/ppermute | solution.py:691
  81.5 4.9 %collective-permute-start.5 = (bf16[16,768]{1,0:T(8,128)(2,1)S(1)}, bf16[16,768]{1,0:T(8,128)(2,1)S(1)}, u32[]{:S(2)}, u32[]{:S(2)}) collective-permute-start(bf16[16,768]{1,0:T(8,128)(2,1)S(1)} %get-tuple-element.42), channel_id=1, source_target_pairs={{0,6},{1,7},{2,0},{3,1},{4,2},{5,3},{6,4},{7,5},{8,14},{9,15},{10,... | collective-permute-start | bytes 73736 | tf_op jit(solution)/shard_map/ppermute | solution.py:691
  83.9 3.1 %collective-permute-start.6 = (bf16[16,768]{1,0:T(8,128)(2,1)S(1)}, bf16[16,768]{1,0:T(8,128)(2,1)S(1)}, u32[]{:S(2)}, u32[]{:S(2)}) collective-permute-start(bf16[16,768]{1,0:T(8,128)(2,1)S(1)} %get-tuple-element.43), channel_id=1, source_target_pairs={{0,7},{1,0},{2,1},{3,2},{4,3},{5,4},{6,5},{7,6},{8,15},{9,8},{10,9... | collective-permute-start | bytes 73736 | tf_op jit(solution)/shard_map/ppermute | solution.py:691
  87.0 9.9 %collective-permute-start.7 = (bf16[16,768]{1,0:T(8,128)(2,1)S(1)}, bf16[16,768]{1,0:T(8,128)(2,1)S(1)}, u32[]{:S(2)}, u32[]{:S(2)}) collective-permute-start(bf16[16,768]{1,0:T(8,128)(2,1)S(1)} %shard_map.206.refs_0_), channel_id=1, source_target_pairs={{0,1},{1,2},{2,3},{3,4},{4,5},{5,6},{6,7},{7,0},{8,9},{9,10},{10,1... | collective-permute-start | bytes 73736 | tf_op jit(solution)/shard_map/ppermute | solution.py:691
  87.1 10.7 %collective-permute-start.8 = (bf16[16,768]{1,0:T(8,128)(2,1)S(1)}, bf16[16,768]{1,0:T(8,128)(2,1)S(1)}, u32[]{:S(2)}, u32[]{:S(2)}) collective-permute-start(bf16[16,768]{1,0:T(8,128)(2,1)S(1)} %shard_map.206.refs_0_), channel_id=1, source_target_pairs={{0,2},{1,3},{2,4},{3,5},{4,6},{5,7},{6,0},{7,1},{8,10},{9,11},{10,... | collective-permute-start | bytes 73736 | tf_op jit(solution)/shard_map/ppermute | solution.py:691
  88.5 9.4 %collective-permute-start.9 = (bf16[16,768]{1,0:T(8,128)(2,1)S(1)}, bf16[16,768]{1,0:T(8,128)(2,1)S(1)}, u32[]{:S(2)}, u32[]{:S(2)}) collective-permute-start(bf16[16,768]{1,0:T(8,128)(2,1)S(1)} %shard_map.206.refs_0_), channel_id=1, source_target_pairs={{0,3},{1,4},{2,5},{3,6},{4,7},{5,0},{6,1},{7,2},{8,11},{9,12},{10,... | collective-permute-start | bytes 73736 | tf_op jit(solution)/shard_map/ppermute | solution.py:691
  92.1 7.1 %collective-permute-start.10 = (bf16[16,768]{1,0:T(8,128)(2,1)S(1)}, bf16[16,768]{1,0:T(8,128)(2,1)S(1)}, u32[]{:S(2)}, u32[]{:S(2)}) collective-permute-start(bf16[16,768]{1,0:T(8,128)(2,1)S(1)} %shard_map.206.refs_0_), channel_id=1, source_target_pairs={{0,4},{1,5},{2,6},{3,7},{4,0},{5,1},{6,2},{7,3},{8,12},{9,13},{10,... | collective-permute-start | bytes 73736 | tf_op jit(solution)/shard_map/ppermute | solution.py:691
  93.2 6.1 %collective-permute-start.11 = (bf16[16,768]{1,0:T(8,128)(2,1)S(1)}, bf16[16,768]{1,0:T(8,128)(2,1)S(1)}, u32[]{:S(2)}, u32[]{:S(2)}) collective-permute-start(bf16[16,768]{1,0:T(8,128)(2,1)S(1)} %shard_map.206.refs_0_), channel_id=1, source_target_pairs={{0,5},{1,6},{2,7},{3,0},{4,1},{5,2},{6,3},{7,4},{8,13},{9,14},{10,... | collective-permute-start | bytes 73736 | tf_op jit(solution)/shard_map/ppermute | solution.py:691
  96.9 4.5 %collective-permute-start.12 = (bf16[16,768]{1,0:T(8,128)(2,1)S(1)}, bf16[16,768]{1,0:T(8,128)(2,1)S(1)}, u32[]{:S(2)}, u32[]{:S(2)}) collective-permute-start(bf16[16,768]{1,0:T(8,128)(2,1)S(1)} %shard_map.206.refs_0_), channel_id=1, source_target_pairs={{0,6},{1,7},{2,0},{3,1},{4,2},{5,3},{6,4},{7,5},{8,14},{9,15},{10,... | collective-permute-start | bytes 73736 | tf_op jit(solution)/shard_map/ppermute | solution.py:691
  97.8 3.6 %collective-permute-start.13 = (bf16[16,768]{1,0:T(8,128)(2,1)S(1)}, bf16[16,768]{1,0:T(8,128)(2,1)S(1)}, u32[]{:S(2)}, u32[]{:S(2)}) collective-permute-start(bf16[16,768]{1,0:T(8,128)(2,1)S(1)} %shard_map.206.refs_0_), channel_id=1, source_target_pairs={{0,7},{1,0},{2,1},{3,2},{4,3},{5,4},{6,5},{7,6},{8,15},{9,8},{10,9... | collective-permute-start | bytes 73736 | tf_op jit(solution)/shard_map/ppermute | solution.py:691
  114.6 43.2 %all-to-all-start.3 = ((bf16[32,304,128]{2,1,0:T(8,128)(2,1)}), bf16[32,304,128]{2,1,0:T(8,128)(2,1)S(1)}, u32[]{:S(2)}, u32[]{:S(2)}) async-start(bf16[32,304,128]{2,1,0:T(8,128)(2,1)} %get-tuple-element.51), calls=%async_computation.3 | async-start | bytes 4980736 | tf_op jit(solution)/shard_map/all_to_all | solution.py:619

commit v6 on v5

--- a/solution.py
+++ b/solution.py
@@ -113,7 +113,7 @@
         out_specs=pl.BlockSpec((step, tail_rows + rows, LANES), lambda i: (i, 0, 0)),
         out_shape=jax.ShapeDtypeStruct((slots, tail_rows + rows, LANES), BF),
         scratch_shapes=[VMEM((rows, LANES), F32), VMEM((slots * tail_rows, LANES), F32)],
-        compiler_params=params(16),
+        compiler_params=params(8),
     )(*pin(conv_rows, store_state))
 
 
@@ -162,7 +162,7 @@
             VMEM((blocks, rows, LANES), BF),
             pltpu.SemaphoreType.DMA((2, blocks, len(sources))),
         ],
-        compiler_params=params(32),
+        compiler_params=params(6),
     )(asked, *sources, after)
 
 

time: 163 us -> 163 us (level)
  no operation moved by 1% of the time
where the time goes in v6:
time: 163 us; the launch traced here: 162 us
  starting transfers between devices  56.7 us (35%)
  waiting for transfers between devices  48.1 us (30%)
  Pallas kernels  47.9 us (29%)
  local copies, waits for them, and re-layouts  7.16 us (4%)
    all_to_all x4, waiting for transfers between devices, exchange(): return lax.all_to_all(blocks, axis, split_axis=0, concat_axis=0, tiled=True)  42.2 us
    all_to_all x4, starting transfers between devices, exchange(): return lax.all_to_all(blocks, axis, split_axis=0, concat_axis=0, tiled=True)  29.3 us
    ppermute x14, starting transfers between devices, turned(): lax.ppermute(value, 'tp', [(k, (k + step) % tp_count) for k in range(tp_c...  27.4 us
    pallas_call x1, Pallas kernels, attend(): pl.pallas_call(functools.partial(attend_kernel, count), grid=(1,), in_spe...  14.1 us
    pallas_call x1, Pallas kernels, scan(): pl.pallas_call(functools.partial(scan_kernel, state_rows // groups, count...  12.2 us
    unnamed x24, local copies, waits for them, and re-layouts  6.98 us
    ppermute x14, waiting for transfers between devices, turned(): lax.ppermute(value, 'tp', [(k, (k + step) % tp_count) for k in range(tp_c...  5.83 us
    pallas_call x1, Pallas kernels, pick(): pl.pallas_call(functools.partial(pick_kernel, len(sources)), in_specs=in_...  4.27 us
  transfers between devices with their start and end apart: 18, of which 8 were waited for; matrix products, arithmetic and copies ran while one was open for 1% of the time, Pallas kernels for 25%

profile of v6, /device:TPU:1, one launch (start us, length us, event | category | flops | bytes accessed | tf_op | source)
XLA Modules:
  0.0 162.2 jit_solution(6497829622987517514)
XLA Ops:
  0.6 1.4 shard_map.201
  2.1 8.6 %all-to-all-start = ((s32[32,1,128]{2,1,0:T(1,128)}), s32[32,1,128]{2,1,0:T(1,128)S(1)}, u32[]{:S(2)}, u32[]{:S(2)}) async-start(s32[32,1,128]{2,1,0:T(1,128)} %get-tuple-element.30), calls=%async_computation | async-start | bytes 32768 | tf_op jit(solution)/shard_map/all_to_all | solution.py:619
  10.7 4.0 %shard_map.202.tiles_ref = bf16[20,304,128]{2,1,0:T(8,128)(2,1)S(1)} custom-call(bf16[3,20,2048]{2,1,0:T(8,128)(2,1)} %bitcast.19, f32[20,16,2048]{2,1,0:T(8,128)} %store_ref.1), custom_call_target="tpu_custom_call" | custom-call | tf_op jit(solution)/shard_map/pallas_call | solution.py:108
  14.7 2.9 %all-to-all-done = s32[32,1,128]{2,1,0:T(1,128)S(1)} async-done(((s32[32,1,128]{2,1,0:T(1,128)}), s32[32,1,128]{2,1,0:T(1,128)S(1)}, u32[]{:S(2)}, u32[]{:S(2)}) %all-to-all-start) | async-done | bytes 16416 | tf_op jit(solution)/shard_map/all_to_all | solution.py:619
  17.6 2.2 %shard_map.203.after_ref = bf16[32,304,128]{2,1,0:T(8,128)(2,1)} custom-call(s32[32,128]{1,0:T(8,128)S(1)} %bitcast.16, bf16[20,304,128]{2,1,0:T(8,128)(2,1)S(1)} %shard_map.202.tiles_ref), custom_call_target="tpu_custom_call" | custom-call | tf_op jit(solution)/shard_map/pallas_call | solution.py:191
  19.8 4.7 %all-to-all-start.1 = ((bf16[32,304,128]{2,1,0:T(8,128)(2,1)}), bf16[32,304,128]{2,1,0:T(8,128)(2,1)S(1)}, u32[]{:S(2)}, u32[]{:S(2)}) async-start(bf16[32,304,128]{2,1,0:T(8,128)(2,1)} %shard_map.203.after_ref), calls=%async_computation.1 | async-start | bytes 4980736 | tf_op jit(solution)/shard_map/all_to_all | solution.py:619
  26.1 2.6 %shard_map.204 = (bf16[128,2048]{1,0:T(8,128)(2,1)S(1)}, bf16[480,256]{1,0:T(8,128)(2,1)S(1)}, f32[4,2048]{1,0:T(4,128)S(1)}, bf16[2048,512]{1,0:T(8,128)(2,1)S(...) custom-call(bf16[32,304,128]{2,1,0:T(8,128)(2,1)} %shard_map.203.aft, ...), custom_call_target="tpu_custom_call" | custom-call | tf_op jit(solution)/shard_map/pallas_call | solution.py:223
  28.7 1.4 copy-done
  30.1 1.3 copy-done.2
  32.7 4.3 %shard_map.208 = bf16[32,512,128]{2,1,0:T(8,128)(2,1)} custom-call(s32[32,128]{1,0:T(8,128)S(1)} %bitcast.17, bf16[20,256,128]{2,1,0:T(8,128)(2,1)} %refs_0_.3, bf16[20,256,128]{2,1,0:T(8,128)(2,1)} %refs_1_.1, f32[1,2048]{1,0:T(1,128)S(1)} %get-tuple-element.46.refs_10_.refs_2_), custom_call_target="tpu_custom_call" | custom-call | tf_op jit(solution)/shard_map/pallas_call | solution.py:156
  37.0 20.0 %all-to-all-done.1.got_ref.refs_14_ = bf16[32,304,128]{2,1,0:T(8,128)(2,1)S(1)} async-done(((bf16[32,304,128]{2,1,0:T(8,128)(2,1)}), bf16[32,304,128]{2,1,0:T(8,128)(2,1)S(1)}, u32[]{:S(2)}, u32[]{:S(2)}) %all-to-all-start.1) | async-done | bytes 2490400 | tf_op jit(solution)/shard_map/all_to_all | solution.py:619
  57.0 5.4 %all-to-all-start.2 = ((bf16[32,512,128]{2,1,0:T(8,128)(2,1)}), bf16[32,512,128]{2,1,0:T(8,128)(2,1)}, u32[]{:S(2)}, u32[]{:S(2)}) async-start(bf16[32,512,128]{2,1,0:T(8,128)(2,1)} %shard_map.208), calls=%async_computation.2 | async-start | bytes 8388608 | tf_op jit(solution)/shard_map/all_to_all | solution.py:619
  62.4 1.6 copy-done.3
  65.3 2.8 %shard_map.205 = (bf16[16,768]{1,0:T(8,128)(2,1)S(1)}, bf16[16,768]{1,0:T(8,128)(2,1)S(1)}, bf16[16,768]{1,0:T(8,128)(2,1)S(1)}, bf16[16,768]{1,0:T(8,128)(2,1)S...) custom-call(s32[49]{0:T(128)S(1)} %copy-done.9, ...), custom_call_target="tpu_custom_call" | custom-call | tf_op jit(solution)/shard_map/pallas_call | solution.py:289
  68.1 1.7 %collective-permute-start = (bf16[16,768]{1,0:T(8,128)(2,1)S(1)}, bf16[16,768]{1,0:T(8,128)(2,1)S(1)}, u32[]{:S(2)}, u32[]{:S(2)}) collective-permute-start(bf16[16,768]{1,0:T(8,128)(2,1)S(1)} %get-tuple-element.37), channel_id=1, source_target_pairs={{0,1},{1,2},{2,3},{3,4},{4,5},{5,6},{6,7},{7,0},{8,9},{9,10},{10,1... | collective-permute-start | bytes 73736 | tf_op jit(solution)/shard_map/ppermute | solution.py:691
  69.8 3.0 %collective-permute-start.1 = (bf16[16,768]{1,0:T(8,128)(2,1)S(1)}, bf16[16,768]{1,0:T(8,128)(2,1)S(1)}, u32[]{:S(2)}, u32[]{:S(2)}) collective-permute-start(bf16[16,768]{1,0:T(8,128)(2,1)S(1)} %get-tuple-element.38), channel_id=1, source_target_pairs={{0,2},{1,3},{2,4},{3,5},{4,6},{5,7},{6,0},{7,1},{8,10},{9,11},{10,... | collective-permute-start | bytes 73736 | tf_op jit(solution)/shard_map/ppermute | solution.py:691
  72.8 3.8 %collective-permute-start.2 = (bf16[16,768]{1,0:T(8,128)(2,1)S(1)}, bf16[16,768]{1,0:T(8,128)(2,1)S(1)}, u32[]{:S(2)}, u32[]{:S(2)}) collective-permute-start(bf16[16,768]{1,0:T(8,128)(2,1)S(1)} %get-tuple-element.39), channel_id=1, source_target_pairs={{0,3},{1,4},{2,5},{3,6},{4,7},{5,0},{6,1},{7,2},{8,11},{9,12},{10,... | collective-permute-start | bytes 73736 | tf_op jit(solution)/shard_map/ppermute | solution.py:691
  77.0 4.5 %collective-permute-start.4 = (bf16[16,768]{1,0:T(8,128)(2,1)S(1)}, bf16[16,768]{1,0:T(8,128)(2,1)S(1)}, u32[]{:S(2)}, u32[]{:S(2)}) collective-permute-start(bf16[16,768]{1,0:T(8,128)(2,1)S(1)} %get-tuple-element.41), channel_id=1, source_target_pairs={{0,5},{1,6},{2,7},{3,0},{4,1},{5,2},{6,3},{7,4},{8,13},{9,14},{10,... | collective-permute-start | bytes 73736 | tf_op jit(solution)/shard_map/ppermute | solution.py:691
  81.5 2.4 %collective-permute-start.5 = (bf16[16,768]{1,0:T(8,128)(2,1)S(1)}, bf16[16,768]{1,0:T(8,128)(2,1)S(1)}, u32[]{:S(2)}, u32[]{:S(2)}) collective-permute-start(bf16[16,768]{1,0:T(8,128)(2,1)S(1)} %get-tuple-element.42), channel_id=1, source_target_pairs={{0,6},{1,7},{2,0},{3,1},{4,2},{5,3},{6,4},{7,5},{8,14},{9,15},{10,... | collective-permute-start | bytes 73736 | tf_op jit(solution)/shard_map/ppermute | solution.py:691
  84.6 1.8 %collective-permute-done.5.refs_6_ = bf16[16,768]{1,0:T(8,128)(2,1)S(1)} collective-permute-done((bf16[16,768]{1,0:T(8,128)(2,1)S(1)}, bf16[16,768]{1,0:T(8,128)(2,1)S(1)}, u32[]{:S(2)}, u32[]{:S(2)}) %collective-permute-start.5) | collective-permute-done | bytes 24608 | tf_op jit(solution)/shard_map/ppermute | solution.py:691
  87.1 1.4 collective-permute-start.8
  88.5 3.6 %collective-permute-start.9 = (bf16[16,768]{1,0:T(8,128)(2,1)S(1)}, bf16[16,768]{1,0:T(8,128)(2,1)S(1)}, u32[]{:S(2)}, u32[]{:S(2)}) collective-permute-start(bf16[16,768]{1,0:T(8,128)(2,1)S(1)} %shard_map.206.refs_0_), channel_id=1, source_target_pairs={{0,3},{1,4},{2,5},{3,6},{4,7},{5,0},{6,1},{7,2},{8,11},{9,12},{10,... | collective-permute-start | bytes 73736 | tf_op jit(solution)/shard_map/ppermute | solution.py:691
  92.1 1.0 collective-permute-start.10
  93.2 3.7 %collective-permute-start.11 = (bf16[16,768]{1,0:T(8,128)(2,1)S(1)}, bf16[16,768]{1,0:T(8,128)(2,1)S(1)}, u32[]{:S(2)}, u32[]{:S(2)}) collective-permute-start(bf16[16,768]{1,0:T(8,128)(2,1)S(1)} %shard_map.206.refs_0_), channel_id=1, source_target_pairs={{0,5},{1,6},{2,7},{3,0},{4,1},{5,2},{6,3},{7,4},{8,13},{9,14},{10,... | collective-permute-start | bytes 73736 | tf_op jit(solution)/shard_map/ppermute | solution.py:691
  97.9 1.3 collective-permute-done.10.refs_4_
  99.2 2.2 %collective-permute-done.12.refs_6_ = bf16[16,768]{1,0:T(8,128)(2,1)S(1)} collective-permute-done((bf16[16,768]{1,0:T(8,128)(2,1)S(1)}, bf16[16,768]{1,0:T(8,128)(2,1)S(1)}, u32[]{:S(2)}, u32[]{:S(2)}) %collective-permute-start.12) | collective-permute-done | bytes 24608 | tf_op jit(solution)/shard_map/ppermute | solution.py:691
  101.4 12.2 %shard_map.207 = (bf16[128,2048]{1,0:T(8,128)(2,1)}, bf16[32,304,128]{2,1,0:T(8,128)(2,1)}) custom-call(s32[49]{0:T(128)S(1)} %copy-done.9, bf16[16,768]{1,0:T(8,128)(2,1)S(1)} %shard_map.206.refs_0_, bf16[16,768]{1,0:T(8,128)(2,1)S(1)} %collective-permute-done.7.refs_1_, bf16[16,768]{1,0:T(8,128)(2,1)S(1)} %collective-permute-done.8.refs_2_, ...), custom_call_target="tpu_custom_call" | custom-call | tf_op jit(solution)/shard_map/pallas_call | solution.py:433
  113.6 1.0 all-to-all-done.2.got_ref
  114.6 10.7 %all-to-all-start.3 = ((bf16[32,304,128]{2,1,0:T(8,128)(2,1)}), bf16[32,304,128]{2,1,0:T(8,128)(2,1)S(1)}, u32[]{:S(2)}, u32[]{:S(2)}) async-start(bf16[32,304,128]{2,1,0:T(8,128)(2,1)} %get-tuple-element.51), calls=%async_computation.3 | async-start | bytes 4980736 | tf_op jit(solution)/shard_map/all_to_all | solution.py:619
  125.3 14.1 %shard_map.209 = bf16[128,512]{1,0:T(8,128)(2,1)} custom-call(s32[49]{0:T(128)} %get-tuple-element.29.plan_ref, bf16[128,512]{1,0:T(8,128)(2,1)} %q_ref.1, bf16[128,128]{1,0:T(8,128)(2,1)} %k_ref.1, bf16[128,128]{1,0:T(8,128)(2,1)} %v_ref.1, bf16[32,512,128]{2,1,0:T(8,128)(2,1)} %all-to-all-done.2.got_ref), custom_call_target="tpu_custom_call" | custom-call | tf_op jit(solution)/shard_map/pallas_call | solution.py:516
  139.5 18.4 %all-to-all-done.3.back_ref = bf16[32,304,128]{2,1,0:T(8,128)(2,1)S(1)} async-done(((bf16[32,304,128]{2,1,0:T(8,128)(2,1)}), bf16[32,304,128]{2,1,0:T(8,128)(2,1)S(1)}, u32[]{:S(2)}, u32[]{:S(2)}) %all-to-all-start.3) | async-done | bytes 2490400 | tf_op jit(solution)/shard_map/all_to_all | solution.py:619
  157.8 4.2 %shard_map.210 = (bf16[3,20,2048]{2,1,0:T(8,128)(2,1)}, f32[20,16,2048]{2,1,0:T(8,128)}) custom-call(s32[32,128]{1,0:T(8,128)S(1)} %bitcast.18, bf16[3,20,2048]{2,1,0:T(8,128)(2,1)} %bitcast.20, f32[20,16,2048]{2,1,0:T(8,128)} %store_ref.1, bf16[32,304,128]{2,1,0:T(8,128)(2,1)S(1)} %all-to-all-done.3.back_ref), custom_call_target="tpu_custom_call" | custom-call | tf_op jit(solution)/shard_map/pallas_call | solution.py:598
  (54 shorter events, 7.1 us)
Async XLA Ops:
  2.1 15.5 %all-to-all-start = ((s32[32,1,128]{2,1,0:T(1,128)}), s32[32,1,128]{2,1,0:T(1,128)S(1)}, u32[]{:S(2)}, u32[]{:S(2)}) async-start(s32[32,1,128]{2,1,0:T(1,128)} %get-tuple-element.30), calls=%async_computation | async-start | bytes 32768 | tf_op jit(solution)/shard_map/all_to_all | solution.py:619
  19.7 4.7 %copy-start.10 = (s32[1,16]{1,0:T(1,128)S(1)}, s32[1,16]{1,0:T(1,128)}, u32[]{:S(2)}) copy-start(s32[1,16]{1,0:T(1,128)} %length_ref.1) | copy-start | bytes 196
  19.7 5.0 %copy-start.11 = (s32[16]{0:T(128)S(1)}, s32[16]{0:T(128)}, u32[]{:S(2)}) copy-start(s32[16]{0:T(128)} %entry_ref.1) | copy-start | bytes 196
  19.8 6.3 %copy-start.4 = (f32[16,2048]{1,0:T(8,128)S(1)}, f32[16,2048]{1,0:T(8,128)}, u32[]{:S(2)}) copy-start(f32[16,2048]{1,0:T(8,128)} %refs_8_.1) | copy-start | bytes 393220
  19.8 37.2 %all-to-all-start.1 = ((bf16[32,304,128]{2,1,0:T(8,128)(2,1)}), bf16[32,304,128]{2,1,0:T(8,128)(2,1)S(1)}, u32[]{:S(2)}, u32[]{:S(2)}) async-start(bf16[32,304,128]{2,1,0:T(8,128)(2,1)} %shard_map.203.after_ref), calls=%async_computation.1 | async-start | bytes 4980736 | tf_op jit(solution)/shard_map/all_to_all | solution.py:619
  28.7 1.4 copy-start
  30.1 1.3 copy-start.2
  31.4 0.7 copy-start.5
  32.1 0.6 copy-start.7
  37.0 25.4 %copy-start.6 = (bf16[32,2048]{1,0:T(8,128)(2,1)S(1)}, bf16[32,2048]{1,0:T(8,128)(2,1)}, u32[]{:S(2)}) copy-start(bf16[32,2048]{1,0:T(8,128)(2,1)} %copy-done.5) | copy-start | bytes 393220
  57.0 57.7 %all-to-all-start.2 = ((bf16[32,512,128]{2,1,0:T(8,128)(2,1)}), bf16[32,512,128]{2,1,0:T(8,128)(2,1)}, u32[]{:S(2)}, u32[]{:S(2)}) async-start(bf16[32,512,128]{2,1,0:T(8,128)(2,1)} %shard_map.208), calls=%async_computation.2 | async-start | bytes 8388608 | tf_op jit(solution)/shard_map/all_to_all | solution.py:619
  62.4 1.6 copy-start.3
  64.0 0.8 copy-start.8
  64.7 0.6 copy-start.9
  65.3 36.1 %copy-start.1 = (bf16[512,2048]{1,0:T(8,128)(2,1)S(1)}, bf16[512,2048]{1,0:T(8,128)(2,1)}, u32[]{:S(2)}) copy-start(bf16[512,2048]{1,0:T(8,128)(2,1)} %copy-done) | copy-start | bytes 6291460
  68.1 13.4 %collective-permute-start = (bf16[16,768]{1,0:T(8,128)(2,1)S(1)}, bf16[16,768]{1,0:T(8,128)(2,1)S(1)}, u32[]{:S(2)}, u32[]{:S(2)}) collective-permute-start(bf16[16,768]{1,0:T(8,128)(2,1)S(1)} %get-tuple-element.37), channel_id=1, source_target_pairs={{0,1},{1,2},{2,3},{3,4},{4,5},{5,6},{6,7},{7,0},{8,9},{9,10},{10,1... | collective-permute-start | bytes 73736 | tf_op jit(solution)/shard_map/ppermute | solution.py:691
  69.8 14.1 %collective-permute-start.1 = (bf16[16,768]{1,0:T(8,128)(2,1)S(1)}, bf16[16,768]{1,0:T(8,128)(2,1)S(1)}, u32[]{:S(2)}, u32[]{:S(2)}) collective-permute-start(bf16[16,768]{1,0:T(8,128)(2,1)S(1)} %get-tuple-element.38), channel_id=1, source_target_pairs={{0,2},{1,3},{2,4},{3,5},{4,6},{5,7},{6,0},{7,1},{8,10},{9,11},{10,... | collective-permute-start | bytes 73736 | tf_op jit(solution)/shard_map/ppermute | solution.py:691
  72.8 11.8 %collective-permute-start.2 = (bf16[16,768]{1,0:T(8,128)(2,1)S(1)}, bf16[16,768]{1,0:T(8,128)(2,1)S(1)}, u32[]{:S(2)}, u32[]{:S(2)}) collective-permute-start(bf16[16,768]{1,0:T(8,128)(2,1)S(1)} %get-tuple-element.39), channel_id=1, source_target_pairs={{0,3},{1,4},{2,5},{3,6},{4,7},{5,0},{6,1},{7,2},{8,11},{9,12},{10,... | collective-permute-start | bytes 73736 | tf_op jit(solution)/shard_map/ppermute | solution.py:691
  76.6 8.0 %collective-permute-start.3 = (bf16[16,768]{1,0:T(8,128)(2,1)S(1)}, bf16[16,768]{1,0:T(8,128)(2,1)S(1)}, u32[]{:S(2)}, u32[]{:S(2)}) collective-permute-start(bf16[16,768]{1,0:T(8,128)(2,1)S(1)} %get-tuple-element.40), channel_id=1, source_target_pairs={{0,4},{1,5},{2,6},{3,7},{4,0},{5,1},{6,2},{7,3},{8,12},{9,13},{10,... | collective-permute-start | bytes 73736 | tf_op jit(solution)/shard_map/ppermute | solution.py:691
  77.0 7.6 %collective-permute-start.4 = (bf16[16,768]{1,0:T(8,128)(2,1)S(1)}, bf16[16,768]{1,0:T(8,128)(2,1)S(1)}, u32[]{:S(2)}, u32[]{:S(2)}) collective-permute-start(bf16[16,768]{1,0:T(8,128)(2,1)S(1)} %get-tuple-element.41), channel_id=1, source_target_pairs={{0,5},{1,6},{2,7},{3,0},{4,1},{5,2},{6,3},{7,4},{8,13},{9,14},{10,... | collective-permute-start | bytes 73736 | tf_op jit(solution)/shard_map/ppermute | solution.py:691
  81.5 4.9 %collective-permute-start.5 = (bf16[16,768]{1,0:T(8,128)(2,1)S(1)}, bf16[16,768]{1,0:T(8,128)(2,1)S(1)}, u32[]{:S(2)}, u32[]{:S(2)}) collective-permute-start(bf16[16,768]{1,0:T(8,128)(2,1)S(1)} %get-tuple-element.42), channel_id=1, source_target_pairs={{0,6},{1,7},{2,0},{3,1},{4,2},{5,3},{6,4},{7,5},{8,14},{9,15},{10,... | collective-permute-start | bytes 73736 | tf_op jit(solution)/shard_map/ppermute | solution.py:691
  83.9 3.1 %collective-permute-start.6 = (bf16[16,768]{1,0:T(8,128)(2,1)S(1)}, bf16[16,768]{1,0:T(8,128)(2,1)S(1)}, u32[]{:S(2)}, u32[]{:S(2)}) collective-permute-start(bf16[16,768]{1,0:T(8,128)(2,1)S(1)} %get-tuple-element.43), channel_id=1, source_target_pairs={{0,7},{1,0},{2,1},{3,2},{4,3},{5,4},{6,5},{7,6},{8,15},{9,8},{10,9... | collective-permute-start | bytes 73736 | tf_op jit(solution)/shard_map/ppermute | solution.py:691
  87.0 9.9 %collective-permute-start.7 = (bf16[16,768]{1,0:T(8,128)(2,1)S(1)}, bf16[16,768]{1,0:T(8,128)(2,1)S(1)}, u32[]{:S(2)}, u32[]{:S(2)}) collective-permute-start(bf16[16,768]{1,0:T(8,128)(2,1)S(1)} %shard_map.206.refs_0_), channel_id=1, source_target_pairs={{0,1},{1,2},{2,3},{3,4},{4,5},{5,6},{6,7},{7,0},{8,9},{9,10},{10,1... | collective-permute-start | bytes 73736 | tf_op jit(solution)/shard_map/ppermute | solution.py:691
  87.1 10.7 %collective-permute-start.8 = (bf16[16,768]{1,0:T(8,128)(2,1)S(1)}, bf16[16,768]{1,0:T(8,128)(2,1)S(1)}, u32[]{:S(2)}, u32[]{:S(2)}) collective-permute-start(bf16[16,768]{1,0:T(8,128)(2,1)S(1)} %shard_map.206.refs_0_), channel_id=1, source_target_pairs={{0,2},{1,3},{2,4},{3,5},{4,6},{5,7},{6,0},{7,1},{8,10},{9,11},{10,... | collective-permute-start | bytes 73736 | tf_op jit(solution)/shard_map/ppermute | solution.py:691
  88.5 9.4 %collective-permute-start.9 = (bf16[16,768]{1,0:T(8,128)(2,1)S(1)}, bf16[16,768]{1,0:T(8,128)(2,1)S(1)}, u32[]{:S(2)}, u32[]{:S(2)}) collective-permute-start(bf16[16,768]{1,0:T(8,128)(2,1)S(1)} %shard_map.206.refs_0_), channel_id=1, source_target_pairs={{0,3},{1,4},{2,5},{3,6},{4,7},{5,0},{6,1},{7,2},{8,11},{9,12},{10,... | collective-permute-start | bytes 73736 | tf_op jit(solution)/shard_map/ppermute | solution.py:691
  92.1 7.1 %collective-permute-start.10 = (bf16[16,768]{1,0:T(8,128)(2,1)S(1)}, bf16[16,768]{1,0:T(8,128)(2,1)S(1)}, u32[]{:S(2)}, u32[]{:S(2)}) collective-permute-start(bf16[16,768]{1,0:T(8,128)(2,1)S(1)} %shard_map.206.refs_0_), channel_id=1, source_target_pairs={{0,4},{1,5},{2,6},{3,7},{4,0},{5,1},{6,2},{7,3},{8,12},{9,13},{10,... | collective-permute-start | bytes 73736 | tf_op jit(solution)/shard_map/ppermute | solution.py:691
  93.2 6.1 %collective-permute-start.11 = (bf16[16,768]{1,0:T(8,128)(2,1)S(1)}, bf16[16,768]{1,0:T(8,128)(2,1)S(1)}, u32[]{:S(2)}, u32[]{:S(2)}) collective-permute-start(bf16[16,768]{1,0:T(8,128)(2,1)S(1)} %shard_map.206.refs_0_), channel_id=1, source_target_pairs={{0,5},{1,6},{2,7},{3,0},{4,1},{5,2},{6,3},{7,4},{8,13},{9,14},{10,... | collective-permute-start | bytes 73736 | tf_op jit(solution)/shard_map/ppermute | solution.py:691
  96.9 4.5 %collective-permute-start.12 = (bf16[16,768]{1,0:T(8,128)(2,1)S(1)}, bf16[16,768]{1,0:T(8,128)(2,1)S(1)}, u32[]{:S(2)}, u32[]{:S(2)}) collective-permute-start(bf16[16,768]{1,0:T(8,128)(2,1)S(1)} %shard_map.206.refs_0_), channel_id=1, source_target_pairs={{0,6},{1,7},{2,0},{3,1},{4,2},{5,3},{6,4},{7,5},{8,14},{9,15},{10,... | collective-permute-start | bytes 73736 | tf_op jit(solution)/shard_map/ppermute | solution.py:691
  97.8 3.6 %collective-permute-start.13 = (bf16[16,768]{1,0:T(8,128)(2,1)S(1)}, bf16[16,768]{1,0:T(8,128)(2,1)S(1)}, u32[]{:S(2)}, u32[]{:S(2)}) collective-permute-start(bf16[16,768]{1,0:T(8,128)(2,1)S(1)} %shard_map.206.refs_0_), channel_id=1, source_target_pairs={{0,7},{1,0},{2,1},{3,2},{4,3},{5,4},{6,5},{7,6},{8,15},{9,8},{10,9... | collective-permute-start | bytes 73736 | tf_op jit(solution)/shard_map/ppermute | solution.py:691
  114.6 43.2 %all-to-all-start.3 = ((bf16[32,304,128]{2,1,0:T(8,128)(2,1)}), bf16[32,304,128]{2,1,0:T(8,128)(2,1)S(1)}, u32[]{:S(2)}, u32[]{:S(2)}) async-start(bf16[32,304,128]{2,1,0:T(8,128)(2,1)} %get-tuple-element.51), calls=%async_computation.3 | async-start | bytes 4980736 | tf_op jit(solution)/shard_map/all_to_all | solution.py:619
